TPU v7x, 256 devices: a whole 4x4x8 slice. The times are simulated.
256 devices in a mesh: src: 8 (over y, core), tgt: 32 (over x, z).
Axes of the slice: x: 4, y: 4, z: 8, core: 2. Of those that a mesh axis runs over, the one named last changes fastest.
Arguments:
- cost: bfloat16 [8, 96, 1024, 1024], P('src', 'tgt'), may hold values from -60 to 4
- cost_scale: float32 [8, 96], P('src', 'tgt'), may hold values from 0.5 to 2
- slot_block_row: int32 [8, 96], P('src', 'tgt'), may hold values from 0 to 31, as said below
- slot_block_column: int32 [8, 96], P('src', 'tgt'), may hold values from 0 to 127, as said below
- device_block_count: int32 [8, 32], P('src', 'tgt'), may hold values from 1 to 3, as said below
- log_a: float32 [32768], P('src'), may hold values from -1 to 1
- log_b: float32 [131072], P('tgt'), may hold values from -1 to 1
- labels: bfloat16 [32768, 64], P(('src', 'tgt')), may hold values from 0 to 1
Outputs:
- f_pot: float32 [32768], P('src')
- g_pot: float32 [131072], P('tgt')
- transported: bfloat16 [131072, 64], P('tgt')
Inputs may be any that keep to these rules, and one draw needn't show every extreme that they name: `device_block_count`: live slots of one device; slot 0 is always live and some device has 3. `slot_block_row`: block rows of device (i, j) lie in i * 4 to i * 4 + 3; the blocks of one device are distinct; every block row and every block column holds a live block. `slot_block_column`: block columns of device (i, j) lie in j * 4 to j * 4 + 3.
All inputs are finite; a program needn't handle non-finite values.
Results may differ from a plain program's by a relative error of at most 0.0043.
Values may be sent and summed in bfloat16 or wider, within the bound.
No kernel may reach another device: no remote copies, remote signals or barrier semaphores. Data moves between devices by JAX's collectives and lax.ppermute only.
A program may use at most 64 MiB of HBM per device.

v0:
```python
import jax
import jax.numpy as jnp
from jax import lax
from jax.sharding import PartitionSpec as P

ITERS = 4


EPS = 0.5
NEG = -1e30


def combine_lse(first, second):
    top = jnp.maximum(first[0], second[0])
    total = first[1] * jnp.exp(first[0] - top) + second[1] * jnp.exp(second[0] - top)
    return (top, total)


def local_lse(
    cost, cost_scale, other, offsets_near, offsets_far, slot_live_mask, count, along_rows
):
    m_all = jnp.full((count,), NEG, jnp.float32)
    s_all = jnp.zeros((count,), jnp.float32)
    block_tile = cost.shape[2]
    for slot_number in range(cost.shape[1]):
        dense = cost_scale[0, slot_number] * cost[0, slot_number].astype(jnp.float32)
        part = lax.dynamic_slice_in_dim(other, offsets_far[slot_number], block_tile, 0)
        if along_rows:
            z_vals = (part[None, :] - dense) / EPS
            axis_id = 1
        else:
            z_vals = (part[:, None] - dense) / EPS
            axis_id = 0
        block_max = jnp.max(z_vals, axis=axis_id)
        block_sum = jnp.sum(jnp.exp(z_vals - jnp.expand_dims(block_max, axis_id)), axis=axis_id)
        old_m = lax.dynamic_slice_in_dim(m_all, offsets_near[slot_number], block_tile, 0)
        old_s = lax.dynamic_slice_in_dim(s_all, offsets_near[slot_number], block_tile, 0)
        new_m, new_s = combine_lse((old_m, old_s), (block_max, block_sum))
        new_m = jnp.where(slot_live_mask[slot_number], new_m, old_m)
        new_s = jnp.where(slot_live_mask[slot_number], new_s, old_s)
        m_all = lax.dynamic_update_slice_in_dim(m_all, new_m, offsets_near[slot_number], 0)
        s_all = lax.dynamic_update_slice_in_dim(s_all, new_s, offsets_near[slot_number], 0)
    return (m_all, s_all)


def local(
    cost, cost_scale, slot_block_row, slot_block_column, device_block_count, log_a, log_b, labels
):
    rows_here = log_a.shape[0]
    cols_here = log_b.shape[0]
    block_tile = cost.shape[2]
    slot_total_count = cost.shape[1]
    row_start_index = lax.axis_index("src") * rows_here
    column_start_index = lax.axis_index("tgt") * cols_here
    row_block_offsets = [
        slot_block_row[0, slot_position] * block_tile - row_start_index
        for slot_position in range(slot_total_count)
    ]
    column_block_offsets = [
        slot_block_column[0, slot_position] * block_tile - column_start_index
        for slot_position in range(slot_total_count)
    ]
    slot_live_mask = [
        slot_position < device_block_count[0, 0] for slot_position in range(slot_total_count)
    ]
    label_block = lax.all_gather(labels, "tgt", axis=0, tiled=True)
    g_pot = jnp.zeros((cols_here,), jnp.float32)
    f_pot = jnp.zeros((rows_here,), jnp.float32)
    for step_id in range(ITERS):
        row_m, row_s = local_lse(
            cost,
            cost_scale,
            g_pot,
            row_block_offsets,
            column_block_offsets,
            slot_live_mask,
            rows_here,
            True,
        )
        row_top = lax.pmax(row_m, "tgt")
        row_total = lax.psum(row_s * jnp.exp(row_m - row_top), "tgt")
        row_lse = row_top + jnp.log(row_total)
        f_pot = EPS * log_a - EPS * row_lse
        col_m, col_s = local_lse(
            cost,
            cost_scale,
            f_pot,
            column_block_offsets,
            row_block_offsets,
            slot_live_mask,
            cols_here,
            False,
        )
        col_top = lax.pmax(col_m, "src")
        col_total = lax.psum(col_s * jnp.exp(col_m - col_top), "src")
        col_lse = col_top + jnp.log(col_total)
        g_pot = EPS * log_b - EPS * col_lse
    classes = labels.shape[1]
    acc = jnp.zeros((cols_here, classes), jnp.float32)
    for slot_number in range(slot_total_count):
        f_part = lax.dynamic_slice_in_dim(f_pot, row_block_offsets[slot_number], block_tile, 0)
        g_part = lax.dynamic_slice_in_dim(g_pot, column_block_offsets[slot_number], block_tile, 0)
        dense = cost_scale[0, slot_number] * cost[0, slot_number].astype(jnp.float32)
        plan = jnp.exp((f_part[:, None] + g_part[None, :] - dense) / EPS).astype(jnp.bfloat16)
        lab = lax.dynamic_slice_in_dim(label_block, row_block_offsets[slot_number], block_tile, 0)
        term = lax.dot_general(
            plan, lab, (((0,), (0,)), ((), ())), preferred_element_type=jnp.float32
        )
        old = lax.dynamic_slice_in_dim(acc, column_block_offsets[slot_number], block_tile, 0)
        new = old + jnp.where(slot_live_mask[slot_number], term, jnp.zeros_like(term))
        acc = lax.dynamic_update_slice_in_dim(acc, new, column_block_offsets[slot_number], 0)
    transported = lax.psum(acc, "src").astype(jnp.bfloat16)
    return (f_pot, g_pot, transported)


def solution(mesh):
    in_specs = (
        P("src", "tgt", None, None),
        P("src", "tgt"),
        P("src", "tgt"),
        P("src", "tgt"),
        P("src", "tgt"),
        P("src"),
        P("tgt"),
        P(("src", "tgt"), None),
    )
    out_specs = (P("src"), P("tgt"), P("tgt", None))
    return jax.shard_map(local, mesh=mesh, in_specs=in_specs, out_specs=out_specs, check_vma=False)
```

profile of v0, /device:TPU:1, one launch (start us, length us, event | category | flops | bytes accessed | tf_op | source)
XLA Modules:
  0.0 1527.9 jit_solution(1905750464359345650)
XLA Ops:
  9.3 6.3 fusion.40
  15.7 6.0 exponential_reduce_fusion.21
  21.8 118.7 %pmax.56 = f32[4096]{0:T(1024)S(1)} all-reduce(f32[4096]{0:T(1024)S(1)} %get-tuple-element.73), channel_id=1, replica_groups=mesh['src'=8,'tgt'=32] {'tgt'}, use_global_device_ids=true, to_apply=%region_3.4 | all-reduce | flops 4096 | bytes 32768 | tf_op jit(solution)/shard_map/pmax | solution.py:80
  140.5 110.4 %psum.63 = f32[4096]{0:T(1024)S(1)} all-reduce(f32[4096]{0:T(1024)S(1)} %exponential_multiply_fusion.7), channel_id=1, replica_groups=mesh['src'=8,'tgt'=32] {'tgt'}, use_global_device_ids=true, to_apply=%region_7.8 | all-reduce | flops 4096 | bytes 32768 | tf_op jit(solution)/shard_map/psum | solution.py:81
  254.1 6.3 exponential_reduce_fusion.18
  260.4 3.7 exponential_reduce_fusion.19
  264.2 75.9 %pmax.57 = f32[4096]{0:T(1024)S(1)} all-reduce(f32[4096]{0:T(1024)S(1)} %get-tuple-element.69), channel_id=1, replica_groups=mesh['src'=8,'tgt'=32] {'src'}, use_global_device_ids=true, to_apply=%region_11.12 | all-reduce | flops 4096 | bytes 32768 | tf_op jit(solution)/shard_map/pmax | solution.py:94
  340.1 23.6 %psum.64 = f32[4096]{0:T(1024)S(1)} all-reduce(f32[4096]{0:T(1024)S(1)} %exponential_multiply_fusion.6), channel_id=1, replica_groups=mesh['src'=8,'tgt'=32] {'src'}, use_global_device_ids=true, to_apply=%region_15.16 | all-reduce | flops 4096 | bytes 32768 | tf_op jit(solution)/shard_map/psum | solution.py:95
  366.6 6.6 exponential_reduce_fusion.15
  373.2 5.4 exponential_reduce_fusion.16
  378.8 110.4 %pmax.58 = f32[4096]{0:T(1024)S(1)} all-reduce(f32[4096]{0:T(1024)S(1)} %get-tuple-element.65), channel_id=1, replica_groups=mesh['src'=8,'tgt'=32] {'tgt'}, use_global_device_ids=true, to_apply=%region_19.20 | all-reduce | flops 4096 | bytes 32768 | tf_op jit(solution)/shard_map/pmax | solution.py:80
  489.2 110.9 %psum.65 = f32[4096]{0:T(1024)S(1)} all-reduce(f32[4096]{0:T(1024)S(1)} %exponential_multiply_fusion.5), channel_id=1, replica_groups=mesh['src'=8,'tgt'=32] {'tgt'}, use_global_device_ids=true, to_apply=%region_23.24 | all-reduce | flops 4096 | bytes 32768 | tf_op jit(solution)/shard_map/psum | solution.py:81
  603.2 6.3 exponential_reduce_fusion.12
  613.3 78.1 %pmax.59 = f32[4096]{0:T(1024)S(1)} all-reduce(f32[4096]{0:T(1024)S(1)} %get-tuple-element.61), channel_id=1, replica_groups=mesh['src'=8,'tgt'=32] {'src'}, use_global_device_ids=true, to_apply=%region_27.28 | all-reduce | flops 4096 | bytes 32768 | tf_op jit(solution)/shard_map/pmax | solution.py:94
  691.5 23.6 %psum.66 = f32[4096]{0:T(1024)S(1)} all-reduce(f32[4096]{0:T(1024)S(1)} %exponential_multiply_fusion.4), channel_id=1, replica_groups=mesh['src'=8,'tgt'=32] {'src'}, use_global_device_ids=true, to_apply=%region_31.32 | all-reduce | flops 4096 | bytes 32768 | tf_op jit(solution)/shard_map/psum | solution.py:95
  717.9 6.6 exponential_reduce_fusion.9
  724.6 5.4 exponential_reduce_fusion.10
  730.1 110.4 %pmax.60 = f32[4096]{0:T(1024)S(1)} all-reduce(f32[4096]{0:T(1024)S(1)} %get-tuple-element.57), channel_id=1, replica_groups=mesh['src'=8,'tgt'=32] {'tgt'}, use_global_device_ids=true, to_apply=%region_35.36 | all-reduce | flops 4096 | bytes 32768 | tf_op jit(solution)/shard_map/pmax | solution.py:80
  840.5 110.6 %psum.67 = f32[4096]{0:T(1024)S(1)} all-reduce(f32[4096]{0:T(1024)S(1)} %exponential_multiply_fusion.3), channel_id=1, replica_groups=mesh['src'=8,'tgt'=32] {'tgt'}, use_global_device_ids=true, to_apply=%region_39.40 | all-reduce | flops 4096 | bytes 32768 | tf_op jit(solution)/shard_map/psum | solution.py:81
  954.2 6.3 exponential_reduce_fusion.6
  964.3 78.1 %pmax.61 = f32[4096]{0:T(1024)S(1)} all-reduce(f32[4096]{0:T(1024)S(1)} %get-tuple-element.53), channel_id=1, replica_groups=mesh['src'=8,'tgt'=32] {'src'}, use_global_device_ids=true, to_apply=%region_43.44 | all-reduce | flops 4096 | bytes 32768 | tf_op jit(solution)/shard_map/pmax | solution.py:94
  1042.5 23.6 %psum.68 = f32[4096]{0:T(1024)S(1)} all-reduce(f32[4096]{0:T(1024)S(1)} %exponential_multiply_fusion.2), channel_id=1, replica_groups=mesh['src'=8,'tgt'=32] {'src'}, use_global_device_ids=true, to_apply=%region_47.48 | all-reduce | flops 4096 | bytes 32768 | tf_op jit(solution)/shard_map/psum | solution.py:95
  1069.0 6.6 exponential_reduce_fusion.3
  1075.6 5.4 exponential_reduce_fusion.4
  1081.1 110.4 %pmax.62 = f32[4096]{0:T(1024)S(1)} all-reduce(f32[4096]{0:T(1024)S(1)} %get-tuple-element.49), channel_id=1, replica_groups=mesh['src'=8,'tgt'=32] {'tgt'}, use_global_device_ids=true, to_apply=%region_51.52 | all-reduce | flops 4096 | bytes 32768 | tf_op jit(solution)/shard_map/pmax | solution.py:80
  1191.5 110.6 %psum.69 = f32[4096]{0:T(1024)S(1)} all-reduce(f32[4096]{0:T(1024)S(1)} %exponential_multiply_fusion.1), channel_id=1, replica_groups=mesh['src'=8,'tgt'=32] {'tgt'}, use_global_device_ids=true, to_apply=%region_55.56 | all-reduce | flops 4096 | bytes 32768 | tf_op jit(solution)/shard_map/psum | solution.py:81
  1305.3 6.3 exponential_reduce_fusion
  1311.7 3.7 exponential_reduce_fusion.1
  1315.4 78.1 %pmax.63 = f32[4096]{0:T(1024)S(1)} all-reduce(f32[4096]{0:T(1024)S(1)} %get-tuple-element.45), channel_id=1, replica_groups=mesh['src'=8,'tgt'=32] {'src'}, use_global_device_ids=true, to_apply=%region_59.60 | all-reduce | flops 4096 | bytes 32768 | tf_op jit(solution)/shard_map/pmax | solution.py:94
  1393.6 23.6 %psum.70 = f32[4096]{0:T(1024)S(1)} all-reduce(f32[4096]{0:T(1024)S(1)} %exponential_multiply_fusion), channel_id=1, replica_groups=mesh['src'=8,'tgt'=32] {'src'}, use_global_device_ids=true, to_apply=%region_63.64 | all-reduce | flops 4096 | bytes 32768 | tf_op jit(solution)/shard_map/psum | solution.py:95
  1417.2 35.3 %all_gather.3 = bf16[4096,64]{0,1:T(8,128)(2,1)S(1)} all-gather(bf16[128,64]{0,1:T(8,128)(2,1)S(1)} %copy-done.5), channel_id=1, replica_groups=mesh['src'=8,'tgt'=32] {'tgt'}, dimensions={0}, use_global_device_ids=true | all-gather | bytes 540672 | tf_op jit(solution)/shard_map/all_gather | solution.py:66
  1463.0 64.7 %all-reduce.1 = bf16[4096,64]{0,1:T(8,128)(2,1)} all-reduce(f32[4096,64]{0,1:T(8,128)S(1)} %fusion.69), channel_id=1, replica_groups=mesh['src'=8,'tgt'=32] {'src'}, use_global_device_ids=true, to_apply=%region_64.65 | all-reduce | flops 262144 | bytes 1572864 | tf_op jit(solution)/shard_map/psum | solution.py:112
  (112 shorter events, 43.9 us)
Async XLA Ops:
  9.3 6.4 copy-start
  15.7 235.3 %copy-start.1 = (f32[4096]{0:T(1024)S(1)}, f32[4096]{0:T(1024)}, u32[]{:S(2)}) copy-start(f32[4096]{0:T(1024)} %param.13) | copy-start | bytes 49156
  15.7 244.7 %slice-start = ((s8[6291456]{0:T(1024)(128)(4,1)}), s8[2097152]{0:T(1024)(128)(4,1)S(1)}, s32[]{:S(2)}) async-start(s8[6291456]{0:T(1024)(128)(4,1)} %bitcast.223), calls=%async_computation | async-start | bytes 4194304
  250.9 9.4 slice-start.1
  254.1 109.6 %copy-start.2 = (f32[4096]{0:T(1024)S(1)}, f32[4096]{0:T(1024)}, u32[]{:S(2)}) copy-start(f32[4096]{0:T(1024)} %param.14) | copy-start | bytes 49156
  373.2 236.2 %slice-start.2 = ((s8[6291456]{0:T(1024)(128)(4,1)}), s8[2097152]{0:T(1024)(128)(4,1)S(1)}, s32[]{:S(2)}) async-start(s8[6291456]{0:T(1024)(128)(4,1)} %bitcast.225), calls=%async_computation.2 | async-start | bytes 4194304
  600.1 9.4 slice-start.3
  724.6 236.0 %slice-start.4 = ((s8[6291456]{0:T(1024)(128)(4,1)}), s8[2097152]{0:T(1024)(128)(4,1)S(1)}, s32[]{:S(2)}) async-start(s8[6291456]{0:T(1024)(128)(4,1)} %bitcast.227), calls=%async_computation.4 | async-start | bytes 4194304
  951.1 9.4 slice-start.5
  1075.6 236.0 %slice-start.6 = ((s8[6291456]{0:T(1024)(128)(4,1)}), s8[2097152]{0:T(1024)(128)(4,1)S(1)}, s32[]{:S(2)}) async-start(s8[6291456]{0:T(1024)(128)(4,1)} %bitcast.229), calls=%async_computation.6 | async-start | bytes 4194304
  1302.1 9.5 copy-start.3
  1302.2 9.5 slice-start.7
  1305.3 111.9 %copy-start.5 = (bf16[128,64]{0,1:T(8,128)(2,1)S(1)}, bf16[128,64]{0,1:T(8,128)(2,1)}, u32[]{:S(2)}) copy-start(bf16[128,64]{0,1:T(8,128)(2,1)} %param.15) | copy-start | bytes 49156
  1417.2 38.9 %copy-start.4 = (f32[4096]{0:T(1024)}, f32[4096]{0:T(1024)S(1)}, u32[]{:S(2)}) copy-start(f32[4096]{0:T(1024)S(1)} %multiply_subtract_fusion) | copy-start | bytes 49156
where the time goes:
time: 1540 us; the launch traced here: 1530 us
  blocking collectives  1400 us (91%)
  other arithmetic  110 us (7%)
    pmax x4, blocking collectives, local(): row_top = lax.pmax(row_m, 'tgt')  450 us
    psum x4, blocking collectives, local(): row_total = lax.psum(row_s * jnp.exp(row_m - row_top), 'tgt')  442 us
    pmax x4, blocking collectives, local(): col_top = lax.pmax(col_m, 'src')  310 us
    psum x4, blocking collectives, local(): col_total = lax.psum(col_s * jnp.exp(col_m - col_top), 'src')  94.2 us
    reduce_sum x15, other arithmetic, local_lse(): jnp.sum(jnp.exp(z_vals - jnp.expand_dims(block_max, axis_id)), axis=axis_id)  82 us
    psum x1, blocking collectives, local(): transported = lax.psum(acc, 'src').astype(jnp.bfloat16)  64.7 us
    all_gather x1, blocking collectives, local(): label_block = lax.all_gather(labels, 'tgt', axis=0, tiled=True)  35.3 us

commit v1 on v0

v1 whole, which is shorter than its diff:
```python
import functools

import jax
import jax.numpy as jnp
from jax import lax
from jax.experimental import pallas as pl
from jax.experimental.pallas import tpu as pltpu
from jax.sharding import PartitionSpec as P

ITERS = 4
EPS = 0.5
NEG = -1e30
LOG2E = 1.4426950408889634
TO2 = LOG2E / EPS
INNER = 8
LIMIT = 40 * 1024 * 1024
F32, BF16 = jnp.float32, jnp.bfloat16


def tree_sum(parts):
    while len(parts) > 1:
        parts = [a + b for a, b in zip(parts[0::2], parts[1::2])]
    return parts[0]


def lse(parts):
    top = functools.reduce(jnp.maximum, parts)
    return top + jnp.log(tree_sum([jnp.exp(p - top) for p in parts]))


def xor_exchange(x, axis, size, steps):
    return [x] + [lax.ppermute(x, axis, [(i, i ^ k) for i in range(size)]) for k in steps]


class Slots:
    def __init__(self, scale, row, col, count, rb, cb, total):
        src, tgt = lax.axis_index("src"), lax.axis_index("tgt")
        self.total = total
        self.scale = [scale[0, s] for s in range(total)]
        self.row = [row[0, s] - src * rb for s in range(total)]
        self.col = [col[0, s] - tgt * cb for s in range(total)]
        self.live = [s < count[0, 0] for s in range(total)]
        self.src, self.tgt = src, tgt


def split_rows(x):
    x = jnp.broadcast_to(x, (16, x.shape[1]))
    hi = x.astype(BF16).astype(F32)
    rest = x - hi
    mid = rest.astype(BF16).astype(F32)
    low = (rest - mid).astype(BF16).astype(F32)
    at = lax.broadcasted_iota(jnp.int32, x.shape, 0)
    zero = jnp.zeros_like(x)
    return jnp.where(at == 0, hi, jnp.where(at == 1, mid, jnp.where(at == 2, low, zero))).astype(BF16)


def k_row(lhs, k_block):
    return lax.dot_general(lhs, k_block, (((1,), (1,)), ((), ())), preferred_element_type=F32)


def k_col(lhs, k_block):
    return lax.dot_general(lhs, k_block, (((1,), (0,)), ((), ())), preferred_element_type=F32)


def chunked(row, out_ref):
    for c in range(out_ref.shape[0]):
        out_ref[c : c + 1, :] = row[:, c * 128 : (c + 1) * 128]


def tile_z(cost_v, scale, other8, out_chunk, red_chunk, rows_mode):
    mine = pl.ds(pl.multiple_of(out_chunk * 128, 128), 128)
    summed = pl.ds(pl.multiple_of(red_chunk * 128, 128), 128)
    other = jnp.broadcast_to(other8[pl.ds(red_chunk, 1), :], (128, 128)).T
    if rows_mode:
        tile = cost_v[mine, summed].astype(F32).T
    else:
        tile = cost_v[summed, mine].astype(F32)
    return (other - scale * tile) / EPS


def slow_lse(slots, cost_hbm, cost_v, sem, other8, out8, other_ref, l_ref, rows_mode):
    l_ref[...] = jnp.full(l_ref.shape, NEG, F32)
    chunks = out8.shape[0]
    for s in range(slots.total):
        out_at, other_at = (slots.row[s], slots.col[s]) if rows_mode else (slots.col[s], slots.row[s])

        @pl.when(slots.live[s])
        def _():
            copy = pltpu.make_async_copy(cost_hbm.at[0, s], cost_v, sem)
            copy.start()
            copy.wait()
            chunked(other_ref[pl.ds(other_at, 1), :], other8)

            @pl.loop(0, chunks)
            def _(i):
                def step(j, carry):
                    m, total = carry
                    z = tile_z(cost_v, slots.scale[s], other8, i, j, rows_mode)
                    top = jnp.maximum(m, jnp.max(z, axis=0, keepdims=True))
                    total = total * jnp.exp(m - top) + jnp.sum(jnp.exp(z - top), axis=0, keepdims=True)
                    return top, total

                first = (jnp.full((1, 128), NEG, F32), jnp.zeros((1, 128), F32))
                m, total = lax.fori_loop(0, chunks, step, first)
                out8[pl.ds(i, 1), :] = m + jnp.log(total)

            new = jnp.concatenate([out8[c : c + 1, :] for c in range(chunks)], axis=1)
            old = l_ref[pl.ds(out_at, 1), :]
            top = jnp.maximum(old, new)
            l_ref[pl.ds(out_at, 1), :] = top + jnp.log(jnp.exp(old - top) + jnp.exp(new - top))


def piece_of(ref, piece, width):
    per = ref.shape[1] // width
    row = ref[pl.ds(piece // per, 1), :]
    out = row[:, :width]
    for c in range(1, per):
        out = jnp.where(piece % per == c, row[:, c * width : (c + 1) * width], out)
    return out


def to_log(total, shift):
    return jnp.where(total > 0, jnp.log(jnp.maximum(total, 1e-38)) - shift / EPS, NEG)


def sums_fine(low, high, others):
    return (low >= 2.0**-80 * jnp.maximum(others, 1.0)) & (high <= 2.0**100)


def build_kernel(dims, scale, row, col, count, cost_hbm, k_ref, l_ref, ref_ref, cost_v, sums, zero, other8, out8, sems):
    slots = Slots(scale, row, col, count, *dims)
    total = slots.total
    half = cost_v.shape[1] // 2
    copies = [
        [
            pltpu.make_async_copy(
                cost_hbm.at[0, s, pl.ds(h * half, half)], cost_v.at[s, pl.ds(h * half, half)], sems.at[s, h]
            )
            for h in range(2)
        ]
        for s in range(total)
    ]
    for s in range(total):

        @pl.when(slots.live[s])
        def _():
            for h in range(2):
                copies[s][h].start()

    chunk = 32
    ones = jnp.ones((16, cost_v.shape[2]), BF16)

    def build(shift, wait):
        sums[...] = jnp.zeros(sums.shape, F32)
        ref_ref[0, 0] = shift
        ref_ref[0, 1] = 0.0
        ref_ref[0, 2] = jnp.float32(jnp.inf)
        for s in range(total):

            @pl.when(slots.live[s])
            def _():
                for h in range(2):
                    if wait:
                        copies[s][h].wait()

                    @pl.loop(0, half // chunk, unroll=2)
                    def _(i):
                        here = pl.ds(pl.multiple_of(h * half + i * chunk, chunk), chunk)
                        x = cost_v[s, here, :].astype(F32)
                        x = x * (-TO2 * slots.scale[s]) + shift * TO2
                        k_ref[s, here, :] = jnp.exp2(x).astype(BF16)

                part = k_row(ones, k_ref[s])[0:1]
                at = pl.ds(slots.row[s], 1)
                sums[at, :] = sums[at, :] + part
                ref_ref[0, 1] = jnp.maximum(ref_ref[0, 1], jnp.max(part))
                ref_ref[0, 2] = jnp.minimum(ref_ref[0, 2], jnp.min(part))

        l_ref[...] = to_log(sums[...], shift)
        return sums_fine(ref_ref[0, 2], ref_ref[0, 1], ref_ref[0, 1])

    fine = build(jnp.float32(0.0), True)

    @pl.when(jnp.logical_not(fine))
    def _():
        ref_ref[0, 3] = jnp.float32(jnp.inf)
        for s in range(total):

            @pl.when(slots.live[s])
            def _():
                def lowest(i, low):
                    here = pl.ds(pl.multiple_of(i * chunk, chunk), chunk)
                    return jnp.minimum(low, jnp.min(cost_v[s, here, :].astype(F32)))

                low = lax.fori_loop(0, 2 * half // chunk, lowest, jnp.float32(jnp.inf))
                ref_ref[0, 3] = jnp.minimum(ref_ref[0, 3], low * slots.scale[s])

        shifted = build(ref_ref[0, 3], False)

        @pl.when(jnp.logical_not(shifted))
        def _():
            zero[...] = jnp.zeros(zero.shape, F32)
            slow_lse(slots, cost_hbm, cost_v.at[0], sems.at[0, 0], other8, out8, zero, l_ref, True)


def row_kernel(dims, n_parts, scale, row, col, count, ref, log_b, cost_hbm, k_ref, *rest):
    parts, (l_ref, g, sums, stat, cost_v, other8, out8, sem) = rest[:n_parts], rest[n_parts:]
    slots = Slots(scale, row, col, count, *dims)
    g[...] = EPS * log_b[...] - EPS * lse([p[...] for p in parts])
    sums[...] = jnp.zeros(sums.shape, F32)
    stat[0] = jnp.float32(0.0)
    stat[1] = jnp.float32(jnp.inf)
    stat[2] = ref[0, 1]
    for s in range(slots.total):

        @pl.when(slots.live[s])
        def _():
            v = jnp.exp2(g[pl.ds(slots.col[s], 1), :] * TO2)
            part = jnp.sum(k_row(split_rows(v), k_ref[s]), axis=0, keepdims=True)
            at = pl.ds(slots.row[s], 1)
            sums[at, :] = sums[at, :] + part
            stat[0] = jnp.maximum(stat[0], jnp.max(part))
            stat[1] = jnp.minimum(stat[1], jnp.min(part))
            stat[2] = jnp.maximum(stat[2], jnp.max(v))

    l_ref[...] = to_log(sums[...], ref[0, 0])

    @pl.when(jnp.logical_not(sums_fine(stat[1], stat[0], stat[2])))
    def _():
        slow_lse(slots, cost_hbm, cost_v, sem, other8, out8, g, l_ref, True)


def col_kernel(dims, n_parts, scale, row, col, count, ref, log_a, cost_hbm, k_ref, *rest):
    parts, (l_ref, f, sums, stat, cost_v, other8, out8, sem) = rest[:n_parts], rest[n_parts:]
    slots = Slots(scale, row, col, count, *dims)
    f[...] = EPS * log_a[...] - EPS * lse([p[...] for p in parts])
    sums[...] = jnp.zeros(sums.shape, F32)
    stat[0] = jnp.float32(0.0)
    stat[1] = jnp.float32(jnp.inf)
    stat[2] = ref[0, 1]
    for s in range(slots.total):

        @pl.when(slots.live[s])
        def _():
            u = jnp.exp2(f[pl.ds(slots.row[s], 1), :] * TO2)
            part = jnp.sum(k_col(split_rows(u), k_ref[s]), axis=0, keepdims=True)
            at = pl.ds(slots.col[s], 1)
            sums[at, :] = sums[at, :] + part
            stat[0] = jnp.maximum(stat[0], jnp.max(part))
            stat[1] = jnp.minimum(stat[1], jnp.min(part))
            stat[2] = jnp.maximum(stat[2], jnp.max(u))

    l_ref[...] = to_log(sums[...], ref[0, 0])

    @pl.when(jnp.logical_not(sums_fine(stat[1], stat[0], stat[2])))
    def _():
        slow_lse(slots, cost_hbm, cost_v, sem, other8, out8, f, l_ref, False)


def label_kernel(dims, n_parts, n_out, scale, row, col, count, ref, log_a, cost_hbm, k_ref, labels, *rest):
    parts, rest = rest[:n_parts], rest[n_parts:]
    l_ref, f_out, outs, rest = rest[0], rest[1], rest[2 : 2 + n_out], rest[2 + n_out :]
    acc, sums, stat, cost_v, other8, out8, sem = rest
    slots = Slots(scale, row, col, count, *dims)
    classes = acc.shape[1]
    f_out[...] = EPS * log_a[...] - EPS * lse([p[...] for p in parts])
    sums[...] = jnp.zeros(sums.shape, F32)
    acc[...] = jnp.zeros(acc.shape, F32)
    stat[0] = jnp.float32(0.0)
    stat[1] = jnp.float32(jnp.inf)
    stat[2] = ref[0, 1]
    my_outer, my_inner = slots.tgt // INNER, slots.tgt % INNER
    for s in range(slots.total):

        @pl.when(slots.live[s])
        def _():
            u = jnp.exp2(f_out[pl.ds(slots.row[s], 1), :] * TO2)
            outer = slots.row[s] ^ my_outer
            lab = jnp.concatenate([labels[outer, z ^ my_inner] for z in range(INNER)], axis=1)
            weighted = lab.astype(F32) * u
            hi = weighted.astype(BF16)
            low = (weighted - hi.astype(F32)).astype(BF16)
            res = k_col(jnp.concatenate([hi, low, split_rows(u)], axis=0), k_ref[s])
            part = jnp.sum(res[2 * classes :], axis=0, keepdims=True)
            at = pl.ds(slots.col[s], 1)
            sums[at, :] = sums[at, :] + part
            acc[slots.col[s]] = acc[slots.col[s]] + (res[:classes] + res[classes : 2 * classes])
            stat[0] = jnp.maximum(stat[0], jnp.max(part))
            stat[1] = jnp.minimum(stat[1], jnp.min(part))
            stat[2] = jnp.maximum(stat[2], jnp.max(u))

    l_ref[...] = to_log(sums[...], ref[0, 0])

    @pl.when(jnp.logical_not(sums_fine(stat[1], stat[0], stat[2])))
    def _():
        slow_lse(slots, cost_hbm, cost_v, sem, other8, out8, f_out, l_ref, False)
        acc[...] = jnp.zeros(acc.shape, F32)
        sums[...] = jnp.ones(sums.shape, F32)
        chunks = cost_v.shape[0] // 128
        for s in range(slots.total):

            @pl.when(slots.live[s])
            def _():
                copy = pltpu.make_async_copy(cost_hbm.at[0, s], cost_v, sem)
                copy.start()
                copy.wait()
                chunked(f_out[pl.ds(slots.row[s], 1), :], other8)
                chunked(l_ref[pl.ds(slots.col[s], 1), :], out8)

                @pl.loop(0, chunks * chunks)
                def _(ij):
                    i, j = ij // chunks, ij % chunks
                    here = pl.ds(pl.multiple_of(i * 128, 128), 128)
                    z = tile_z(cost_v, slots.scale[s], other8, i, j, False)
                    p = jnp.exp(z - out8[pl.ds(i, 1), :]).astype(BF16)
                    lab = labels[slots.row[s] ^ my_outer, j ^ my_inner]
                    term = jnp.dot(lab, p, preferred_element_type=F32)
                    acc[slots.col[s], :, here] = acc[slots.col[s], :, here] + term

    width = outs[0].shape[1]
    per = acc.shape[2] // width
    for k in range(n_out):
        piece = slots.src ^ k
        here = pl.ds(pl.multiple_of((piece % per) * width, width), width)
        total = piece_of(sums, piece, width)
        inv = jnp.where(total > 0, 1.0 / jnp.maximum(total, 1e-38), 0.0)
        outs[k][...] = (acc[piece // per, :, here] * inv).astype(BF16)


def combine_kernel(n_src, log_b, *rest):
    means, parts, (g_out, out) = rest[:n_src], rest[n_src : 2 * n_src], rest[2 * n_src :]
    src = lax.axis_index("src")
    total = lse([p[...] for p in parts])
    g_out[...] = EPS * log_b[...] - EPS * total
    width = out.shape[1]
    ls = [piece_of(p, src, width) for p in parts]
    top = lse(ls) - piece_of(log_b, src, width)
    out[...] = tree_sum([means[k][...].astype(F32) * jnp.exp(ls[k] - top) for k in range(n_src)]).astype(BF16)


def assemble_kernel(n_src, *refs):
    pieces, out = refs[:n_src], refs[n_src]
    src = lax.axis_index("src")
    width = pieces[0].shape[1]
    for k in range(n_src):
        out[:, pl.ds(pl.multiple_of((src ^ k) * width, width), width)] = pieces[k][...]


VM = pl.BlockSpec(memory_space=pltpu.VMEM)
SM = pl.BlockSpec(memory_space=pltpu.SMEM)
HB = pl.BlockSpec(memory_space=pltpu.HBM)
PARAMS = pltpu.CompilerParams(vmem_limit_bytes=LIMIT)


def local(cost, cost_scale, slot_block_row, slot_block_column, device_block_count, log_a, log_b, labels):
    n_src, n_tgt = lax.axis_size("src"), lax.axis_size("tgt")
    slots, tile = cost.shape[1], cost.shape[2]
    rb, cb = log_a.shape[0] // tile, log_b.shape[0] // tile
    classes = labels.shape[1]
    dims = (rb, cb, slots)
    scalars = (cost_scale, slot_block_row, slot_block_column, device_block_count)
    log_a = log_a.reshape(rb, tile)
    log_b = log_b.reshape(cb, tile)
    outer = n_tgt // INNER

    lab = jnp.stack(xor_exchange(labels.T, "tgt", n_tgt, range(1, INNER)))
    lab = jnp.stack(xor_exchange(lab, "tgt", n_tgt, [k * INNER for k in range(1, outer)]))

    k_type = pltpu.VMEM((slots, tile, tile), BF16)
    vec = functools.partial(jax.ShapeDtypeStruct, dtype=F32)
    chunks = pltpu.VMEM((tile // 128, 128), F32)
    slow = [pltpu.VMEM((tile, tile), BF16), chunks, chunks, pltpu.SemaphoreType.DMA]
    work = [pltpu.SMEM((3,), F32)] + slow

    k_all, row_l, ref = pl.pallas_call(
        functools.partial(build_kernel, dims),
        out_shape=(k_type, vec((rb, tile)), vec((1, 4))),
        in_specs=[SM] * 4 + [HB],
        out_specs=(VM, VM, SM),
        scratch_shapes=[
            pltpu.VMEM((slots, tile, tile), BF16),
            pltpu.VMEM((rb, tile), F32),
            pltpu.VMEM((cb, tile), F32),
            chunks,
            chunks,
            pltpu.SemaphoreType.DMA((slots, 2)),
        ],
        compiler_params=PARAMS,
    )(*scalars, cost)
    k_all = pltpu.with_memory_space_constraint(k_all, pltpu.VMEM)
    common = [SM] * 5 + [VM, HB, VM]

    def row_exchange(part):
        part = lse(xor_exchange(part, "tgt", n_tgt, range(1, INNER)))
        return xor_exchange(part, "tgt", n_tgt, [k * INNER for k in range(1, outer)])

    for step in range(ITERS):
        row_parts = row_exchange(row_l)
        if step == ITERS - 1:
            break
        col_l = pl.pallas_call(
            functools.partial(col_kernel, dims, outer),
            out_shape=vec((cb, tile)),
            in_specs=common + [VM] * outer,
            out_specs=VM,
            scratch_shapes=[pltpu.VMEM((rb, tile), F32), pltpu.VMEM((cb, tile), F32)] + work,
            compiler_params=PARAMS,
        )(*scalars, ref, log_a, cost, k_all, *row_parts)
        col_parts = xor_exchange(col_l, "src", n_src, range(1, n_src))
        row_l = pl.pallas_call(
            functools.partial(row_kernel, dims, n_src),
            out_shape=vec((rb, tile)),
            in_specs=common + [VM] * n_src,
            out_specs=VM,
            scratch_shapes=[pltpu.VMEM((cb, tile), F32), pltpu.VMEM((rb, tile), F32)] + work,
            compiler_params=PARAMS,
        )(*scalars, ref, log_b, cost, k_all, *col_parts)

    width = cb * tile // n_src
    piece = jax.ShapeDtypeStruct((classes, width), BF16)
    col_l, f_pot, *means = pl.pallas_call(
        functools.partial(label_kernel, dims, outer, n_src),
        out_shape=(vec((cb, tile)), vec((rb, tile))) + (piece,) * n_src,
        in_specs=common + [VM] + [VM] * outer,
        out_specs=(VM,) * (2 + n_src),
        scratch_shapes=[pltpu.VMEM((cb, classes, tile), F32), pltpu.VMEM((cb, tile), F32)] + work,
        compiler_params=PARAMS,
    )(*scalars, ref, log_a, cost, k_all, lab, *row_parts)
    col_parts = xor_exchange(col_l, "src", n_src, range(1, n_src))
    means = [means[0]] + [
        lax.ppermute(means[k], "src", [(i, i ^ k) for i in range(n_src)]) for k in range(1, n_src)
    ]
    g_pot, out = pl.pallas_call(
        functools.partial(combine_kernel, n_src),
        out_shape=(vec((cb, tile)), piece),
        in_specs=[VM] * (1 + 2 * n_src),
        out_specs=(VM, VM),
        compiler_params=PARAMS,
    )(log_b, *means, *col_parts)
    out = pl.pallas_call(
        functools.partial(assemble_kernel, n_src),
        out_shape=jax.ShapeDtypeStruct((classes, cb * tile), BF16),
        in_specs=[VM] * n_src,
        out_specs=VM,
        compiler_params=PARAMS,
    )(*xor_exchange(out, "src", n_src, range(1, n_src)))
    return f_pot.reshape(-1), g_pot.reshape(-1), out.T


def solution(mesh):
    in_specs = (
        P("src", "tgt", None, None),
        P("src", "tgt"),
        P("src", "tgt"),
        P("src", "tgt"),
        P("src", "tgt"),
        P("src"),
        P("tgt"),
        P(("src", "tgt"), None),
    )
    out_specs = (P("src"), P("tgt"), P("tgt", None))
    return jax.shard_map(local, mesh=mesh, in_specs=in_specs, out_specs=out_specs, check_vma=False)
```

time: 1540 us -> 520 us (0.34)
  blocking collectives: 1400 us -> 0 us
  starting transfers between devices: 0 us -> 249 us
  Pallas kernels: 0 us -> 214 us
  other arithmetic: 110 us -> 0.33 us
  waiting for transfers between devices: 0 us -> 26.3 us
    pmax x8 -> x0, blocking collectives: 760 us -> none  [the longest x4 450 us: local(): row_top = lax.pmax(row_m, 'tgt')]
    psum x9 -> x0, blocking collectives: 601 us -> none  [the longest x4 442 us: local(): row_total = lax.psum(row_s * jnp.exp(row_m - row_top), 'tgt')]
    ppermute x0 -> x92, starting transfers between devices: none -> 249 us  [the longest x85 210 us: xor_exchange(): lax.ppermute(x, axis, [(i, i ^ k) for i in range(size)])]
    pallas_call x0 -> x10, Pallas kernels: none -> 214 us  [the longest x3 64.5 us: local(): pl.pallas_call(functools.partial(row_kernel, dims, n_src), out_shape=vec(...]
    reduce_sum x15 -> x0, other arithmetic: 82 us -> none  [local_lse(): jnp.sum(jnp.exp(z_vals - jnp.expand_dims(block_max, axis_id)), axis=axis_id)]
    all_gather x1 -> x0, blocking collectives: 35.3 us -> none  [local(): label_block = lax.all_gather(labels, 'tgt', axis=0, tiled=True)]
    reduce_max x8 -> x0, other arithmetic: 27.6 us -> none  [local_lse(): block_max = jnp.max(z_vals, axis=axis_id)]
    ppermute x0 -> x92, waiting for transfers between devices: none -> 26.3 us  [the longest x85 21.7 us: xor_exchange(): lax.ppermute(x, axis, [(i, i ^ k) for i in range(size)])]
  transfers between devices with their start and end apart: 0 -> 92, of which waited for: 0 -> 32; matrix products, arithmetic and copies ran while one was open for 0% -> 0% of each run, Pallas kernels for 0% -> 12%
where the time goes in v1:
time: 520 us; the launch traced here: 511 us
  starting transfers between devices  249 us (48%)
  Pallas kernels  214 us (41%)
  waiting for transfers between devices  26.3 us (5%)
  local copies, waits for them, and re-layouts  19.2 us (4%)
    ppermute x85, starting transfers between devices, xor_exchange(): lax.ppermute(x, axis, [(i, i ^ k) for i in range(size)])  210 us
    pallas_call x3, Pallas kernels, local(): pl.pallas_call(functools.partial(row_kernel, dims, n_src), out_shape=vec(...  64.5 us
    pallas_call x3, Pallas kernels, local(): pl.pallas_call(functools.partial(col_kernel, dims, outer), out_shape=vec(...  62 us
    pallas_call x1, Pallas kernels, local(): pl.pallas_call(functools.partial(label_kernel, dims, outer, n_src), out_s...  50.8 us
    ppermute x7, starting transfers between devices, local(): lax.ppermute(means[k], 'src', [(i, i ^ k) for i in range(n_src)])  39.2 us
    pallas_call x1, Pallas kernels, local(): pl.pallas_call(functools.partial(build_kernel, dims), out_shape=(k_type,...  35.8 us
    ppermute x85, waiting for transfers between devices, xor_exchange(): lax.ppermute(x, axis, [(i, i ^ k) for i in range(size)])  21.7 us
    unnamed x37, local copies, waits for them, and re-layouts  18.5 us
  transfers between devices with their start and end apart: 92, of which 32 were waited for; matrix products, arithmetic and copies ran while one was open for 0% of the time, Pallas kernels for 12%

profile of v1, /device:TPU:1, one launch (start us, length us, event | category | flops | bytes accessed | tf_op | source)
XLA Modules:
  0.0 511.1 jit_solution(7937073896133007806)
XLA Ops:
  6.1 35.8 %shard_map.103 = (bf16[3,1024,1024]{2,1,0:T(8,128)(2,1)S(1)}, f32[4,1024]{1,0:T(4,128)S(1)}, f32[1,4]{1,0:T(1,128)S(1)}) custom-call(f32[1,3]{1,0:T(1,128)S(1)} %copy-done.6, s32[1,3]{1,0:T(1,128)S(1)} %copy-done.8, s32[1,3]{1,0:T(1,128)S(1)} %copy-done.10, s32[1,1]{1,0:T(1,128)S(6)} %copy.22.count, bf16[1,3,1024,1024]{3,2,1,0:T(8,128)(2,1)S(1)} %copy-done), custom_call_target="tpu_custom_call" | custom-call | tf_op jit(solution)/shard_map/pallas_call | solution.py:375
  44.5 23.0 %collective-permute-start.15 = (f32[4,1024]{1,0:T(4,128)S(1)}, f32[4,1024]{1,0:T(4,128)S(1)}, u32[]{:S(2)}, u32[]{:S(2)}) collective-permute-start(f32[4,1024]{1,0:T(4,128)S(1)} %get-tuple-element.20), channel_id=1, source_target_pairs={{0,6},{1,7},{2,4},{3,5},{4,2},{5,3},{6,0},{7,1},{8,14},{9,15},{10,... | collective-permute-start | bytes 49160 | tf_op jit(solution)/shard_map/ppermute | solution.py:32
  71.0 3.6 collective-permute-start.11
  77.9 3.6 collective-permute-start.19
  82.6 3.0 collective-permute-done.18.rest_2_
  91.1 20.7 %shard_map.104.rest_0_ = f32[4,1024]{1,0:T(4,128)S(1)} custom-call(f32[1,3]{1,0:T(1,128)S(1)} %copy-done.7, s32[1,3]{1,0:T(1,128)S(1)} %copy-done.9, s32[1,3]{1,0:T(1,128)S(1)} %copy-done.11, s32[1,1]{1,0:T(1,128)S(6)} %copy.22.count, f32[1,4]{1,0:T(1,128)S(1)} %get-tuple-element.18.ref, f32[4,1024]{1,0:T(4,128)S(1)} %reshape.18.log_a, ...), custom_call_target="tpu_custom_call" | custom-call | tf_op jit(solution)/shard_map/pallas_call | solution.py:401
  111.8 6.7 %collective-permute-start.26 = (f32[4,1024]{1,0:T(4,128)S(1)}, f32[4,1024]{1,0:T(4,128)S(1)}, u32[]{:S(2)}, u32[]{:S(2)}) collective-permute-start(f32[4,1024]{1,0:T(4,128)S(1)} %shard_map.104.rest_0_), channel_id=1, source_target_pairs={{0,224},{32,192},{64,160},{96,128},{128,96},{160,64},{192,32},{224... | collective-permute-start | bytes 49160 | tf_op jit(solution)/shard_map/ppermute | solution.py:32
  118.5 10.7 %collective-permute-start.25 = (f32[4,1024]{1,0:T(4,128)S(1)}, f32[4,1024]{1,0:T(4,128)S(1)}, u32[]{:S(2)}, u32[]{:S(2)}) collective-permute-start(f32[4,1024]{1,0:T(4,128)S(1)} %shard_map.104.rest_0_), channel_id=1, source_target_pairs={{0,192},{32,224},{64,128},{96,160},{128,64},{160,96},{192,0},{224,... | collective-permute-start | bytes 49160 | tf_op jit(solution)/shard_map/ppermute | solution.py:32
  130.9 3.7 collective-permute-start.21
  136.0 2.8 copy-done.2
  141.5 21.5 %shard_map.105 = f32[4,1024]{1,0:T(4,128)S(1)} custom-call(f32[1,3]{1,0:T(1,128)S(1)} %copy-done.7, s32[1,3]{1,0:T(1,128)S(1)} %copy-done.9, s32[1,3]{1,0:T(1,128)S(1)} %copy-done.11, s32[1,1]{1,0:T(1,128)S(6)} %copy.22.count, f32[1,4]{1,0:T(1,128)S(1)} %get-tuple-element.18.ref, f32[4,1024]{1,0:T(4,128)S(1)} %reshape.19.log_b, ...), custom_call_target="tpu_custom_call" | custom-call | tf_op jit(solution)/shard_map/pallas_call | solution.py:410
  163.1 14.4 %collective-permute-start.32 = (f32[4,1024]{1,0:T(4,128)S(1)}, f32[4,1024]{1,0:T(4,128)S(1)}, u32[]{:S(2)}, u32[]{:S(2)}) collective-permute-start(f32[4,1024]{1,0:T(4,128)S(1)} %shard_map.105), channel_id=1, source_target_pairs={{0,6},{1,7},{2,4},{3,5},{4,2},{5,3},{6,0},{7,1},{8,14},{9,15},{10,... | collective-permute-start | bytes 49160 | tf_op jit(solution)/shard_map/ppermute | solution.py:32
  180.3 4.1 collective-permute-start.28
  192.2 20.7 %shard_map.106.rest_0_ = f32[4,1024]{1,0:T(4,128)S(1)} custom-call(f32[1,3]{1,0:T(1,128)S(1)} %copy-done.7, s32[1,3]{1,0:T(1,128)S(1)} %copy-done.9, s32[1,3]{1,0:T(1,128)S(1)} %copy-done.11, s32[1,1]{1,0:T(1,128)S(6)} %copy.22.count, f32[1,4]{1,0:T(1,128)S(1)} %get-tuple-element.18.ref, f32[4,1024]{1,0:T(4,128)S(1)} %reshape.18.log_a, ...), custom_call_target="tpu_custom_call" | custom-call | tf_op jit(solution)/shard_map/pallas_call | solution.py:401
  212.8 7.4 %collective-permute-start.43 = (f32[4,1024]{1,0:T(4,128)S(1)}, f32[4,1024]{1,0:T(4,128)S(1)}, u32[]{:S(2)}, u32[]{:S(2)}) collective-permute-start(f32[4,1024]{1,0:T(4,128)S(1)} %shard_map.106.rest_0_), channel_id=1, source_target_pairs={{0,224},{32,192},{64,160},{96,128},{128,96},{160,64},{192,32},{224... | collective-permute-start | bytes 49160 | tf_op jit(solution)/shard_map/ppermute | solution.py:32
  220.3 10.7 %collective-permute-start.42 = (f32[4,1024]{1,0:T(4,128)S(1)}, f32[4,1024]{1,0:T(4,128)S(1)}, u32[]{:S(2)}, u32[]{:S(2)}) collective-permute-start(f32[4,1024]{1,0:T(4,128)S(1)} %shard_map.106.rest_0_), channel_id=1, source_target_pairs={{0,192},{32,224},{64,128},{96,160},{128,64},{160,96},{192,0},{224,... | collective-permute-start | bytes 49160 | tf_op jit(solution)/shard_map/ppermute | solution.py:32
  231.3 3.2 collective-permute-start.40
  238.4 21.5 %shard_map.107 = f32[4,1024]{1,0:T(4,128)S(1)} custom-call(f32[1,3]{1,0:T(1,128)S(1)} %copy-done.7, s32[1,3]{1,0:T(1,128)S(1)} %copy-done.9, s32[1,3]{1,0:T(1,128)S(1)} %copy-done.11, s32[1,1]{1,0:T(1,128)S(6)} %copy.22.count, f32[1,4]{1,0:T(1,128)S(1)} %get-tuple-element.18.ref, f32[4,1024]{1,0:T(4,128)S(1)} %reshape.19.log_b, ...), custom_call_target="tpu_custom_call" | custom-call | tf_op jit(solution)/shard_map/pallas_call | solution.py:410
  260.0 14.6 %collective-permute-start.49 = (f32[4,1024]{1,0:T(4,128)S(1)}, f32[4,1024]{1,0:T(4,128)S(1)}, u32[]{:S(2)}, u32[]{:S(2)}) collective-permute-start(f32[4,1024]{1,0:T(4,128)S(1)} %shard_map.107), channel_id=1, source_target_pairs={{0,6},{1,7},{2,4},{3,5},{4,2},{5,3},{6,0},{7,1},{8,14},{9,15},{10,... | collective-permute-start | bytes 49160 | tf_op jit(solution)/shard_map/ppermute | solution.py:32
  277.4 4.1 collective-permute-start.45
  282.6 4.1 collective-permute-start.3
  294.4 20.7 %shard_map.108.rest_0_ = f32[4,1024]{1,0:T(4,128)S(1)} custom-call(f32[1,3]{1,0:T(1,128)S(1)} %copy-done.7, s32[1,3]{1,0:T(1,128)S(1)} %copy-done.9, s32[1,3]{1,0:T(1,128)S(1)} %copy-done.11, s32[1,1]{1,0:T(1,128)S(6)} %copy.22.count, f32[1,4]{1,0:T(1,128)S(1)} %get-tuple-element.18.ref, f32[4,1024]{1,0:T(4,128)S(1)} %reshape.18.log_a, ...), custom_call_target="tpu_custom_call" | custom-call | tf_op jit(solution)/shard_map/pallas_call | solution.py:401
  315.1 7.1 %collective-permute-start.60 = (f32[4,1024]{1,0:T(4,128)S(1)}, f32[4,1024]{1,0:T(4,128)S(1)}, u32[]{:S(2)}, u32[]{:S(2)}) collective-permute-start(f32[4,1024]{1,0:T(4,128)S(1)} %shard_map.108.rest_0_), channel_id=1, source_target_pairs={{0,224},{32,192},{64,160},{96,128},{128,96},{160,64},{192,32},{224... | collective-permute-start | bytes 49160 | tf_op jit(solution)/shard_map/ppermute | solution.py:32
  322.2 10.6 %collective-permute-start.59 = (f32[4,1024]{1,0:T(4,128)S(1)}, f32[4,1024]{1,0:T(4,128)S(1)}, u32[]{:S(2)}, u32[]{:S(2)}) collective-permute-start(f32[4,1024]{1,0:T(4,128)S(1)} %shard_map.108.rest_0_), channel_id=1, source_target_pairs={{0,192},{32,224},{64,128},{96,160},{128,64},{160,96},{192,0},{224,... | collective-permute-start | bytes 49160 | tf_op jit(solution)/shard_map/ppermute | solution.py:32
  334.4 3.4 collective-permute-start.55
  337.9 4.3 collective-permute-start.6
  342.2 21.5 %shard_map.109 = f32[4,1024]{1,0:T(4,128)S(1)} custom-call(f32[1,3]{1,0:T(1,128)S(1)} %copy-done.7, s32[1,3]{1,0:T(1,128)S(1)} %copy-done.9, s32[1,3]{1,0:T(1,128)S(1)} %copy-done.11, s32[1,1]{1,0:T(1,128)S(6)} %copy.22.count, f32[1,4]{1,0:T(1,128)S(1)} %get-tuple-element.18.ref, f32[4,1024]{1,0:T(4,128)S(1)} %reshape.19.log_b, ...), custom_call_target="tpu_custom_call" | custom-call | tf_op jit(solution)/shard_map/pallas_call | solution.py:410
  363.8 12.5 %collective-permute-start.66 = (f32[4,1024]{1,0:T(4,128)S(1)}, f32[4,1024]{1,0:T(4,128)S(1)}, u32[]{:S(2)}, u32[]{:S(2)}) collective-permute-start(f32[4,1024]{1,0:T(4,128)S(1)} %shard_map.109), channel_id=1, source_target_pairs={{0,6},{1,7},{2,4},{3,5},{4,2},{5,3},{6,0},{7,1},{8,14},{9,15},{10,... | collective-permute-start | bytes 49160 | tf_op jit(solution)/shard_map/ppermute | solution.py:32
  380.3 3.5 collective-permute-start.62
  393.2 50.8 %shard_map.110 = (f32[4,1024]{1,0:T(4,128)S(1)}, f32[4,1024]{1,0:T(4,128)S(1)}, bf16[64,512]{1,0:T(8,128)(2,1)S(1)}, bf16[64,512]{1,0:T(8,128)(2,1)S(1)}, bf16[6...) custom-call(f32[1,3]{1,0:T(1,128)S(1)} %copy-done.7, ...), custom_call_target="tpu_custom_call" | custom-call | tf_op jit(solution)/shard_map/pallas_call | solution.py:421
  444.0 32.5 %collective-permute-start.71 = (bf16[64,512]{1,0:T(8,128)(2,1)S(1)}, bf16[64,512]{1,0:T(8,128)(2,1)S(1)}, u32[]{:S(2)}, u32[]{:S(2)}) collective-permute-start(bf16[64,512]{1,0:T(8,128)(2,1)S(1)} %get-tuple-element.23), channel_id=1, source_target_pairs={{0,32},{32,0},{64,96},{96,64},{128,160},{160,128},{192,224},{224,1... | collective-permute-start | bytes 196616 | tf_op jit(solution)/shard_map/ppermute | solution.py:431
  501.2 3.1 collective-permute-start.88
  (208 shorter events, 99.4 us)
Async XLA Ops:
  44.5 26.5 %collective-permute-start.16 = (f32[4,1024]{1,0:T(4,128)S(1)}, f32[4,1024]{1,0:T(4,128)S(1)}, u32[]{:S(2)}, u32[]{:S(2)}) collective-permute-start(f32[4,1024]{1,0:T(4,128)S(1)} %get-tuple-element.20), channel_id=1, source_target_pairs={{0,7},{1,6},{2,5},{3,4},{4,3},{5,2},{6,1},{7,0},{8,15},{9,14},{10,... | collective-permute-start | bytes 49160 | tf_op jit(solution)/shard_map/ppermute | solution.py:32
  44.5 30.1 %collective-permute-start.15 = (f32[4,1024]{1,0:T(4,128)S(1)}, f32[4,1024]{1,0:T(4,128)S(1)}, u32[]{:S(2)}, u32[]{:S(2)}) collective-permute-start(f32[4,1024]{1,0:T(4,128)S(1)} %get-tuple-element.20), channel_id=1, source_target_pairs={{0,6},{1,7},{2,4},{3,5},{4,2},{5,3},{6,0},{7,1},{8,14},{9,15},{10,... | collective-permute-start | bytes 49160 | tf_op jit(solution)/shard_map/ppermute | solution.py:32
  67.6 7.4 %collective-permute-start.14 = (f32[4,1024]{1,0:T(4,128)S(1)}, f32[4,1024]{1,0:T(4,128)S(1)}, u32[]{:S(2)}, u32[]{:S(2)}) collective-permute-start(f32[4,1024]{1,0:T(4,128)S(1)} %get-tuple-element.20), channel_id=1, source_target_pairs={{0,5},{1,4},{2,7},{3,6},{4,1},{5,0},{6,3},{7,2},{8,13},{9,12},{10,... | collective-permute-start | bytes 49160 | tf_op jit(solution)/shard_map/ppermute | solution.py:32
  111.8 19.1 %collective-permute-start.26 = (f32[4,1024]{1,0:T(4,128)S(1)}, f32[4,1024]{1,0:T(4,128)S(1)}, u32[]{:S(2)}, u32[]{:S(2)}) collective-permute-start(f32[4,1024]{1,0:T(4,128)S(1)} %shard_map.104.rest_0_), channel_id=1, source_target_pairs={{0,224},{32,192},{64,160},{96,128},{128,96},{160,64},{192,32},{224... | collective-permute-start | bytes 49160 | tf_op jit(solution)/shard_map/ppermute | solution.py:32
  118.5 16.0 %collective-permute-start.25 = (f32[4,1024]{1,0:T(4,128)S(1)}, f32[4,1024]{1,0:T(4,128)S(1)}, u32[]{:S(2)}, u32[]{:S(2)}) collective-permute-start(f32[4,1024]{1,0:T(4,128)S(1)} %shard_map.104.rest_0_), channel_id=1, source_target_pairs={{0,192},{32,224},{64,128},{96,160},{128,64},{160,96},{192,0},{224,... | collective-permute-start | bytes 49160 | tf_op jit(solution)/shard_map/ppermute | solution.py:32
  163.0 17.3 %collective-permute-start.33 = (f32[4,1024]{1,0:T(4,128)S(1)}, f32[4,1024]{1,0:T(4,128)S(1)}, u32[]{:S(2)}, u32[]{:S(2)}) collective-permute-start(f32[4,1024]{1,0:T(4,128)S(1)} %shard_map.105), channel_id=1, source_target_pairs={{0,7},{1,6},{2,5},{3,4},{4,3},{5,2},{6,1},{7,0},{8,15},{9,14},{10,... | collective-permute-start | bytes 49160 | tf_op jit(solution)/shard_map/ppermute | solution.py:32
  163.1 21.3 %collective-permute-start.32 = (f32[4,1024]{1,0:T(4,128)S(1)}, f32[4,1024]{1,0:T(4,128)S(1)}, u32[]{:S(2)}, u32[]{:S(2)}) collective-permute-start(f32[4,1024]{1,0:T(4,128)S(1)} %shard_map.105), channel_id=1, source_target_pairs={{0,6},{1,7},{2,4},{3,5},{4,2},{5,3},{6,0},{7,1},{8,14},{9,15},{10,... | collective-permute-start | bytes 49160 | tf_op jit(solution)/shard_map/ppermute | solution.py:32
  212.8 21.7 %collective-permute-start.43 = (f32[4,1024]{1,0:T(4,128)S(1)}, f32[4,1024]{1,0:T(4,128)S(1)}, u32[]{:S(2)}, u32[]{:S(2)}) collective-permute-start(f32[4,1024]{1,0:T(4,128)S(1)} %shard_map.106.rest_0_), channel_id=1, source_target_pairs={{0,224},{32,192},{64,160},{96,128},{128,96},{160,64},{192,32},{224... | collective-permute-start | bytes 49160 | tf_op jit(solution)/shard_map/ppermute | solution.py:32
  220.3 14.8 %collective-permute-start.42 = (f32[4,1024]{1,0:T(4,128)S(1)}, f32[4,1024]{1,0:T(4,128)S(1)}, u32[]{:S(2)}, u32[]{:S(2)}) collective-permute-start(f32[4,1024]{1,0:T(4,128)S(1)} %shard_map.106.rest_0_), channel_id=1, source_target_pairs={{0,192},{32,224},{64,128},{96,160},{128,64},{160,96},{192,0},{224,... | collective-permute-start | bytes 49160 | tf_op jit(solution)/shard_map/ppermute | solution.py:32
  231.2 43.5 %collective-permute-start = (bf16[64,128]{1,0:T(8,128)(2,1)S(1)}, bf16[64,128]{1,0:T(8,128)(2,1)S(1)}, u32[]{:S(2)}, u32[]{:S(2)}) collective-permute-start(bf16[64,128]{1,0:T(8,128)(2,1)S(1)} %bitcast.36), channel_id=1, source_target_pairs={{0,1},{1,0},{2,3},{3,2},{4,5},{5,4},{6,7},{7,6},{8,9},{9,8},{10,11... | collective-permute-start | bytes 49160 | tf_op jit(solution)/shard_map/ppermute | solution.py:32
  236.7 39.0 %collective-permute-start.1 = (bf16[64,128]{1,0:T(8,128)(2,1)S(1)}, bf16[64,128]{1,0:T(8,128)(2,1)S(1)}, u32[]{:S(2)}, u32[]{:S(2)}) collective-permute-start(bf16[64,128]{1,0:T(8,128)(2,1)S(1)} %bitcast.37), channel_id=1, source_target_pairs={{0,2},{1,3},{2,0},{3,1},{4,6},{5,7},{6,4},{7,5},{8,10},{9,11},{10,... | collective-permute-start | bytes 49160 | tf_op jit(solution)/shard_map/ppermute | solution.py:32
  259.9 17.4 %collective-permute-start.50 = (f32[4,1024]{1,0:T(4,128)S(1)}, f32[4,1024]{1,0:T(4,128)S(1)}, u32[]{:S(2)}, u32[]{:S(2)}) collective-permute-start(f32[4,1024]{1,0:T(4,128)S(1)} %shard_map.107), channel_id=1, source_target_pairs={{0,7},{1,6},{2,5},{3,4},{4,3},{5,2},{6,1},{7,0},{8,15},{9,14},{10,... | collective-permute-start | bytes 49160 | tf_op jit(solution)/shard_map/ppermute | solution.py:32
  260.0 21.4 %collective-permute-start.49 = (f32[4,1024]{1,0:T(4,128)S(1)}, f32[4,1024]{1,0:T(4,128)S(1)}, u32[]{:S(2)}, u32[]{:S(2)}) collective-permute-start(f32[4,1024]{1,0:T(4,128)S(1)} %shard_map.107), channel_id=1, source_target_pairs={{0,6},{1,7},{2,4},{3,5},{4,2},{5,3},{6,0},{7,1},{8,14},{9,15},{10,... | collective-permute-start | bytes 49160 | tf_op jit(solution)/shard_map/ppermute | solution.py:32
  275.1 7.4 %collective-permute-start.47 = (f32[4,1024]{1,0:T(4,128)S(1)}, f32[4,1024]{1,0:T(4,128)S(1)}, u32[]{:S(2)}, u32[]{:S(2)}) collective-permute-start(f32[4,1024]{1,0:T(4,128)S(1)} %shard_map.107), channel_id=1, source_target_pairs={{0,4},{1,5},{2,6},{3,7},{4,0},{5,1},{6,2},{7,3},{8,12},{9,13},{10,... | collective-permute-start | bytes 49160 | tf_op jit(solution)/shard_map/ppermute | solution.py:32
  275.7 10.9 %collective-permute-start.46 = (f32[4,1024]{1,0:T(4,128)S(1)}, f32[4,1024]{1,0:T(4,128)S(1)}, u32[]{:S(2)}, u32[]{:S(2)}) collective-permute-start(f32[4,1024]{1,0:T(4,128)S(1)} %shard_map.107), channel_id=1, source_target_pairs={{0,3},{1,2},{2,1},{3,0},{4,7},{5,6},{6,5},{7,4},{8,11},{9,10},{10,... | collective-permute-start | bytes 49160 | tf_op jit(solution)/shard_map/ppermute | solution.py:32
  277.4 11.0 %collective-permute-start.45 = (f32[4,1024]{1,0:T(4,128)S(1)}, f32[4,1024]{1,0:T(4,128)S(1)}, u32[]{:S(2)}, u32[]{:S(2)}) collective-permute-start(f32[4,1024]{1,0:T(4,128)S(1)} %shard_map.107), channel_id=1, source_target_pairs={{0,2},{1,3},{2,0},{3,1},{4,6},{5,7},{6,4},{7,5},{8,10},{9,11},{10,... | collective-permute-start | bytes 49160 | tf_op jit(solution)/shard_map/ppermute | solution.py:32
  281.5 94.8 %collective-permute-start.5 = (bf16[64,128]{1,0:T(8,128)(2,1)S(1)}, bf16[64,128]{1,0:T(8,128)(2,1)S(1)}, u32[]{:S(2)}, u32[]{:S(2)}) collective-permute-start(bf16[64,128]{1,0:T(8,128)(2,1)S(1)} %bitcast.38), channel_id=1, source_target_pairs={{0,6},{1,7},{2,4},{3,5},{4,2},{5,3},{6,0},{7,1},{8,14},{9,15},{10,... | collective-permute-start | bytes 49160 | tf_op jit(solution)/shard_map/ppermute | solution.py:32
  282.6 50.3 %collective-permute-start.3 = (bf16[64,128]{1,0:T(8,128)(2,1)S(1)}, bf16[64,128]{1,0:T(8,128)(2,1)S(1)}, u32[]{:S(2)}, u32[]{:S(2)}) collective-permute-start(bf16[64,128]{1,0:T(8,128)(2,1)S(1)} %bitcast.39), channel_id=1, source_target_pairs={{0,4},{1,5},{2,6},{3,7},{4,0},{5,1},{6,2},{7,3},{8,12},{9,13},{10,... | collective-permute-start | bytes 49160 | tf_op jit(solution)/shard_map/ppermute | solution.py:32
  292.3 40.6 %collective-permute-start.4 = (bf16[64,128]{1,0:T(8,128)(2,1)S(1)}, bf16[64,128]{1,0:T(8,128)(2,1)S(1)}, u32[]{:S(2)}, u32[]{:S(2)}) collective-permute-start(bf16[64,128]{1,0:T(8,128)(2,1)S(1)} %bitcast.41), channel_id=1, source_target_pairs={{0,5},{1,4},{2,7},{3,6},{4,1},{5,0},{6,3},{7,2},{8,13},{9,12},{10,... | collective-permute-start | bytes 49160 | tf_op jit(solution)/shard_map/ppermute | solution.py:32
  315.1 18.3 %collective-permute-start.60 = (f32[4,1024]{1,0:T(4,128)S(1)}, f32[4,1024]{1,0:T(4,128)S(1)}, u32[]{:S(2)}, u32[]{:S(2)}) collective-permute-start(f32[4,1024]{1,0:T(4,128)S(1)} %shard_map.108.rest_0_), channel_id=1, source_target_pairs={{0,224},{32,192},{64,160},{96,128},{128,96},{160,64},{192,32},{224... | collective-permute-start | bytes 49160 | tf_op jit(solution)/shard_map/ppermute | solution.py:32
  322.2 12.2 %collective-permute-start.59 = (f32[4,1024]{1,0:T(4,128)S(1)}, f32[4,1024]{1,0:T(4,128)S(1)}, u32[]{:S(2)}, u32[]{:S(2)}) collective-permute-start(f32[4,1024]{1,0:T(4,128)S(1)} %shard_map.108.rest_0_), channel_id=1, source_target_pairs={{0,192},{32,224},{64,128},{96,160},{128,64},{160,96},{192,0},{224,... | collective-permute-start | bytes 49160 | tf_op jit(solution)/shard_map/ppermute | solution.py:32
  333.4 8.8 %collective-permute-start.56 = (f32[4,1024]{1,0:T(4,128)S(1)}, f32[4,1024]{1,0:T(4,128)S(1)}, u32[]{:S(2)}, u32[]{:S(2)}) collective-permute-start(f32[4,1024]{1,0:T(4,128)S(1)} %shard_map.108.rest_0_), channel_id=1, source_target_pairs={{0,96},{32,64},{64,32},{96,0},{128,224},{160,192},{192,160},{224,1... | collective-permute-start | bytes 49160 | tf_op jit(solution)/shard_map/ppermute | solution.py:32
  334.4 7.7 %collective-permute-start.55 = (f32[4,1024]{1,0:T(4,128)S(1)}, f32[4,1024]{1,0:T(4,128)S(1)}, u32[]{:S(2)}, u32[]{:S(2)}) collective-permute-start(f32[4,1024]{1,0:T(4,128)S(1)} %shard_map.108.rest_0_), channel_id=1, source_target_pairs={{0,64},{32,96},{64,0},{96,32},{128,192},{160,224},{192,128},{224,1... | collective-permute-start | bytes 49160 | tf_op jit(solution)/shard_map/ppermute | solution.py:32
  337.9 40.3 %collective-permute-start.6 = (bf16[64,128]{1,0:T(8,128)(2,1)S(1)}, bf16[64,128]{1,0:T(8,128)(2,1)S(1)}, u32[]{:S(2)}, u32[]{:S(2)}) collective-permute-start(bf16[64,128]{1,0:T(8,128)(2,1)S(1)} %bitcast.42), channel_id=1, source_target_pairs={{0,7},{1,6},{2,5},{3,4},{4,3},{5,2},{6,1},{7,0},{8,15},{9,14},{10,... | collective-permute-start | bytes 49160 | tf_op jit(solution)/shard_map/ppermute | solution.py:32
  363.7 16.6 %collective-permute-start.67 = (f32[4,1024]{1,0:T(4,128)S(1)}, f32[4,1024]{1,0:T(4,128)S(1)}, u32[]{:S(2)}, u32[]{:S(2)}) collective-permute-start(f32[4,1024]{1,0:T(4,128)S(1)} %shard_map.109), channel_id=1, source_target_pairs={{0,7},{1,6},{2,5},{3,4},{4,3},{5,2},{6,1},{7,0},{8,15},{9,14},{10,... | collective-permute-start | bytes 49160 | tf_op jit(solution)/shard_map/ppermute | solution.py:32
  363.8 20.0 %collective-permute-start.66 = (f32[4,1024]{1,0:T(4,128)S(1)}, f32[4,1024]{1,0:T(4,128)S(1)}, u32[]{:S(2)}, u32[]{:S(2)}) collective-permute-start(f32[4,1024]{1,0:T(4,128)S(1)} %shard_map.109), channel_id=1, source_target_pairs={{0,6},{1,7},{2,4},{3,5},{4,2},{5,3},{6,0},{7,1},{8,14},{9,15},{10,... | collective-permute-start | bytes 49160 | tf_op jit(solution)/shard_map/ppermute | solution.py:32
  376.3 7.7 %collective-permute-start.65 = (f32[4,1024]{1,0:T(4,128)S(1)}, f32[4,1024]{1,0:T(4,128)S(1)}, u32[]{:S(2)}, u32[]{:S(2)}) collective-permute-start(f32[4,1024]{1,0:T(4,128)S(1)} %shard_map.109), channel_id=1, source_target_pairs={{0,5},{1,4},{2,7},{3,6},{4,1},{5,0},{6,3},{7,2},{8,13},{9,12},{10,... | collective-permute-start | bytes 49160 | tf_op jit(solution)/shard_map/ppermute | solution.py:32
  378.2 8.3 %collective-permute-start.63 = (f32[4,1024]{1,0:T(4,128)S(1)}, f32[4,1024]{1,0:T(4,128)S(1)}, u32[]{:S(2)}, u32[]{:S(2)}) collective-permute-start(f32[4,1024]{1,0:T(4,128)S(1)} %shard_map.109), channel_id=1, source_target_pairs={{0,3},{1,2},{2,1},{3,0},{4,7},{5,6},{6,5},{7,4},{8,11},{9,10},{10,... | collective-permute-start | bytes 49160 | tf_op jit(solution)/shard_map/ppermute | solution.py:32
  380.3 7.2 %collective-permute-start.62 = (f32[4,1024]{1,0:T(4,128)S(1)}, f32[4,1024]{1,0:T(4,128)S(1)}, u32[]{:S(2)}, u32[]{:S(2)}) collective-permute-start(f32[4,1024]{1,0:T(4,128)S(1)} %shard_map.109), channel_id=1, source_target_pairs={{0,2},{1,3},{2,0},{3,1},{4,6},{5,7},{6,4},{7,5},{8,10},{9,11},{10,... | collective-permute-start | bytes 49160 | tf_op jit(solution)/shard_map/ppermute | solution.py:32
  444.0 47.5 %collective-permute-start.71 = (bf16[64,512]{1,0:T(8,128)(2,1)S(1)}, bf16[64,512]{1,0:T(8,128)(2,1)S(1)}, u32[]{:S(2)}, u32[]{:S(2)}) collective-permute-start(bf16[64,512]{1,0:T(8,128)(2,1)S(1)} %get-tuple-element.23), channel_id=1, source_target_pairs={{0,32},{32,0},{64,96},{96,64},{128,160},{160,128},{192,224},{224,1... | collective-permute-start | bytes 196616 | tf_op jit(solution)/shard_map/ppermute | solution.py:431
  476.5 15.4 %collective-permute-start.72 = (bf16[64,512]{1,0:T(8,128)(2,1)S(1)}, bf16[64,512]{1,0:T(8,128)(2,1)S(1)}, u32[]{:S(2)}, u32[]{:S(2)}) collective-permute-start(bf16[64,512]{1,0:T(8,128)(2,1)S(1)} %get-tuple-element.24), channel_id=1, source_target_pairs={{0,64},{32,96},{64,0},{96,32},{128,192},{160,224},{192,128},{224,1... | collective-permute-start | bytes 196616 | tf_op jit(solution)/shard_map/ppermute | solution.py:431
  498.9 7.2 %collective-permute-start.90 = (bf16[64,512]{1,0:T(8,128)(2,1)S(1)}, bf16[64,512]{1,0:T(8,128)(2,1)S(1)}, u32[]{:S(2)}, u32[]{:S(2)}) collective-permute-start(bf16[64,512]{1,0:T(8,128)(2,1)S(1)} %get-tuple-element.32.refs_0_), channel_id=1, source_target_pairs={{0,192},{32,224},{64,128},{96,160},{128,64},{160,96},{192,0},{224,... | collective-permute-start | bytes 196616 | tf_op jit(solution)/shard_map/ppermute | solution.py:32
  (75 other events, 725.9 us)

commit v2 on v1

--- a/solution.py
+++ b/solution.py
@@ -28,19 +28,16 @@
     return top + jnp.log(tree_sum([jnp.exp(p - top) for p in parts]))
 
 
-def xor_exchange(x, axis, size, steps):
-    return [x] + [lax.ppermute(x, axis, [(i, i ^ k) for i in range(size)]) for k in steps]
-
-
 class Slots:
-    def __init__(self, scale, row, col, count, rb, cb, total):
-        src, tgt = lax.axis_index("src"), lax.axis_index("tgt")
+    def __init__(self, ints, floats, total):
         self.total = total
-        self.scale = [scale[0, s] for s in range(total)]
-        self.row = [row[0, s] - src * rb for s in range(total)]
-        self.col = [col[0, s] - tgt * cb for s in range(total)]
-        self.live = [s < count[0, 0] for s in range(total)]
-        self.src, self.tgt = src, tgt
+        self.row = [ints[0, s] for s in range(total)]
+        self.col = [ints[0, total + s] for s in range(total)]
+        self.count = ints[0, 2 * total]
+        self.live = [s < self.count for s in range(total)]
+        self.scale = [floats[0, s] for s in range(total)]
+        self.shift, self.high = floats[0, total], floats[0, total + 1]
+        self.src, self.tgt = lax.axis_index("src"), lax.axis_index("tgt")
 
 
 def split_rows(x):
@@ -123,13 +120,28 @@
     return jnp.where(total > 0, jnp.log(jnp.maximum(total, 1e-38)) - shift / EPS, NEG)
 
 
+def send_copies(l_ref, copies_ref):
+    for k in range(copies_ref.shape[0]):
+        copies_ref[k] = l_ref[...]
+
+
 def sums_fine(low, high, others):
     return (low >= 2.0**-80 * jnp.maximum(others, 1.0)) & (high <= 2.0**100)
 
 
-def build_kernel(dims, scale, row, col, count, cost_hbm, k_ref, l_ref, ref_ref, cost_v, sums, zero, other8, out8, sems):
-    slots = Slots(scale, row, col, count, *dims)
-    total = slots.total
+def build_kernel(
+    dims, scale, row, col, count, log_a, log_b, cost_hbm,
+    k_ref, copies_ref, ints, floats, a_ref, b_ref,
+    l_ref, cost_v, sums, zero, other8, out8, stat, sems,
+):
+    rb, cb, total = dims
+    src, tgt = lax.axis_index("src"), lax.axis_index("tgt")
+    for s in range(total):
+        ints[0, s] = row[0, s] - src * rb
+        ints[0, total + s] = col[0, s] - tgt * cb
+        floats[0, s] = scale[0, s]
+    ints[0, 2 * total] = count[0, 0]
+    slots = Slots(ints, floats, total)
     half = cost_v.shape[1] // 2
     copies = [
         [
@@ -147,14 +159,19 @@
             for h in range(2):
                 copies[s][h].start()
 
+    tile = cost_v.shape[2]
+    for r in range(rb):
+        a_ref[r : r + 1, :] = log_a[r * tile : (r + 1) * tile].reshape(1, tile)
+    for c in range(cb):
+        b_ref[c : c + 1, :] = log_b[c * tile : (c + 1) * tile].reshape(1, tile)
     chunk = 32
     ones = jnp.ones((16, cost_v.shape[2]), BF16)
 
     def build(shift, wait):
         sums[...] = jnp.zeros(sums.shape, F32)
-        ref_ref[0, 0] = shift
-        ref_ref[0, 1] = 0.0
-        ref_ref[0, 2] = jnp.float32(jnp.inf)
+        floats[0, total] = shift
+        stat[1] = jnp.float32(0.0)
+        stat[2] = jnp.float32(jnp.inf)
         for s in range(total):
 
             @pl.when(slots.live[s])
@@ -173,17 +190,18 @@
                 part = k_row(ones, k_ref[s])[0:1]
                 at = pl.ds(slots.row[s], 1)
                 sums[at, :] = sums[at, :] + part
-                ref_ref[0, 1] = jnp.maximum(ref_ref[0, 1], jnp.max(part))
-                ref_ref[0, 2] = jnp.minimum(ref_ref[0, 2], jnp.min(part))
+                stat[1] = jnp.maximum(stat[1], jnp.max(part))
+                stat[2] = jnp.minimum(stat[2], jnp.min(part))
 
         l_ref[...] = to_log(sums[...], shift)
-        return sums_fine(ref_ref[0, 2], ref_ref[0, 1], ref_ref[0, 1])
+        floats[0, total + 1] = stat[1]
+        return sums_fine(stat[2], stat[1], stat[1])
 
     fine = build(jnp.float32(0.0), True)
 
     @pl.when(jnp.logical_not(fine))
     def _():
-        ref_ref[0, 3] = jnp.float32(jnp.inf)
+        stat[0] = jnp.float32(jnp.inf)
         for s in range(total):
 
             @pl.when(slots.live[s])
@@ -193,24 +211,26 @@
                     return jnp.minimum(low, jnp.min(cost_v[s, here, :].astype(F32)))
 
                 low = lax.fori_loop(0, 2 * half // chunk, lowest, jnp.float32(jnp.inf))
-                ref_ref[0, 3] = jnp.minimum(ref_ref[0, 3], low * slots.scale[s])
-
-        shifted = build(ref_ref[0, 3], False)
+                stat[0] = jnp.minimum(stat[0], low * slots.scale[s])
+
+        shifted = build(stat[0], False)
 
         @pl.when(jnp.logical_not(shifted))
         def _():
             zero[...] = jnp.zeros(zero.shape, F32)
             slow_lse(slots, cost_hbm, cost_v.at[0], sems.at[0, 0], other8, out8, zero, l_ref, True)
 
-
-def row_kernel(dims, n_parts, scale, row, col, count, ref, log_b, cost_hbm, k_ref, *rest):
-    parts, (l_ref, g, sums, stat, cost_v, other8, out8, sem) = rest[:n_parts], rest[n_parts:]
-    slots = Slots(scale, row, col, count, *dims)
+    send_copies(l_ref, copies_ref)
+
+
+def row_kernel(total, n_parts, ints, floats, log_b, cost_hbm, k_ref, _, *rest):
+    parts, (copies_ref, _, l_ref, g, sums, stat, cost_v, other8, out8, sem) = rest[:n_parts], rest[n_parts:]
+    slots = Slots(ints, floats, total)
     g[...] = EPS * log_b[...] - EPS * lse([p[...] for p in parts])
     sums[...] = jnp.zeros(sums.shape, F32)
     stat[0] = jnp.float32(0.0)
     stat[1] = jnp.float32(jnp.inf)
-    stat[2] = ref[0, 1]
+    stat[2] = slots.high
     for s in range(slots.total):
 
         @pl.when(slots.live[s])
@@ -223,21 +243,23 @@
             stat[1] = jnp.minimum(stat[1], jnp.min(part))
             stat[2] = jnp.maximum(stat[2], jnp.max(v))
 
-    l_ref[...] = to_log(sums[...], ref[0, 0])
+    l_ref[...] = to_log(sums[...], slots.shift)
 
     @pl.when(jnp.logical_not(sums_fine(stat[1], stat[0], stat[2])))
     def _():
         slow_lse(slots, cost_hbm, cost_v, sem, other8, out8, g, l_ref, True)
 
-
-def col_kernel(dims, n_parts, scale, row, col, count, ref, log_a, cost_hbm, k_ref, *rest):
-    parts, (l_ref, f, sums, stat, cost_v, other8, out8, sem) = rest[:n_parts], rest[n_parts:]
-    slots = Slots(scale, row, col, count, *dims)
-    f[...] = EPS * log_a[...] - EPS * lse([p[...] for p in parts])
+    send_copies(l_ref, copies_ref)
+
+
+def col_kernel(total, ints, floats, log_a, cost_hbm, k_ref, _, parts, *rest):
+    l_ref, _, f, sums, stat, cost_v, other8, out8, sem = rest
+    slots = Slots(ints, floats, total)
+    f[...] = EPS * log_a[...] - EPS * lse([parts[k] for k in range(parts.shape[0])])
     sums[...] = jnp.zeros(sums.shape, F32)
     stat[0] = jnp.float32(0.0)
     stat[1] = jnp.float32(jnp.inf)
-    stat[2] = ref[0, 1]
+    stat[2] = slots.high
     for s in range(slots.total):
 
         @pl.when(slots.live[s])
@@ -250,25 +272,23 @@
             stat[1] = jnp.minimum(stat[1], jnp.min(part))
             stat[2] = jnp.maximum(stat[2], jnp.max(u))
 
-    l_ref[...] = to_log(sums[...], ref[0, 0])
+    l_ref[...] = to_log(sums[...], slots.shift)
 
     @pl.when(jnp.logical_not(sums_fine(stat[1], stat[0], stat[2])))
     def _():
         slow_lse(slots, cost_hbm, cost_v, sem, other8, out8, f, l_ref, False)
 
 
-def label_kernel(dims, n_parts, n_out, scale, row, col, count, ref, log_a, cost_hbm, k_ref, labels, *rest):
-    parts, rest = rest[:n_parts], rest[n_parts:]
-    l_ref, f_out, outs, rest = rest[0], rest[1], rest[2 : 2 + n_out], rest[2 + n_out :]
-    acc, sums, stat, cost_v, other8, out8, sem = rest
-    slots = Slots(scale, row, col, count, *dims)
+def label_kernel(total, ints, floats, log_a, cost_hbm, k_ref, labels, parts, *rest):
+    f_out, keep, send, acc, l_ref, sums, stat, cost_v, other8, out8, sem = rest
+    slots = Slots(ints, floats, total)
     classes = acc.shape[1]
-    f_out[...] = EPS * log_a[...] - EPS * lse([p[...] for p in parts])
+    f_out[...] = EPS * log_a[...] - EPS * lse([parts[k] for k in range(parts.shape[0])])
     sums[...] = jnp.zeros(sums.shape, F32)
     acc[...] = jnp.zeros(acc.shape, F32)
     stat[0] = jnp.float32(0.0)
     stat[1] = jnp.float32(jnp.inf)
-    stat[2] = ref[0, 1]
+    stat[2] = slots.high
     my_outer, my_inner = slots.tgt // INNER, slots.tgt % INNER
     for s in range(slots.total):
 
@@ -289,7 +309,7 @@
             stat[1] = jnp.minimum(stat[1], jnp.min(part))
             stat[2] = jnp.maximum(stat[2], jnp.max(u))
 
-    l_ref[...] = to_log(sums[...], ref[0, 0])
+    l_ref[...] = to_log(sums[...], slots.shift)
 
     @pl.when(jnp.logical_not(sums_fine(stat[1], stat[0], stat[2])))
     def _():
@@ -317,33 +337,65 @@
                     term = jnp.dot(lab, p, preferred_element_type=F32)
                     acc[slots.col[s], :, here] = acc[slots.col[s], :, here] + term
 
-    width = outs[0].shape[1]
-    per = acc.shape[2] // width
-    for k in range(n_out):
-        piece = slots.src ^ k
-        here = pl.ds(pl.multiple_of((piece % per) * width, width), width)
-        total = piece_of(sums, piece, width)
+    core = slots.src % 2
+    width = keep.shape[2]
+    for c in range(acc.shape[0]):
+        total = sums[c : c + 1, :]
         inv = jnp.where(total > 0, 1.0 / jnp.maximum(total, 1e-38), 0.0)
-        outs[k][...] = (acc[piece // per, :, here] * inv).astype(BF16)
-
-
-def combine_kernel(n_src, log_b, *rest):
-    means, parts, (g_out, out) = rest[:n_src], rest[n_src : 2 * n_src], rest[2 * n_src :]
+        for half in range(2):
+            here = slice(half * width, (half + 1) * width)
+            mean = acc[c, :, here] * inv[:, here]
+            tail = jnp.broadcast_to(l_ref[c : c + 1, here], (8, width))
+
+            @pl.when(core == half)
+            def _():
+                keep[c, :classes] = mean
+                keep[c, classes:] = tail
+
+            @pl.when(core != half)
+            def _():
+                send[c, :classes] = mean
+                send[c, classes:] = tail
+
+
+def merge_kernel(keep, got, *outs):
     src = lax.axis_index("src")
-    total = lse([p[...] for p in parts])
-    g_out[...] = EPS * log_b[...] - EPS * total
-    width = out.shape[1]
-    ls = [piece_of(p, src, width) for p in parts]
-    top = lse(ls) - piece_of(log_b, src, width)
-    out[...] = tree_sum([means[k][...].astype(F32) * jnp.exp(ls[k] - top) for k in range(n_src)]).astype(BF16)
-
-
-def assemble_kernel(n_src, *refs):
-    pieces, out = refs[:n_src], refs[n_src]
+    classes = keep.shape[1] - 8
+    for q, out in enumerate(outs):
+        block = (src // 2) ^ q
+        mine, other = keep[block], got[block]
+        first, second = mine[classes : classes + 1], other[classes : classes + 1]
+        both = lse([first, second])
+        mean = mine[:classes] * jnp.exp(first - both) + other[:classes] * jnp.exp(second - both)
+        out[:classes] = mean.astype(BF16)
+        out[classes:] = split_rows(both)
+
+
+def tail_row(piece):
+    return jnp.sum(piece[piece.shape[0] - 16 :].astype(F32), axis=0, keepdims=True)
+
+
+def combine_kernel(log_b, *rest):
+    pieces, out = rest[:-1], rest[-1]
     src = lax.axis_index("src")
-    width = pieces[0].shape[1]
-    for k in range(n_src):
-        out[:, pl.ds(pl.multiple_of((src ^ k) * width, width), width)] = pieces[k][...]
+    classes, width = out.shape[0] - 16, out.shape[1]
+    ls = [tail_row(p[...]) for p in pieces]
+    total = lse(ls)
+    mass = piece_of(log_b, src, width)
+    top = total - mass
+    out[:classes] = tree_sum([p[:classes].astype(F32) * jnp.exp(l - top) for p, l in zip(pieces, ls)]).astype(BF16)
+    out[classes:] = split_rows(EPS * mass - EPS * total)
+
+
+def assemble_kernel(order, *refs):
+    pieces, (g_out, out, row) = refs[: len(order)], refs[len(order) :]
+    src = lax.axis_index("src")
+    classes, width = out.shape[0], pieces[0].shape[1]
+    for k, piece in zip(order, pieces):
+        here = pl.ds(pl.multiple_of((src ^ k) * width, width), width)
+        out[:, here] = piece[:classes]
+        row[:, here] = tail_row(piece[...])
+    g_out[...] = row[...].reshape(g_out.shape)
 
 
 VM = pl.BlockSpec(memory_space=pltpu.VMEM)
@@ -358,93 +410,143 @@
     rb, cb = log_a.shape[0] // tile, log_b.shape[0] // tile
     classes = labels.shape[1]
     dims = (rb, cb, slots)
-    scalars = (cost_scale, slot_block_row, slot_block_column, device_block_count)
-    log_a = log_a.reshape(rb, tile)
-    log_b = log_b.reshape(cb, tile)
+    in_hbm = functools.partial(pltpu.with_memory_space_constraint, memory_space=pltpu.HBM)
+    in_vmem = functools.partial(pltpu.with_memory_space_constraint, memory_space=pltpu.VMEM)
+    in_smem = functools.partial(pltpu.with_memory_space_constraint, memory_space=pltpu.SMEM)
+
+    def xor(x, axis, k):
+        return lax.ppermute(x, axis, [(i, i ^ k) for i in range(lax.axis_size(axis))])
+
+    def doubled(part, axis):
+        k = 1
+        while 2 * k < lax.axis_size(axis):
+            part = lse([part, xor(part, axis, k)])
+            k *= 2
+        return [part, xor(part, axis, k)]
+
     outer = n_tgt // INNER
-
-    lab = jnp.stack(xor_exchange(labels.T, "tgt", n_tgt, range(1, INNER)))
-    lab = jnp.stack(xor_exchange(lab, "tgt", n_tgt, [k * INNER for k in range(1, outer)]))
-
-    k_type = pltpu.VMEM((slots, tile, tile), BF16)
+    along_z = [[x * INNER + z for z in range(INNER)] for x in range(outer)]
+    along_x = [[x * INNER + z for x in range(outer)] for z in range(INNER)]
+
+    def over_tgt(copies):
+        parts = lax.all_to_all(copies, "tgt", 0, 0, axis_index_groups=along_z, tiled=True)
+        part = lse([parts[z] for z in range(INNER)])
+        copies = jnp.broadcast_to(part[None], (outer,) + part.shape)
+        return lax.all_to_all(copies, "tgt", 0, 0, axis_index_groups=along_x, tiled=True)
+
+    def grow(lab):
+        return jnp.concatenate([lab, xor(lab, "tgt", lab.shape[0])])
+
+    cost = in_hbm(cost)
     vec = functools.partial(jax.ShapeDtypeStruct, dtype=F32)
     chunks = pltpu.VMEM((tile // 128, 128), F32)
-    slow = [pltpu.VMEM((tile, tile), BF16), chunks, chunks, pltpu.SemaphoreType.DMA]
-    work = [pltpu.SMEM((3,), F32)] + slow
-
-    k_all, row_l, ref = pl.pallas_call(
+    work = [pltpu.SMEM((3,), F32), pltpu.VMEM((tile, tile), BF16), chunks, chunks, pltpu.SemaphoreType.DMA]
+    rows, cols = pltpu.VMEM((rb, tile), F32), pltpu.VMEM((cb, tile), F32)
+
+    k_all, row_l, ints, floats, log_a, log_b = pl.pallas_call(
         functools.partial(build_kernel, dims),
-        out_shape=(k_type, vec((rb, tile)), vec((1, 4))),
-        in_specs=[SM] * 4 + [HB],
-        out_specs=(VM, VM, SM),
-        scratch_shapes=[
+        out_shape=(
             pltpu.VMEM((slots, tile, tile), BF16),
+            vec((INNER, rb, tile)),
+            pltpu.SMEM((1, 2 * slots + 1), jnp.int32),
+            pltpu.SMEM((1, slots + 2), F32),
             pltpu.VMEM((rb, tile), F32),
             pltpu.VMEM((cb, tile), F32),
+        ),
+        in_specs=[SM] * 4 + [VM] * 2 + [HB],
+        out_specs=(VM, VM, SM, SM, VM, VM),
+        scratch_shapes=[
+            rows,
+            pltpu.VMEM((slots, tile, tile), BF16),
+            rows,
+            cols,
             chunks,
             chunks,
+            pltpu.SMEM((3,), F32),
             pltpu.SemaphoreType.DMA((slots, 2)),
         ],
         compiler_params=PARAMS,
-    )(*scalars, cost)
-    k_all = pltpu.with_memory_space_constraint(k_all, pltpu.VMEM)
-    common = [SM] * 5 + [VM, HB, VM]
-
-    def row_exchange(part):
-        part = lse(xor_exchange(part, "tgt", n_tgt, range(1, INNER)))
-        return xor_exchange(part, "tgt", n_tgt, [k * INNER for k in range(1, outer)])
-
+    )(
+        in_hbm(cost_scale),
+        in_hbm(slot_block_row),
+        in_hbm(slot_block_column),
+        device_block_count,
+        in_hbm(log_a),
+        in_hbm(log_b),
+        cost,
+    )
+    k_all, log_a, log_b = in_vmem(k_all), in_vmem(log_a), in_vmem(log_b)
+    scalars = (in_smem(ints), in_smem(floats))
+    common = [SM] * 2 + [VM, HB, VM]
+
+    lab = labels.T[None]
+    any_spec = pl.BlockSpec(memory_space=pl.ANY)
     for step in range(ITERS):
-        row_parts = row_exchange(row_l)
+        row_parts = over_tgt(row_l)
         if step == ITERS - 1:
             break
-        col_l = pl.pallas_call(
-            functools.partial(col_kernel, dims, outer),
-            out_shape=vec((cb, tile)),
-            in_specs=common + [VM] * outer,
-            out_specs=VM,
-            scratch_shapes=[pltpu.VMEM((rb, tile), F32), pltpu.VMEM((cb, tile), F32)] + work,
+        col_l, lab = pl.pallas_call(
+            functools.partial(col_kernel, slots),
+            out_shape=(vec((cb, tile)), jax.ShapeDtypeStruct(lab.shape, BF16)),
+            in_specs=common + [any_spec, VM],
+            out_specs=(VM, any_spec),
+            scratch_shapes=[rows, cols] + work,
+            input_output_aliases={5: 1},
             compiler_params=PARAMS,
-        )(*scalars, ref, log_a, cost, k_all, *row_parts)
-        col_parts = xor_exchange(col_l, "src", n_src, range(1, n_src))
-        row_l = pl.pallas_call(
-            functools.partial(row_kernel, dims, n_src),
-            out_shape=vec((rb, tile)),
-            in_specs=common + [VM] * n_src,
-            out_specs=VM,
-            scratch_shapes=[pltpu.VMEM((cb, tile), F32), pltpu.VMEM((rb, tile), F32)] + work,
+        )(*scalars, log_a, cost, k_all, lab, row_parts)
+        for _ in range(2 if step < ITERS - 2 else 1):
+            lab = grow(lab)
+        col_parts = doubled(col_l, "src")
+        row_l, lab = pl.pallas_call(
+            functools.partial(row_kernel, slots, 2),
+            out_shape=(vec((INNER, rb, tile)), jax.ShapeDtypeStruct(lab.shape, BF16)),
+            in_specs=common + [any_spec] + [VM] * 2,
+            out_specs=(VM, any_spec),
+            scratch_shapes=[rows, cols, rows] + work,
+            input_output_aliases={5: 1},
             compiler_params=PARAMS,
-        )(*scalars, ref, log_b, cost, k_all, *col_parts)
+        )(*scalars, log_b, cost, k_all, lab, *col_parts)
+    lab = lab.reshape(outer, INNER, classes, -1)
 
     width = cb * tile // n_src
-    piece = jax.ShapeDtypeStruct((classes, width), BF16)
-    col_l, f_pot, *means = pl.pallas_call(
-        functools.partial(label_kernel, dims, outer, n_src),
-        out_shape=(vec((cb, tile)), vec((rb, tile))) + (piece,) * n_src,
-        in_specs=common + [VM] + [VM] * outer,
-        out_specs=(VM,) * (2 + n_src),
-        scratch_shapes=[pltpu.VMEM((cb, classes, tile), F32), pltpu.VMEM((cb, tile), F32)] + work,
+    half = vec((cb, classes + 8, width))
+    piece = jax.ShapeDtypeStruct((classes + 16, width), BF16)
+    f_pot, keep, send = pl.pallas_call(
+        functools.partial(label_kernel, slots),
+        out_shape=(vec((rb, tile)), half, half),
+        in_specs=common + [VM] + [VM],
+        out_specs=(VM,) * 3,
+        scratch_shapes=[pltpu.VMEM((cb, classes, tile), F32), cols, cols] + work,
         compiler_params=PARAMS,
-    )(*scalars, ref, log_a, cost, k_all, lab, *row_parts)
-    col_parts = xor_exchange(col_l, "src", n_src, range(1, n_src))
-    means = [means[0]] + [
-        lax.ppermute(means[k], "src", [(i, i ^ k) for i in range(n_src)]) for k in range(1, n_src)
-    ]
-    g_pot, out = pl.pallas_call(
-        functools.partial(combine_kernel, n_src),
-        out_shape=(vec((cb, tile)), piece),
-        in_specs=[VM] * (1 + 2 * n_src),
-        out_specs=(VM, VM),
+    )(*scalars, log_a, cost, k_all, lab, row_parts)
+    n_y = n_src // 2
+    pieces = pl.pallas_call(
+        merge_kernel,
+        out_shape=(piece,) * n_y,
+        in_specs=[VM] * 2,
+        out_specs=(VM,) * n_y,
         compiler_params=PARAMS,
-    )(log_b, *means, *col_parts)
-    out = pl.pallas_call(
-        functools.partial(assemble_kernel, n_src),
-        out_shape=jax.ShapeDtypeStruct((classes, cb * tile), BF16),
-        in_specs=[VM] * n_src,
+    )(keep, xor(send, "src", 1))
+    pieces = [pieces[0]] + [xor(pieces[q], "src", 2 * q) for q in range(1, n_y)]
+    done = pl.pallas_call(
+        combine_kernel,
+        out_shape=piece,
+        in_specs=[VM] * (1 + n_y),
         out_specs=VM,
         compiler_params=PARAMS,
-    )(*xor_exchange(out, "src", n_src, range(1, n_src)))
-    return f_pot.reshape(-1), g_pot.reshape(-1), out.T
+    )(log_b, *pieces)
+    pieces = [done] + [xor(done, "src", 2 * q) for q in range(1, n_y)]
+    pieces = pieces + [xor(p, "src", 1) for p in pieces]
+    order = tuple(2 * q for q in range(n_y)) + tuple(2 * q + 1 for q in range(n_y))
+    g_pot, out = pl.pallas_call(
+        functools.partial(assemble_kernel, order),
+        out_shape=(vec((cb * tile,)), jax.ShapeDtypeStruct((classes, cb * tile), BF16)),
+        in_specs=[VM] * n_src,
+        out_specs=(VM, VM),
+        scratch_shapes=[pltpu.VMEM((1, cb * tile), F32)],
+        compiler_params=PARAMS,
+    )(*pieces)
+    return f_pot.reshape(-1), g_pot, out.T
 
 
 def solution(mesh):

time: 520 us -> 501 us (0.963); the launches traced: 511 us -> 500 us
  blocking collectives: 0 us -> 231 us
  Pallas kernels: 214 us -> 75.9 us
  starting transfers between devices: 249 us -> 162 us
  local copies, waits for them, and re-layouts: 19.2 us -> 1.37 us
    all_to_all x0 -> x8, blocking collectives: none -> 231 us  [the longest x4 201 us: over_tgt(): lax.all_to_all(copies, 'tgt', 0, 0, axis_index_groups=along_z, tiled=True)]
    pallas_call x10 -> x11, Pallas kernels: 214 us -> 75.9 us  [the longest x3 34.6 us: local(): pl.pallas_call(functools.partial(col_kernel, slots), out_shape=(vec((cb,...]
    ppermute x92 -> x25, starting transfers between devices: 249 us -> 162 us  [xor(): lax.ppermute(x, axis, [(i, i ^ k) for i in range(lax.axis_size(axis))])]
    unnamed x37 -> x2, local copies, waits for them, and re-layouts: 18.5 us -> 1.33 us
    ppermute x92 -> x25, waiting for transfers between devices: 26.3 us -> 28.2 us  [xor(): lax.ppermute(x, axis, [(i, i ^ k) for i in range(lax.axis_size(axis))])]
  transfers between devices with their start and end apart: 92 -> 25, of which waited for: 32 -> 17; matrix products, arithmetic and copies ran while one was open for 0% -> 0% of each run, Pallas kernels for 12% -> 0%
where the time goes in v2:
time: 501 us; the launch traced here: 500 us
  blocking collectives  231 us (46%)
  starting transfers between devices  162 us (32%)
  Pallas kernels  75.9 us (15%)
  waiting for transfers between devices  28.2 us (6%)
    all_to_all x4, blocking collectives, over_tgt(): lax.all_to_all(copies, 'tgt', 0, 0, axis_index_groups=along_z, tiled=True)  201 us
    ppermute x25, starting transfers between devices, xor(): lax.ppermute(x, axis, [(i, i ^ k) for i in range(lax.axis_size(axis))])  162 us
    pallas_call x3, Pallas kernels, local(): pl.pallas_call(functools.partial(col_kernel, slots), out_shape=(vec((cb,...  34.6 us
    all_to_all x4, blocking collectives, over_tgt(): lax.all_to_all(copies, 'tgt', 0, 0, axis_index_groups=along_x, tiled=True)  29.6 us
    ppermute x25, waiting for transfers between devices, xor(): lax.ppermute(x, axis, [(i, i ^ k) for i in range(lax.axis_size(axis))])  28.2 us
    pallas_call x1, Pallas kernels, local(): pl.pallas_call(functools.partial(label_kernel, slots), out_shape=(vec((rb...  28.1 us
  transfers between devices with their start and end apart: 25, of which 17 were waited for; matrix products, arithmetic and copies ran while one was open for 0% of the time, Pallas kernels for 0%

profile of v2, /device:TPU:1, one launch (start us, length us, event | category | flops | bytes accessed | tf_op | source)
XLA Modules:
  0.0 500.2 jit_solution(17712873188193499546)
XLA Ops:
  2.0 9.6 %shard_map.103 = (bf16[3,1024,1024]{2,1,0:T(8,128)(2,1)S(1)}, f32[8,4,1024]{2,1,0:T(4,128)S(1)}, s32[1,7]{1,0:T(1,128)S(4)}, f32[1,5]{1,0:T(1,128)S(4)}, f32[4,1024]{1,0:T(4,128)S(1)}, /*index=5*/f32[4,1024]{1,0:T(4,128)S(1)}) custom-call(f32[1,3]{1,0:T(1,128)} %scale.1, s32[1,3]{1,0:T(1,128)} %row.1, s32[1,3]{1,0:T(1,128)} %col.1, s32[1,1]{1,0:T(1,128)S(6)} %copy.27.count, ...), custom_call_target="tpu_custom_call" | custom-call | tf_op jit(solution)/shard_map/pallas_call | solution.py:446
  11.6 64.9 %all_to_all.40 = f32[8,4,1024]{2,1,0:T(4,128)S(1)} all-to-all(f32[8,4,1024]{2,1,0:T(4,128)S(1)} %get-tuple-element.35), channel_id=1, replica_groups={{0,1,2,3,4,5,6,7},{8,9,10,11,12,13,14,15},{16,17,18,19,20,21,22,23},{24..., dimensions={0} | all-to-all | bytes 262144 | tf_op jit(solution)/shard_map/all_to_all | solution.py:432
  76.6 9.0 %all_to_all.47.parts = f32[4,4,1024]{2,1,0:T(4,128)S(1)} all-to-all(f32[4,4,1024]{2,1,0:T(4,128)S(1)} %broadcast_in_dim.37), channel_id=1, replica_groups={{0,8,16,24},{1,9,17,25},{2,10,18,26},{3,11,19,27},{4,12,20,28},{5,13,21..., dimensions={0} | all-to-all | bytes 131072 | tf_op jit(solution)/shard_map/all_to_all | solution.py:435
  85.6 11.5 %shard_map.104 = (f32[4,1024]{1,0:T(4,128)S(1)}, bf16[1,64,128]{2,1,0:T(8,128)(2,1)S(1)}) custom-call(s32[1,7]{1,0:T(1,128)S(4)} %get-tuple-element.30.ints, f32[1,5]{1,0:T(1,128)S(4)} %get-tuple-element.31.floats, f32[4,1024]{1,0:T(4,128)S(1)} %get-tuple-element.32.log_a, bf16[1,3,1024,1024]{3,2,1,0:T(8,128)(2,1)} %cost_hbm.15, ...), custom_call_target="tpu_custom_call", output_to_operand_aliasing={{1}: (5, {})} | custom-call | tf_op jit(solution)/shard_map/pallas_call | solution.py:488
  97.1 25.5 %collective-permute-start.2 = (f32[4,1024]{1,0:T(4,128)S(1)}, f32[4,1024]{1,0:T(4,128)S(1)}, u32[]{:S(2)}, u32[]{:S(2)}) collective-permute-start(f32[4,1024]{1,0:T(4,128)S(1)} %get-tuple-element.37), channel_id=1, source_target_pairs={{0,32},{32,0},{64,96},{96,64},{128,160},{160,128},{192,224},{224,1... | collective-permute-start | bytes 49160 | tf_op jit(solution)/shard_map/ppermute | solution.py:418
  123.5 1.9 collective-permute-start.3
  126.6 2.5 collective-permute-done.1
  129.2 1.6 collective-permute-done.4.rest_1_
  131.6 45.8 %all_to_all.41 = f32[8,4,1024]{2,1,0:T(4,128)S(1)} all-to-all(f32[8,4,1024]{2,1,0:T(4,128)S(1)} %get-tuple-element.39), channel_id=1, replica_groups={{0,1,2,3,4,5,6,7},{8,9,10,11,12,13,14,15},{16,17,18,19,20,21,22,23},{24..., dimensions={0} | all-to-all | bytes 262144 | tf_op jit(solution)/shard_map/all_to_all | solution.py:432
  177.4 6.8 %all_to_all.42.parts = f32[4,4,1024]{2,1,0:T(4,128)S(1)} all-to-all(f32[4,4,1024]{2,1,0:T(4,128)S(1)} %broadcast_in_dim.39), channel_id=1, replica_groups={{0,8,16,24},{1,9,17,25},{2,10,18,26},{3,11,19,27},{4,12,20,28},{5,13,21..., dimensions={0} | all-to-all | bytes 131072 | tf_op jit(solution)/shard_map/all_to_all | solution.py:435
  184.3 11.5 %shard_map.106 = (f32[4,1024]{1,0:T(4,128)S(1)}, bf16[4,64,128]{2,1,0:T(8,128)(2,1)S(1)}) custom-call(s32[1,7]{1,0:T(1,128)S(4)} %get-tuple-element.30.ints, f32[1,5]{1,0:T(1,128)S(4)} %get-tuple-element.31.floats, f32[4,1024]{1,0:T(4,128)S(1)} %get-tuple-element.32.log_a, bf16[1,3,1024,1024]{3,2,1,0:T(8,128)(2,1)} %cost_hbm.15, ...), custom_call_target="tpu_custom_call", output_to_operand_aliasing={{1}: (5, {})} | custom-call | tf_op jit(solution)/shard_map/pallas_call | solution.py:488
  195.8 27.6 %collective-permute-start.7 = (f32[4,1024]{1,0:T(4,128)S(1)}, f32[4,1024]{1,0:T(4,128)S(1)}, u32[]{:S(2)}, u32[]{:S(2)}) collective-permute-start(f32[4,1024]{1,0:T(4,128)S(1)} %get-tuple-element.41), channel_id=1, source_target_pairs={{0,32},{32,0},{64,96},{96,64},{128,160},{160,128},{192,224},{224,1... | collective-permute-start | bytes 49160 | tf_op jit(solution)/shard_map/ppermute | solution.py:418
  225.7 4.7 collective-permute-done.5
  230.7 3.7 collective-permute-done.6
  235.6 46.4 %all_to_all.43 = f32[8,4,1024]{2,1,0:T(4,128)S(1)} all-to-all(f32[8,4,1024]{2,1,0:T(4,128)S(1)} %get-tuple-element.43), channel_id=1, replica_groups={{0,1,2,3,4,5,6,7},{8,9,10,11,12,13,14,15},{16,17,18,19,20,21,22,23},{24..., dimensions={0} | all-to-all | bytes 262144 | tf_op jit(solution)/shard_map/all_to_all | solution.py:432
  282.1 6.8 %all_to_all.44.parts = f32[4,4,1024]{2,1,0:T(4,128)S(1)} all-to-all(f32[4,4,1024]{2,1,0:T(4,128)S(1)} %broadcast_in_dim.41), channel_id=1, replica_groups={{0,8,16,24},{1,9,17,25},{2,10,18,26},{3,11,19,27},{4,12,20,28},{5,13,21..., dimensions={0} | all-to-all | bytes 131072 | tf_op jit(solution)/shard_map/all_to_all | solution.py:435
  289.0 11.5 %shard_map.108 = (f32[4,1024]{1,0:T(4,128)S(1)}, bf16[16,64,128]{2,1,0:T(8,128)(2,1)S(1)}) custom-call(s32[1,7]{1,0:T(1,128)S(4)} %get-tuple-element.30.ints, f32[1,5]{1,0:T(1,128)S(4)} %get-tuple-element.31.floats, f32[4,1024]{1,0:T(4,128)S(1)} %get-tuple-element.32.log_a, bf16[1,3,1024,1024]{3,2,1,0:T(8,128)(2,1)} %cost_hbm.15, ...), custom_call_target="tpu_custom_call", output_to_operand_aliasing={{1}: (5, {})} | custom-call | tf_op jit(solution)/shard_map/pallas_call | solution.py:488
  300.5 28.5 %collective-permute-start.11 = (f32[4,1024]{1,0:T(4,128)S(1)}, f32[4,1024]{1,0:T(4,128)S(1)}, u32[]{:S(2)}, u32[]{:S(2)}) collective-permute-start(f32[4,1024]{1,0:T(4,128)S(1)} %get-tuple-element.45), channel_id=1, source_target_pairs={{0,32},{32,0},{64,96},{96,64},{128,160},{160,128},{192,224},{224,1... | collective-permute-start | bytes 49160 | tf_op jit(solution)/shard_map/ppermute | solution.py:418
  330.2 2.3 collective-permute-done.12
  332.6 2.3 collective-permute-start.13
  334.8 3.5 collective-permute-done.10
  339.3 44.3 %all_to_all.45 = f32[8,4,1024]{2,1,0:T(4,128)S(1)} all-to-all(f32[8,4,1024]{2,1,0:T(4,128)S(1)} %get-tuple-element.47), channel_id=1, replica_groups={{0,1,2,3,4,5,6,7},{8,9,10,11,12,13,14,15},{16,17,18,19,20,21,22,23},{24..., dimensions={0} | all-to-all | bytes 262144 | tf_op jit(solution)/shard_map/all_to_all | solution.py:432
  383.7 6.8 %all_to_all.46.parts = f32[4,4,1024]{2,1,0:T(4,128)S(1)} all-to-all(f32[4,4,1024]{2,1,0:T(4,128)S(1)} %broadcast_in_dim.43), channel_id=1, replica_groups={{0,8,16,24},{1,9,17,25},{2,10,18,26},{3,11,19,27},{4,12,20,28},{5,13,21..., dimensions={0} | all-to-all | bytes 131072 | tf_op jit(solution)/shard_map/all_to_all | solution.py:435
  390.5 28.1 %shard_map.110 = (f32[4,1024]{1,0:T(4,128)S(1)}, f32[4,72,512]{2,1,0:T(8,128)S(1)}, f32[4,72,512]{2,1,0:T(8,128)S(1)}) custom-call(s32[1,7]{1,0:T(1,128)S(4)} %get-tuple-element.30.ints, f32[1,5]{1,0:T(1,128)S(4)} %get-tuple-element.31.floats, f32[4,1024]{1,0:T(4,128)S(1)} %get-tuple-element.32.log_a, bf16[1,3,1024,1024]{3,2,1,0:T(8,128)(2,1)} %cost_hbm.15, ...), custom_call_target="tpu_custom_call" | custom-call | tf_op jit(solution)/shard_map/pallas_call | solution.py:514
  418.6 60.3 %collective-permute-start.14 = (f32[4,72,512]{2,1,0:T(8,128)S(1)}, f32[4,72,512]{2,1,0:T(8,128)S(1)}, u32[]{:S(2)}, u32[]{:S(2)}) collective-permute-start(f32[4,72,512]{2,1,0:T(8,128)S(1)} %get-tuple-element.50), channel_id=1, source_target_pairs={{0,32},{32,0},{64,96},{96,64},{128,160},{160,128},{192,224},{224,1... | collective-permute-start | bytes 1769480 | tf_op jit(solution)/shard_map/ppermute | solution.py:418
  479.0 1.6 collective-permute-done.14.got
  481.3 3.4 collective-permute-start.17
  486.1 2.6 collective-permute-done.17.rest_3_
  488.9 1.9 collective-permute-start.20
  492.2 1.5 collective-permute-start.21
  493.7 1.6 collective-permute-start.24
  495.6 2.4 collective-permute-start.23
  (58 shorter events, 16.1 us)
Async XLA Ops:
  97.1 26.4 %collective-permute-start.2 = (f32[4,1024]{1,0:T(4,128)S(1)}, f32[4,1024]{1,0:T(4,128)S(1)}, u32[]{:S(2)}, u32[]{:S(2)}) collective-permute-start(f32[4,1024]{1,0:T(4,128)S(1)} %get-tuple-element.37), channel_id=1, source_target_pairs={{0,32},{32,0},{64,96},{96,64},{128,160},{160,128},{192,224},{224,1... | collective-permute-start | bytes 49160 | tf_op jit(solution)/shard_map/ppermute | solution.py:418
  122.7 2.7 collective-permute-start
  123.5 3.0 collective-permute-start.3
  125.4 3.8 collective-permute-start.1
  126.5 4.2 collective-permute-start.4
  195.8 28.4 %collective-permute-start.7 = (f32[4,1024]{1,0:T(4,128)S(1)}, f32[4,1024]{1,0:T(4,128)S(1)}, u32[]{:S(2)}, u32[]{:S(2)}) collective-permute-start(f32[4,1024]{1,0:T(4,128)S(1)} %get-tuple-element.41), channel_id=1, source_target_pairs={{0,32},{32,0},{64,96},{96,64},{128,160},{160,128},{192,224},{224,1... | collective-permute-start | bytes 49160 | tf_op jit(solution)/shard_map/ppermute | solution.py:418
  223.4 7.0 %collective-permute-start.5 = (bf16[4,64,128]{2,1,0:T(8,128)(2,1)S(1)}, bf16[4,64,128]{2,1,0:T(8,128)(2,1)S(1)}, u32[]{:S(2)}, u32[]{:S(2)}) collective-permute-start(bf16[4,64,128]{2,1,0:T(8,128)(2,1)S(1)} %get-tuple-element.40), channel_id=1, source_target_pairs={{0,4},{1,5},{2,6},{3,7},{4,0},{5,1},{6,2},{7,3},{8,12},{9,13},{10,... | collective-permute-start | bytes 196616 | tf_op jit(solution)/shard_map/ppermute | solution.py:418
  224.3 6.3 %collective-permute-start.8 = (f32[4,1024]{1,0:T(4,128)S(1)}, f32[4,1024]{1,0:T(4,128)S(1)}, u32[]{:S(2)}, u32[]{:S(2)}) collective-permute-start(f32[4,1024]{1,0:T(4,128)S(1)} %log_add_fusion.3), channel_id=1, source_target_pairs={{0,64},{32,96},{64,0},{96,32},{128,192},{160,224},{192,128},{224,1... | collective-permute-start | bytes 49160 | tf_op jit(solution)/shard_map/ppermute | solution.py:418
  230.4 3.9 collective-permute-start.6
  230.6 4.2 collective-permute-start.9
  300.5 29.3 %collective-permute-start.11 = (f32[4,1024]{1,0:T(4,128)S(1)}, f32[4,1024]{1,0:T(4,128)S(1)}, u32[]{:S(2)}, u32[]{:S(2)}) collective-permute-start(f32[4,1024]{1,0:T(4,128)S(1)} %get-tuple-element.45), channel_id=1, source_target_pairs={{0,32},{32,0},{64,96},{96,64},{128,160},{160,128},{192,224},{224,1... | collective-permute-start | bytes 49160 | tf_op jit(solution)/shard_map/ppermute | solution.py:418
  329.0 9.4 %collective-permute-start.10 = (bf16[16,64,128]{2,1,0:T(8,128)(2,1)S(1)}, bf16[16,64,128]{2,1,0:T(8,128)(2,1)S(1)}, u32[]{:S(2)}, u32[]{:S(2)}) collective-permute-start(bf16[16,64,128]{2,1,0:T(8,128)(2,1)S(1)} %get-tuple-element.44), channel_id=1, source_target_pairs={{0,16},{1,17},{2,18},{3,19},{4,20},{5,21},{6,22},{7,23},{8,24},{9,... | collective-permute-start | bytes 786440 | tf_op jit(solution)/shard_map/ppermute | solution.py:418
  329.8 2.7 collective-permute-start.12
  332.6 5.8 %collective-permute-start.13 = (f32[4,1024]{1,0:T(4,128)S(1)}, f32[4,1024]{1,0:T(4,128)S(1)}, u32[]{:S(2)}, u32[]{:S(2)}) collective-permute-start(f32[4,1024]{1,0:T(4,128)S(1)} %log_add_fusion.rest_0_), channel_id=1, source_target_pairs={{0,128},{32,160},{64,192},{96,224},{128,0},{160,32},{192,64},{224,... | collective-permute-start | bytes 49160 | tf_op jit(solution)/shard_map/ppermute | solution.py:418
  418.6 62.0 %collective-permute-start.14 = (f32[4,72,512]{2,1,0:T(8,128)S(1)}, f32[4,72,512]{2,1,0:T(8,128)S(1)}, u32[]{:S(2)}, u32[]{:S(2)}) collective-permute-start(f32[4,72,512]{2,1,0:T(8,128)S(1)} %get-tuple-element.50), channel_id=1, source_target_pairs={{0,32},{32,0},{64,96},{96,64},{128,160},{160,128},{192,224},{224,1... | collective-permute-start | bytes 1769480 | tf_op jit(solution)/shard_map/ppermute | solution.py:418
  480.7 3.9 collective-permute-start.15
  481.3 4.8 collective-permute-start.16
  481.3 7.4 %collective-permute-start.17 = (bf16[80,512]{1,0:T(8,128)(2,1)S(1)}, bf16[80,512]{1,0:T(8,128)(2,1)S(1)}, u32[]{:S(2)}, u32[]{:S(2)}) collective-permute-start(bf16[80,512]{1,0:T(8,128)(2,1)S(1)} %get-tuple-element.54), channel_id=1, source_target_pairs={{0,192},{32,224},{64,128},{96,160},{128,64},{160,96},{192,0},{224,... | collective-permute-start | bytes 245768 | tf_op jit(solution)/shard_map/ppermute | solution.py:418
  488.9 4.9 collective-permute-start.20
  490.8 4.8 collective-permute-start.19
  490.8 7.2 %collective-permute-start.18 = (bf16[80,512]{1,0:T(8,128)(2,1)S(1)}, bf16[80,512]{1,0:T(8,128)(2,1)S(1)}, u32[]{:S(2)}, u32[]{:S(2)}) collective-permute-start(bf16[80,512]{1,0:T(8,128)(2,1)S(1)} %shard_map.112.refs_0_), channel_id=1, source_target_pairs={{0,64},{32,96},{64,0},{96,32},{128,192},{160,224},{192,128},{224,1... | collective-permute-start | bytes 245768 | tf_op jit(solution)/shard_map/ppermute | solution.py:418
  492.2 6.4 %collective-permute-start.21 = (bf16[80,512]{1,0:T(8,128)(2,1)S(1)}, bf16[80,512]{1,0:T(8,128)(2,1)S(1)}, u32[]{:S(2)}, u32[]{:S(2)}) collective-permute-start(bf16[80,512]{1,0:T(8,128)(2,1)S(1)} %shard_map.112.refs_0_), channel_id=1, source_target_pairs={{0,32},{32,0},{64,96},{96,64},{128,160},{160,128},{192,224},{224,1... | collective-permute-start | bytes 245768 | tf_op jit(solution)/shard_map/ppermute | solution.py:418
  493.7 4.9 collective-permute-start.24
  495.6 3.4 collective-permute-start.23
  498.0 1.3 collective-permute-start.22

commit v3 on v2

--- a/solution.py
+++ b/solution.py
@@ -12,7 +12,6 @@
 NEG = -1e30
 LOG2E = 1.4426950408889634
 TO2 = LOG2E / EPS
-INNER = 8
 LIMIT = 40 * 1024 * 1024
 F32, BF16 = jnp.float32, jnp.bfloat16
 
@@ -131,8 +130,8 @@
 
 def build_kernel(
     dims, scale, row, col, count, log_a, log_b, cost_hbm,
-    k_ref, copies_ref, ints, floats, a_ref, b_ref,
-    l_ref, cost_v, sums, zero, other8, out8, stat, sems,
+    k_hbm, copies_ref, ints, floats, a_ref, b_ref,
+    l_ref, k_ref, cost_v, sums, zero, other8, out8, stat, sems, k_sems,
 ):
     rb, cb, total = dims
     src, tgt = lax.axis_index("src"), lax.axis_index("tgt")
@@ -159,6 +158,7 @@
             for h in range(2):
                 copies[s][h].start()
 
+    k_copies = [pltpu.make_async_copy(k_ref.at[s], k_hbm.at[s], k_sems.at[s]) for s in range(total)]
     tile = cost_v.shape[2]
     for r in range(rb):
         a_ref[r : r + 1, :] = log_a[r * tile : (r + 1) * tile].reshape(1, tile)
@@ -187,12 +187,19 @@
                         x = x * (-TO2 * slots.scale[s]) + shift * TO2
                         k_ref[s, here, :] = jnp.exp2(x).astype(BF16)
 
+                k_copies[s].start()
                 part = k_row(ones, k_ref[s])[0:1]
                 at = pl.ds(slots.row[s], 1)
                 sums[at, :] = sums[at, :] + part
                 stat[1] = jnp.maximum(stat[1], jnp.max(part))
                 stat[2] = jnp.minimum(stat[2], jnp.min(part))
 
+        for s in range(total):
+
+            @pl.when(slots.live[s])
+            def _():
+                k_copies[s].wait()
+
         l_ref[...] = to_log(sums[...], shift)
         floats[0, total + 1] = stat[1]
         return sums_fine(stat[2], stat[1], stat[1])
@@ -223,10 +230,10 @@
     send_copies(l_ref, copies_ref)
 
 
-def row_kernel(total, n_parts, ints, floats, log_b, cost_hbm, k_ref, _, *rest):
-    parts, (copies_ref, _, l_ref, g, sums, stat, cost_v, other8, out8, sem) = rest[:n_parts], rest[n_parts:]
+def row_kernel(total, ints, floats, log_b, cost_hbm, k_ref, parts, *rest):
+    copies_ref, l_ref, g, sums, stat, cost_v, other8, out8, sem = rest
     slots = Slots(ints, floats, total)
-    g[...] = EPS * log_b[...] - EPS * lse([p[...] for p in parts])
+    g[...] = EPS * log_b[...] - EPS * lse([parts[k] for k in range(parts.shape[0])])
     sums[...] = jnp.zeros(sums.shape, F32)
     stat[0] = jnp.float32(0.0)
     stat[1] = jnp.float32(jnp.inf)
@@ -252,8 +259,8 @@
     send_copies(l_ref, copies_ref)
 
 
-def col_kernel(total, ints, floats, log_a, cost_hbm, k_ref, _, parts, *rest):
-    l_ref, _, f, sums, stat, cost_v, other8, out8, sem = rest
+def col_kernel(total, ints, floats, log_a, cost_hbm, k_ref, parts, *rest):
+    copies_ref, l_ref, f, sums, stat, cost_v, other8, out8, sem = rest
     slots = Slots(ints, floats, total)
     f[...] = EPS * log_a[...] - EPS * lse([parts[k] for k in range(parts.shape[0])])
     sums[...] = jnp.zeros(sums.shape, F32)
@@ -277,6 +284,8 @@
     @pl.when(jnp.logical_not(sums_fine(stat[1], stat[0], stat[2])))
     def _():
         slow_lse(slots, cost_hbm, cost_v, sem, other8, out8, f, l_ref, False)
+
+    send_copies(l_ref, copies_ref)
 
 
 def label_kernel(total, ints, floats, log_a, cost_hbm, k_ref, labels, parts, *rest):
@@ -289,14 +298,13 @@
     stat[0] = jnp.float32(0.0)
     stat[1] = jnp.float32(jnp.inf)
     stat[2] = slots.high
-    my_outer, my_inner = slots.tgt // INNER, slots.tgt % INNER
+    per = labels.shape[0] // acc.shape[0]
     for s in range(slots.total):
 
         @pl.when(slots.live[s])
         def _():
             u = jnp.exp2(f_out[pl.ds(slots.row[s], 1), :] * TO2)
-            outer = slots.row[s] ^ my_outer
-            lab = jnp.concatenate([labels[outer, z ^ my_inner] for z in range(INNER)], axis=1)
+            lab = jnp.concatenate([labels[slots.row[s] * per + p] for p in range(per)], axis=1)
             weighted = lab.astype(F32) * u
             hi = weighted.astype(BF16)
             low = (weighted - hi.astype(F32)).astype(BF16)
@@ -333,7 +341,7 @@
                     here = pl.ds(pl.multiple_of(i * 128, 128), 128)
                     z = tile_z(cost_v, slots.scale[s], other8, i, j, False)
                     p = jnp.exp(z - out8[pl.ds(i, 1), :]).astype(BF16)
-                    lab = labels[slots.row[s] ^ my_outer, j ^ my_inner]
+                    lab = labels[slots.row[s] * per + j]
                     term = jnp.dot(lab, p, preferred_element_type=F32)
                     acc[slots.col[s], :, here] = acc[slots.col[s], :, here] + term
 
@@ -356,6 +364,10 @@
             def _():
                 send[c, :classes] = mean
                 send[c, classes:] = tail
+
+
+def pass_kernel(*refs):
+    pass
 
 
 def merge_kernel(keep, got, *outs):
@@ -417,25 +429,10 @@
     def xor(x, axis, k):
         return lax.ppermute(x, axis, [(i, i ^ k) for i in range(lax.axis_size(axis))])
 
-    def doubled(part, axis):
-        k = 1
-        while 2 * k < lax.axis_size(axis):
-            part = lse([part, xor(part, axis, k)])
-            k *= 2
-        return [part, xor(part, axis, k)]
-
-    outer = n_tgt // INNER
-    along_z = [[x * INNER + z for z in range(INNER)] for x in range(outer)]
-    along_x = [[x * INNER + z for x in range(outer)] for z in range(INNER)]
-
-    def over_tgt(copies):
-        parts = lax.all_to_all(copies, "tgt", 0, 0, axis_index_groups=along_z, tiled=True)
-        part = lse([parts[z] for z in range(INNER)])
-        copies = jnp.broadcast_to(part[None], (outer,) + part.shape)
-        return lax.all_to_all(copies, "tgt", 0, 0, axis_index_groups=along_x, tiled=True)
-
-    def grow(lab):
-        return jnp.concatenate([lab, xor(lab, "tgt", lab.shape[0])])
+    def everyone(copies, axis):
+        return lax.all_to_all(copies, axis, 0, 0, tiled=True)
+
+    lab = everyone(jnp.broadcast_to(labels.T[None], (n_tgt, classes, labels.shape[0])), "tgt")
 
     cost = in_hbm(cost)
     vec = functools.partial(jax.ShapeDtypeStruct, dtype=F32)
@@ -446,17 +443,18 @@
     k_all, row_l, ints, floats, log_a, log_b = pl.pallas_call(
         functools.partial(build_kernel, dims),
         out_shape=(
-            pltpu.VMEM((slots, tile, tile), BF16),
-            vec((INNER, rb, tile)),
+            jax.ShapeDtypeStruct((slots, tile, tile), BF16),
+            vec((n_tgt, rb, tile)),
             pltpu.SMEM((1, 2 * slots + 1), jnp.int32),
             pltpu.SMEM((1, slots + 2), F32),
             pltpu.VMEM((rb, tile), F32),
             pltpu.VMEM((cb, tile), F32),
         ),
         in_specs=[SM] * 4 + [VM] * 2 + [HB],
-        out_specs=(VM, VM, SM, SM, VM, VM),
+        out_specs=(HB, VM, SM, SM, VM, VM),
         scratch_shapes=[
             rows,
+            pltpu.VMEM((slots, tile, tile), BF16),
             pltpu.VMEM((slots, tile, tile), BF16),
             rows,
             cols,
@@ -464,7 +462,11 @@
             chunks,
             pltpu.SMEM((3,), F32),
             pltpu.SemaphoreType.DMA((slots, 2)),
+            pltpu.SemaphoreType.DMA((slots,)),
         ],
+        cost_estimate=pl.CostEstimate(
+            flops=40 * slots * tile * tile, bytes_accessed=4 * slots * tile * tile, transcendentals=slots * tile * tile
+        ),
         compiler_params=PARAMS,
     )(
         in_hbm(cost_scale),
@@ -479,34 +481,35 @@
     scalars = (in_smem(ints), in_smem(floats))
     common = [SM] * 2 + [VM, HB, VM]
 
-    lab = labels.T[None]
     any_spec = pl.BlockSpec(memory_space=pl.ANY)
+    row_l, lab = pl.pallas_call(
+        pass_kernel,
+        out_shape=tuple(jax.ShapeDtypeStruct(x.shape, x.dtype) for x in (row_l, lab)),
+        in_specs=[any_spec] * 2,
+        out_specs=(any_spec,) * 2,
+        input_output_aliases={0: 0, 1: 1},
+        compiler_params=PARAMS,
+    )(row_l, lab)
     for step in range(ITERS):
-        row_parts = over_tgt(row_l)
+        row_parts = everyone(row_l, "tgt")
         if step == ITERS - 1:
             break
-        col_l, lab = pl.pallas_call(
+        col_l = pl.pallas_call(
             functools.partial(col_kernel, slots),
-            out_shape=(vec((cb, tile)), jax.ShapeDtypeStruct(lab.shape, BF16)),
-            in_specs=common + [any_spec, VM],
-            out_specs=(VM, any_spec),
-            scratch_shapes=[rows, cols] + work,
-            input_output_aliases={5: 1},
+            out_shape=vec((n_src, cb, tile)),
+            in_specs=common + [VM],
+            out_specs=VM,
+            scratch_shapes=[cols, rows, cols] + work,
             compiler_params=PARAMS,
-        )(*scalars, log_a, cost, k_all, lab, row_parts)
-        for _ in range(2 if step < ITERS - 2 else 1):
-            lab = grow(lab)
-        col_parts = doubled(col_l, "src")
-        row_l, lab = pl.pallas_call(
-            functools.partial(row_kernel, slots, 2),
-            out_shape=(vec((INNER, rb, tile)), jax.ShapeDtypeStruct(lab.shape, BF16)),
-            in_specs=common + [any_spec] + [VM] * 2,
-            out_specs=(VM, any_spec),
+        )(*scalars, log_a, cost, k_all, row_parts)
+        row_l = pl.pallas_call(
+            functools.partial(row_kernel, slots),
+            out_shape=vec((n_tgt, rb, tile)),
+            in_specs=common + [VM],
+            out_specs=VM,
             scratch_shapes=[rows, cols, rows] + work,
-            input_output_aliases={5: 1},
             compiler_params=PARAMS,
-        )(*scalars, log_b, cost, k_all, lab, *col_parts)
-    lab = lab.reshape(outer, INNER, classes, -1)
+        )(*scalars, log_b, cost, k_all, everyone(col_l, "src"))
 
     width = cb * tile // n_src
     half = vec((cb, classes + 8, width))

time: 501 us -> 516 us (1.030)
  Pallas kernels: 75.9 us -> 238 us
  starting transfers between devices: 162 us -> 53.9 us
  blocking collectives: 231 us -> 205 us
  waiting for transfers between devices: 28.2 us -> 8.17 us
  local copies, waits for them, and re-layouts: 1.37 us -> 7.68 us
    pallas_call x7 -> x8, Pallas kernels: 46.7 us -> 181 us  [the longest x3 71.8 us: local(): pl.pallas_call(functools.partial(row_kernel, slots), out_shape=vec((n_tgt...]
    ppermute x25 -> x11, starting transfers between devices: 162 us -> 42 us  [xor(): lax.ppermute(x, axis, [(i, i ^ k) for i in range(lax.axis_size(axis))])]
    pallas_call x1, Pallas kernels: 28.1 us -> 56 us  [local(): pl.pallas_call(functools.partial(label_kernel, slots), out_shape=(vec((rb...]
    all_to_all x8 -> x7, blocking collectives: 231 us -> 205 us  [everyone(): return lax.all_to_all(copies, axis, 0, 0, tiled=True)]
    ppermute x25 -> x11, waiting for transfers between devices: 28.2 us -> 8.17 us  [xor(): lax.ppermute(x, axis, [(i, i ^ k) for i in range(lax.axis_size(axis))])]
    all_to_all x0 -> x1, starting transfers between devices: none -> 11.9 us  [everyone(): return lax.all_to_all(copies, axis, 0, 0, tiled=True)]
  transfers between devices with their start and end apart: 25 -> 12, of which waited for: 17 -> 6; matrix products, arithmetic and copies ran while one was open for 0% -> 0% of each run, Pallas kernels for 0% -> 8%
where the time goes in v3:
time: 516 us; the launch traced here: 515 us
  Pallas kernels  238 us (46%)
  blocking collectives  205 us (40%)
  starting transfers between devices  53.9 us (10%)
  waiting for transfers between devices  8.17 us (2%)
  local copies, waits for them, and re-layouts  7.68 us (1%)
    all_to_all x7, blocking collectives, everyone(): return lax.all_to_all(copies, axis, 0, 0, tiled=True)  205 us
    pallas_call x3, Pallas kernels, local(): pl.pallas_call(functools.partial(row_kernel, slots), out_shape=vec((n_tgt...  71.8 us
    pallas_call x3, Pallas kernels, local(): pl.pallas_call(functools.partial(col_kernel, slots), out_shape=vec((n_src...  69.3 us
    pallas_call x1, Pallas kernels, local(): pl.pallas_call(functools.partial(label_kernel, slots), out_shape=(vec((rb...  56 us
    ppermute x11, starting transfers between devices, xor(): lax.ppermute(x, axis, [(i, i ^ k) for i in range(lax.axis_size(axis))])  42 us
    pallas_call x1, Pallas kernels, local(): pl.pallas_call(functools.partial(build_kernel, dims), out_shape=(jax.Shap...  40 us
    all_to_all x1, starting transfers between devices, everyone(): return lax.all_to_all(copies, axis, 0, 0, tiled=True)  11.9 us
  transfers between devices with their start and end apart: 12, of which 6 were waited for; matrix products, arithmetic and copies ran while one was open for 0% of the time, Pallas kernels for 8%

profile of v3, /device:TPU:1, one launch (start us, length us, event | category | flops | bytes accessed | tf_op | source)
XLA Modules:
  0.0 514.9 jit_solution(18042451601633986580)
XLA Ops:
  0.6 1.6 broadcast_in_dim.2
  2.3 11.9 %all-to-all-start = ((bf16[32,64,128]{2,1,0:T(8,128)(2,1)}), bf16[32,64,128]{2,1,0:T(8,128)(2,1)S(1)}, u32[]{:S(2)}, u32[]{:S(2)}) async-start(bf16[32,64,128]{2,1,0:T(8,128)(2,1)} %broadcast_in_dim.2), calls=%async_computation | async-start | bytes 1048576 | tf_op jit(solution)/shard_map/all_to_all | solution.py:433
  14.8 40.0 %shard_map.103 = (bf16[3,1024,1024]{2,1,0:T(8,128)(2,1)S(1)}, f32[32,4,1024]{2,1,0:T(4,128)S(1)}, s32[1,7]{1,0:T(1,128)S(4)}, f32[1,5]{1,0:T(1,128)S(4)}, f32[4,1024]{1,0:T(4,128)S(1)}, /*index=5*/f32[4,1024]{1,0:T(4,128)S(1)}) custom-call(f32[1,3]{1,0:T(1,128)} %scale.1, s32[1,3]{1,0:T(1,128)} %row.1, s32[1,3]{1,0:T(1,128)} %col.1, s32[1,1]{1,0:T(1,128)S(6)} %copy.18.count, ...), custom_call_target="tpu_custom_call" | custom-call | flops 125829120 | bytes 12582912 | tf_op jit(solution)/shard_map/pallas_call | solution.py:443
  54.8 2.7 copy-done
  57.5 41.4 %all_to_all.40.parts = f32[32,4,1024]{2,1,0:T(4,128)S(1)} all-to-all(f32[32,4,1024]{2,1,0:T(4,128)S(1)} %get-tuple-element.27), channel_id=1, replica_groups=mesh['src'=8,'tgt'=32] {'tgt'}, dimensions={0} | all-to-all | bytes 1048576 | tf_op jit(solution)/shard_map/all_to_all | solution.py:433
  98.9 2.8 copy-done.1
  101.7 23.1 %shard_map.105 = f32[8,4,1024]{2,1,0:T(4,128)S(1)} custom-call(s32[1,7]{1,0:T(1,128)S(4)} %get-tuple-element.20.ints, f32[1,5]{1,0:T(1,128)S(4)} %get-tuple-element.21.floats, f32[4,1024]{1,0:T(4,128)S(1)} %get-tuple-element.22.log_a, bf16[1,3,1024,1024]{3,2,1,0:T(8,128)(2,1)} %cost_hbm.15, bf16[3,1024,1024]{2,1,0:T(8,128)(2,1)S(1)} %copy-done.1, ...), custom_call_target="tpu_custom_call" | custom-call | tf_op jit(solution)/shard_map/pallas_call | solution.py:497
  124.8 25.0 %all_to_all.41.parts = f32[8,4,1024]{2,1,0:T(4,128)S(1)} all-to-all(f32[8,4,1024]{2,1,0:T(4,128)S(1)} %shard_map.105), channel_id=1, replica_groups=mesh['src'=8,'tgt'=32] {'src'}, dimensions={0} | all-to-all | bytes 262144 | tf_op jit(solution)/shard_map/all_to_all | solution.py:433
  149.8 23.9 %shard_map.106 = f32[32,4,1024]{2,1,0:T(4,128)S(1)} custom-call(s32[1,7]{1,0:T(1,128)S(4)} %get-tuple-element.20.ints, f32[1,5]{1,0:T(1,128)S(4)} %get-tuple-element.21.floats, f32[4,1024]{1,0:T(4,128)S(1)} %get-tuple-element.26.log_b, bf16[1,3,1024,1024]{3,2,1,0:T(8,128)(2,1)} %cost_hbm.15, bf16[3,1024,1024]{2,1,0:T(8,128)(2,1)S(1)} %copy-done.1, ...), custom_call_target="tpu_custom_call" | custom-call | tf_op jit(solution)/shard_map/pallas_call | solution.py:505
  173.8 31.5 %all_to_all.42.parts = f32[32,4,1024]{2,1,0:T(4,128)S(1)} all-to-all(f32[32,4,1024]{2,1,0:T(4,128)S(1)} %shard_map.106), channel_id=1, replica_groups=mesh['src'=8,'tgt'=32] {'tgt'}, dimensions={0} | all-to-all | bytes 1048576 | tf_op jit(solution)/shard_map/all_to_all | solution.py:433
  205.2 23.1 %shard_map.107 = f32[8,4,1024]{2,1,0:T(4,128)S(1)} custom-call(s32[1,7]{1,0:T(1,128)S(4)} %get-tuple-element.20.ints, f32[1,5]{1,0:T(1,128)S(4)} %get-tuple-element.21.floats, f32[4,1024]{1,0:T(4,128)S(1)} %get-tuple-element.22.log_a, bf16[1,3,1024,1024]{3,2,1,0:T(8,128)(2,1)} %cost_hbm.15, bf16[3,1024,1024]{2,1,0:T(8,128)(2,1)S(1)} %copy-done.1, ...), custom_call_target="tpu_custom_call" | custom-call | tf_op jit(solution)/shard_map/pallas_call | solution.py:497
  228.4 22.8 %all_to_all.43.parts = f32[8,4,1024]{2,1,0:T(4,128)S(1)} all-to-all(f32[8,4,1024]{2,1,0:T(4,128)S(1)} %shard_map.107), channel_id=1, replica_groups=mesh['src'=8,'tgt'=32] {'src'}, dimensions={0} | all-to-all | bytes 262144 | tf_op jit(solution)/shard_map/all_to_all | solution.py:433
  251.1 23.9 %shard_map.108 = f32[32,4,1024]{2,1,0:T(4,128)S(1)} custom-call(s32[1,7]{1,0:T(1,128)S(4)} %get-tuple-element.20.ints, f32[1,5]{1,0:T(1,128)S(4)} %get-tuple-element.21.floats, f32[4,1024]{1,0:T(4,128)S(1)} %get-tuple-element.26.log_b, bf16[1,3,1024,1024]{3,2,1,0:T(8,128)(2,1)} %cost_hbm.15, bf16[3,1024,1024]{2,1,0:T(8,128)(2,1)S(1)} %copy-done.1, ...), custom_call_target="tpu_custom_call" | custom-call | tf_op jit(solution)/shard_map/pallas_call | solution.py:505
  275.1 30.6 %all_to_all.44.parts = f32[32,4,1024]{2,1,0:T(4,128)S(1)} all-to-all(f32[32,4,1024]{2,1,0:T(4,128)S(1)} %shard_map.108), channel_id=1, replica_groups=mesh['src'=8,'tgt'=32] {'tgt'}, dimensions={0} | all-to-all | bytes 1048576 | tf_op jit(solution)/shard_map/all_to_all | solution.py:433
  305.7 23.1 %shard_map.109 = f32[8,4,1024]{2,1,0:T(4,128)S(1)} custom-call(s32[1,7]{1,0:T(1,128)S(4)} %get-tuple-element.20.ints, f32[1,5]{1,0:T(1,128)S(4)} %get-tuple-element.21.floats, f32[4,1024]{1,0:T(4,128)S(1)} %get-tuple-element.22.log_a, bf16[1,3,1024,1024]{3,2,1,0:T(8,128)(2,1)} %cost_hbm.15, bf16[3,1024,1024]{2,1,0:T(8,128)(2,1)S(1)} %copy-done.1, ...), custom_call_target="tpu_custom_call" | custom-call | tf_op jit(solution)/shard_map/pallas_call | solution.py:497
  328.8 23.0 %all_to_all.45.parts = f32[8,4,1024]{2,1,0:T(4,128)S(1)} all-to-all(f32[8,4,1024]{2,1,0:T(4,128)S(1)} %shard_map.109), channel_id=1, replica_groups=mesh['src'=8,'tgt'=32] {'src'}, dimensions={0} | all-to-all | bytes 262144 | tf_op jit(solution)/shard_map/all_to_all | solution.py:433
  351.8 23.9 %shard_map.110 = f32[32,4,1024]{2,1,0:T(4,128)S(1)} custom-call(s32[1,7]{1,0:T(1,128)S(4)} %get-tuple-element.20.ints, f32[1,5]{1,0:T(1,128)S(4)} %get-tuple-element.21.floats, f32[4,1024]{1,0:T(4,128)S(1)} %get-tuple-element.26.log_b, bf16[1,3,1024,1024]{3,2,1,0:T(8,128)(2,1)} %cost_hbm.15, bf16[3,1024,1024]{2,1,0:T(8,128)(2,1)S(1)} %copy-done.1, ...), custom_call_target="tpu_custom_call" | custom-call | tf_op jit(solution)/shard_map/pallas_call | solution.py:505
  375.8 31.2 %all_to_all.46.parts = f32[32,4,1024]{2,1,0:T(4,128)S(1)} all-to-all(f32[32,4,1024]{2,1,0:T(4,128)S(1)} %shard_map.110), channel_id=1, replica_groups=mesh['src'=8,'tgt'=32] {'tgt'}, dimensions={0} | all-to-all | bytes 1048576 | tf_op jit(solution)/shard_map/all_to_all | solution.py:433
  407.0 56.0 %shard_map.111 = (f32[4,1024]{1,0:T(4,128)S(1)}, f32[4,72,512]{2,1,0:T(8,128)S(1)}, f32[4,72,512]{2,1,0:T(8,128)S(1)}) custom-call(s32[1,7]{1,0:T(1,128)S(4)} %get-tuple-element.20.ints, f32[1,5]{1,0:T(1,128)S(4)} %get-tuple-element.21.floats, f32[4,1024]{1,0:T(4,128)S(1)} %get-tuple-element.22.log_a, bf16[1,3,1024,1024]{3,2,1,0:T(8,128)(2,1)} %cost_hbm.15, ...), custom_call_target="tpu_custom_call" | custom-call | tf_op jit(solution)/shard_map/pallas_call | solution.py:517
  463.1 2.0 collective-permute-done.got
  465.2 31.2 %collective-permute-start.1 = (bf16[80,512]{1,0:T(8,128)(2,1)S(1)}, bf16[80,512]{1,0:T(8,128)(2,1)S(1)}, u32[]{:S(2)}, u32[]{:S(2)}) collective-permute-start(bf16[80,512]{1,0:T(8,128)(2,1)S(1)} %get-tuple-element.32), channel_id=1, source_target_pairs={{0,64},{32,96},{64,0},{96,32},{128,192},{160,224},{192,128},{224,1... | collective-permute-start | bytes 245768 | tf_op jit(solution)/shard_map/ppermute | solution.py:430
  496.5 2.2 collective-permute-start.2
  499.0 3.6 collective-permute-done.2.rest_2_
  502.6 1.9 collective-permute-done.3.rest_3_
  504.7 0.5 collective-permute-start.6
  505.2 0.8 collective-permute-start.5
  506.0 2.0 collective-permute-start.4
  508.0 1.9 collective-permute-start.7
  510.1 2.4 collective-permute-start.10
  512.6 0.6 collective-permute-start.8
  513.2 0.6 copy.15
  514.1 0.8 shard_map.114
  (17 shorter events, 1.3 us)
Async XLA Ops:
  2.3 55.2 %all-to-all-start = ((bf16[32,64,128]{2,1,0:T(8,128)(2,1)}), bf16[32,64,128]{2,1,0:T(8,128)(2,1)S(1)}, u32[]{:S(2)}, u32[]{:S(2)}) async-start(bf16[32,64,128]{2,1,0:T(8,128)(2,1)} %broadcast_in_dim.2), calls=%async_computation | async-start | bytes 1048576 | tf_op jit(solution)/shard_map/all_to_all | solution.py:433
  54.8 2.7 copy-start
  98.9 2.8 copy-start.1
  463.0 2.1 collective-permute-start
  465.2 33.7 %collective-permute-start.1 = (bf16[80,512]{1,0:T(8,128)(2,1)S(1)}, bf16[80,512]{1,0:T(8,128)(2,1)S(1)}, u32[]{:S(2)}, u32[]{:S(2)}) collective-permute-start(bf16[80,512]{1,0:T(8,128)(2,1)S(1)} %get-tuple-element.32), channel_id=1, source_target_pairs={{0,64},{32,96},{64,0},{96,32},{128,192},{160,224},{192,128},{224,1... | collective-permute-start | bytes 245768 | tf_op jit(solution)/shard_map/ppermute | solution.py:430
  496.5 6.1 %collective-permute-start.2 = (bf16[80,512]{1,0:T(8,128)(2,1)S(1)}, bf16[80,512]{1,0:T(8,128)(2,1)S(1)}, u32[]{:S(2)}, u32[]{:S(2)}) collective-permute-start(bf16[80,512]{1,0:T(8,128)(2,1)S(1)} %get-tuple-element.33), channel_id=1, source_target_pairs={{0,128},{32,160},{64,192},{96,224},{128,0},{160,32},{192,64},{224,... | collective-permute-start | bytes 245768 | tf_op jit(solution)/shard_map/ppermute | solution.py:430
  498.7 5.9 %collective-permute-start.3 = (bf16[80,512]{1,0:T(8,128)(2,1)S(1)}, bf16[80,512]{1,0:T(8,128)(2,1)S(1)}, u32[]{:S(2)}, u32[]{:S(2)}) collective-permute-start(bf16[80,512]{1,0:T(8,128)(2,1)S(1)} %get-tuple-element.34), channel_id=1, source_target_pairs={{0,192},{32,224},{64,128},{96,160},{128,64},{160,96},{192,0},{224,... | collective-permute-start | bytes 245768 | tf_op jit(solution)/shard_map/ppermute | solution.py:430
  504.7 5.5 %collective-permute-start.6 = (bf16[80,512]{1,0:T(8,128)(2,1)S(1)}, bf16[80,512]{1,0:T(8,128)(2,1)S(1)}, u32[]{:S(2)}, u32[]{:S(2)}) collective-permute-start(bf16[80,512]{1,0:T(8,128)(2,1)S(1)} %shard_map.113.refs_0_), channel_id=1, source_target_pairs={{0,192},{32,224},{64,128},{96,160},{128,64},{160,96},{192,0},{224,... | collective-permute-start | bytes 245768 | tf_op jit(solution)/shard_map/ppermute | solution.py:430
  505.2 7.4 %collective-permute-start.5 = (bf16[80,512]{1,0:T(8,128)(2,1)S(1)}, bf16[80,512]{1,0:T(8,128)(2,1)S(1)}, u32[]{:S(2)}, u32[]{:S(2)}) collective-permute-start(bf16[80,512]{1,0:T(8,128)(2,1)S(1)} %shard_map.113.refs_0_), channel_id=1, source_target_pairs={{0,128},{32,160},{64,192},{96,224},{128,0},{160,32},{192,64},{224,... | collective-permute-start | bytes 245768 | tf_op jit(solution)/shard_map/ppermute | solution.py:430
  506.0 6.6 %collective-permute-start.4 = (bf16[80,512]{1,0:T(8,128)(2,1)S(1)}, bf16[80,512]{1,0:T(8,128)(2,1)S(1)}, u32[]{:S(2)}, u32[]{:S(2)}) collective-permute-start(bf16[80,512]{1,0:T(8,128)(2,1)S(1)} %shard_map.113.refs_0_), channel_id=1, source_target_pairs={{0,64},{32,96},{64,0},{96,32},{128,192},{160,224},{192,128},{224,1... | collective-permute-start | bytes 245768 | tf_op jit(solution)/shard_map/ppermute | solution.py:430
  508.0 5.8 %collective-permute-start.7 = (bf16[80,512]{1,0:T(8,128)(2,1)S(1)}, bf16[80,512]{1,0:T(8,128)(2,1)S(1)}, u32[]{:S(2)}, u32[]{:S(2)}) collective-permute-start(bf16[80,512]{1,0:T(8,128)(2,1)S(1)} %shard_map.113.refs_0_), channel_id=1, source_target_pairs={{0,32},{32,0},{64,96},{96,64},{128,160},{160,128},{192,224},{224,1... | collective-permute-start | bytes 245768 | tf_op jit(solution)/shard_map/ppermute | solution.py:430
  510.1 3.6 collective-permute-start.10
  512.6 1.3 collective-permute-start.9
  512.6 1.5 collective-permute-start.8

commit v4 on v2

--- a/solution.py
+++ b/solution.py
@@ -13,6 +13,8 @@
 LOG2E = 1.4426950408889634
 TO2 = LOG2E / EPS
 INNER = 8
+FLAT = (16, 256)
+SHARE = ((0, 1, 2), (3, 4, 5), (6, 7))
 LIMIT = 40 * 1024 * 1024
 F32, BF16 = jnp.float32, jnp.bfloat16
 
@@ -123,6 +125,27 @@
 def send_copies(l_ref, copies_ref):
     for k in range(copies_ref.shape[0]):
         copies_ref[k] = l_ref[...]
+
+
+def send_relative(l_ref, pot, log_mass, flat, copies_ref):
+    rel = jnp.exp(l_ref[...] + pot[...] / EPS - log_mass[...])
+    count, width = rel.shape[0], flat.shape[1]
+    for c in range(rel.shape[1] // width):
+        flat[c * count : (c + 1) * count, :] = rel[:, c * width : (c + 1) * width]
+    rel = flat[...].astype(BF16)
+    for k in range(copies_ref.shape[0]):
+        copies_ref[k, : flat.shape[0]] = rel
+
+
+def new_potential(out, log_mass, parts, prev, flat):
+    if prev is None:
+        out[...] = EPS * log_mass[...] - EPS * lse([parts[k] for k in range(parts.shape[0])])
+        return
+    flat[...] = tree_sum([parts[k, : flat.shape[0]].astype(F32) for k in range(parts.shape[0])])
+    count, width = out.shape[0], flat.shape[1]
+    for c in range(out.shape[1] // width):
+        here = slice(c * width, (c + 1) * width)
+        out[:, here] = prev[:, here] - EPS * jnp.log(flat[c * count : (c + 1) * count, :])
 
 
 def sums_fine(low, high, others):
@@ -223,10 +246,12 @@
     send_copies(l_ref, copies_ref)
 
 
-def row_kernel(total, n_parts, ints, floats, log_b, cost_hbm, k_ref, _, *rest):
-    parts, (copies_ref, _, l_ref, g, sums, stat, cost_v, other8, out8, sem) = rest[:n_parts], rest[n_parts:]
+def row_kernel(total, first, with_labels, ints, floats, log_b, cost_hbm, k_ref, parts, log_a, f, *rest):
+    prev, rest = (None, rest) if first else (rest[0], rest[1:])
+    lab, rest = (rest[0], rest[1:]) if with_labels else (None, rest)
+    copies_ref, g, l_ref, flat, sums, stat, cost_v, other8, out8, sem = rest
     slots = Slots(ints, floats, total)
-    g[...] = EPS * log_b[...] - EPS * lse([p[...] for p in parts])
+    new_potential(g, log_b, parts, prev, flat)
     sums[...] = jnp.zeros(sums.shape, F32)
     stat[0] = jnp.float32(0.0)
     stat[1] = jnp.float32(jnp.inf)
@@ -249,13 +274,28 @@
     def _():
         slow_lse(slots, cost_hbm, cost_v, sem, other8, out8, g, l_ref, True)
 
-    send_copies(l_ref, copies_ref)
-
-
-def col_kernel(total, ints, floats, log_a, cost_hbm, k_ref, _, parts, *rest):
-    l_ref, _, f, sums, stat, cost_v, other8, out8, sem = rest
+    send_relative(l_ref, f, log_a, flat, copies_ref)
+    if with_labels:
+        half = lab.shape[0] // 2
+        for k in range(copies_ref.shape[0]):
+            copies_ref[k, flat.shape[0] :] = jnp.concatenate([lab[:half], lab[half:]], axis=1)
+
+
+def relay_kernel(share, parts, lab, copies_ref):
+    rows = FLAT[0]
+    total = tree_sum([parts[k, :rows].astype(F32) for k in range(parts.shape[0])]).astype(BF16)
+    high = lab.shape[1] - rows
+    for k in range(copies_ref.shape[0]):
+        copies_ref[k, :rows] = total
+        for i, p in enumerate(share):
+            copies_ref[k, rows + i * high : rows + (i + 1) * high] = lab[p, rows:]
+
+
+def col_kernel(total, first, ints, floats, log_a, cost_hbm, k_ref, parts, *rest):
+    (prev, log_b, g), rest = ((None, None, None), rest) if first else (rest[:3], rest[3:])
+    copies_ref, f, l_ref, flat, sums, stat, cost_v, other8, out8, sem = rest
     slots = Slots(ints, floats, total)
-    f[...] = EPS * log_a[...] - EPS * lse([parts[k] for k in range(parts.shape[0])])
+    new_potential(f, log_a, parts, prev, flat)
     sums[...] = jnp.zeros(sums.shape, F32)
     stat[0] = jnp.float32(0.0)
     stat[1] = jnp.float32(jnp.inf)
@@ -278,25 +318,37 @@
     def _():
         slow_lse(slots, cost_hbm, cost_v, sem, other8, out8, f, l_ref, False)
 
-
-def label_kernel(total, ints, floats, log_a, cost_hbm, k_ref, labels, parts, *rest):
-    f_out, keep, send, acc, l_ref, sums, stat, cost_v, other8, out8, sem = rest
+    if first:
+        send_copies(l_ref, copies_ref)
+    else:
+        send_relative(l_ref, g, log_b, flat, copies_ref)
+
+
+def label_kernel(total, ints, floats, log_a, cost_hbm, k_ref, prev, *rest):
+    boxes, rest = rest[: len(SHARE)], rest[len(SHARE) :]
+    f_out, keep, send, acc, l_ref, flat, lab_v, sums, stat, cost_v, other8, out8, sem = rest
     slots = Slots(ints, floats, total)
     classes = acc.shape[1]
-    f_out[...] = EPS * log_a[...] - EPS * lse([parts[k] for k in range(parts.shape[0])])
+    new_potential(f_out, log_a, boxes[-1], prev, flat)
     sums[...] = jnp.zeros(sums.shape, F32)
     acc[...] = jnp.zeros(acc.shape, F32)
     stat[0] = jnp.float32(0.0)
     stat[1] = jnp.float32(jnp.inf)
     stat[2] = slots.high
-    my_outer, my_inner = slots.tgt // INNER, slots.tgt % INNER
+    high = classes // 2
+
+    def label_piece(block, p):
+        box = [i for i, share in enumerate(SHARE) if p in share][0]
+        at = FLAT[0] + SHARE[box].index(p) * high
+        both = boxes[box][block, at : at + high]
+        return jnp.concatenate([both[:, :128], both[:, 128:]], axis=0)
+
     for s in range(slots.total):
 
         @pl.when(slots.live[s])
         def _():
             u = jnp.exp2(f_out[pl.ds(slots.row[s], 1), :] * TO2)
-            outer = slots.row[s] ^ my_outer
-            lab = jnp.concatenate([labels[outer, z ^ my_inner] for z in range(INNER)], axis=1)
+            lab = jnp.concatenate([label_piece(slots.row[s], p) for p in range(INNER)], axis=1)
             weighted = lab.astype(F32) * u
             hi = weighted.astype(BF16)
             low = (weighted - hi.astype(F32)).astype(BF16)
@@ -326,6 +378,8 @@
                 copy.wait()
                 chunked(f_out[pl.ds(slots.row[s], 1), :], other8)
                 chunked(l_ref[pl.ds(slots.col[s], 1), :], out8)
+                for p in range(INNER):
+                    lab_v[p] = label_piece(slots.row[s], p)
 
                 @pl.loop(0, chunks * chunks)
                 def _(ij):
@@ -333,8 +387,7 @@
                     here = pl.ds(pl.multiple_of(i * 128, 128), 128)
                     z = tile_z(cost_v, slots.scale[s], other8, i, j, False)
                     p = jnp.exp(z - out8[pl.ds(i, 1), :]).astype(BF16)
-                    lab = labels[slots.row[s] ^ my_outer, j ^ my_inner]
-                    term = jnp.dot(lab, p, preferred_element_type=F32)
+                    term = jnp.dot(lab_v[j], p, preferred_element_type=F32)
                     acc[slots.col[s], :, here] = acc[slots.col[s], :, here] + term
 
     core = slots.src % 2
@@ -428,14 +481,8 @@
     along_z = [[x * INNER + z for z in range(INNER)] for x in range(outer)]
     along_x = [[x * INNER + z for x in range(outer)] for z in range(INNER)]
 
-    def over_tgt(copies):
-        parts = lax.all_to_all(copies, "tgt", 0, 0, axis_index_groups=along_z, tiled=True)
-        part = lse([parts[z] for z in range(INNER)])
-        copies = jnp.broadcast_to(part[None], (outer,) + part.shape)
-        return lax.all_to_all(copies, "tgt", 0, 0, axis_index_groups=along_x, tiled=True)
-
-    def grow(lab):
-        return jnp.concatenate([lab, xor(lab, "tgt", lab.shape[0])])
+    def everyone(copies, axis, groups=None):
+        return lax.all_to_all(copies, axis, 0, 0, axis_index_groups=groups, tiled=True)
 
     cost = in_hbm(cost)
     vec = functools.partial(jax.ShapeDtypeStruct, dtype=F32)
@@ -479,34 +526,50 @@
     scalars = (in_smem(ints), in_smem(floats))
     common = [SM] * 2 + [VM, HB, VM]
 
-    lab = labels.T[None]
-    any_spec = pl.BlockSpec(memory_space=pl.ANY)
+    flat = pltpu.VMEM(FLAT, F32)
+    sent = functools.partial(jax.ShapeDtypeStruct, dtype=BF16)
+    lab_t, boxes = labels.T, []
+    f_pot = g_pot = lab_z = None
     for step in range(ITERS):
-        row_parts = over_tgt(row_l)
+        along = everyone(row_l, "tgt", along_z)
+        if step == 0:
+            part = lse([along[z] for z in range(INNER)])
+            copies = jnp.broadcast_to(part[None], (outer,) + part.shape)
+        else:
+            lab_z = along if step == 1 else lab_z
+            share = SHARE[step - 1]
+            high = FLAT[0] + len(share) * (lab_z.shape[1] - FLAT[0])
+            copies = pl.pallas_call(
+                functools.partial(relay_kernel, share),
+                out_shape=sent((outer, high, FLAT[1])),
+                in_specs=[VM] * 2,
+                out_specs=VM,
+                compiler_params=PARAMS,
+            )(along, lab_z)
+        row_parts = everyone(copies, "tgt", along_x)
+        if step:
+            boxes.append(row_parts)
         if step == ITERS - 1:
             break
-        col_l, lab = pl.pallas_call(
-            functools.partial(col_kernel, slots),
-            out_shape=(vec((cb, tile)), jax.ShapeDtypeStruct(lab.shape, BF16)),
-            in_specs=common + [any_spec, VM],
-            out_specs=(VM, any_spec),
-            scratch_shapes=[rows, cols] + work,
-            input_output_aliases={5: 1},
+        first = step == 0
+        col_l, f_pot = pl.pallas_call(
+            functools.partial(col_kernel, slots, first),
+            out_shape=(vec((n_src, cb, tile)) if first else sent((n_src,) + FLAT), vec((rb, tile))),
+            in_specs=common + [VM] * (1 if first else 4),
+            out_specs=(VM, VM),
+            scratch_shapes=[cols, flat, cols] + work,
             compiler_params=PARAMS,
-        )(*scalars, log_a, cost, k_all, lab, row_parts)
-        for _ in range(2 if step < ITERS - 2 else 1):
-            lab = grow(lab)
-        col_parts = doubled(col_l, "src")
-        row_l, lab = pl.pallas_call(
-            functools.partial(row_kernel, slots, 2),
-            out_shape=(vec((INNER, rb, tile)), jax.ShapeDtypeStruct(lab.shape, BF16)),
-            in_specs=common + [any_spec] + [VM] * 2,
-            out_specs=(VM, any_spec),
-            scratch_shapes=[rows, cols, rows] + work,
-            input_output_aliases={5: 1},
+        )(*scalars, log_a, cost, k_all, row_parts, *(() if first else (f_pot, log_b, g_pot)))
+        col_parts = everyone(col_l, "src")
+        extra = FLAT[0] * lab_t.size // (FLAT[0] * FLAT[1]) if first else 0
+        row_l, g_pot = pl.pallas_call(
+            functools.partial(row_kernel, slots, first, first),
+            out_shape=(sent((INNER, FLAT[0] + extra, FLAT[1])), vec((cb, tile))),
+            in_specs=common + [VM] * 4,
+            out_specs=(VM, VM),
+            scratch_shapes=[rows, flat, rows] + work,
             compiler_params=PARAMS,
-        )(*scalars, log_b, cost, k_all, lab, *col_parts)
-    lab = lab.reshape(outer, INNER, classes, -1)
+        )(*scalars, log_b, cost, k_all, col_parts, log_a, f_pot, lab_t if first else g_pot)
 
     width = cb * tile // n_src
     half = vec((cb, classes + 8, width))
@@ -514,11 +577,17 @@
     f_pot, keep, send = pl.pallas_call(
         functools.partial(label_kernel, slots),
         out_shape=(vec((rb, tile)), half, half),
-        in_specs=common + [VM] + [VM],
+        in_specs=common + [VM] * (1 + len(SHARE)),
         out_specs=(VM,) * 3,
-        scratch_shapes=[pltpu.VMEM((cb, classes, tile), F32), cols, cols] + work,
+        scratch_shapes=[
+            pltpu.VMEM((cb, classes, tile), F32),
+            cols,
+            flat,
+            pltpu.VMEM((INNER, classes, 128), BF16),
+            cols,
+        ] + work,
         compiler_params=PARAMS,
-    )(*scalars, log_a, cost, k_all, lab, row_parts)
+    )(*scalars, log_a, cost, k_all, f_pot, *boxes)
     n_y = n_src // 2
     pieces = pl.pallas_call(
         merge_kernel,

time: 501 us -> 490 us (0.978)
  the two profiles are of different devices: /device:TPU:1 before, /device:TPU:33 now
where the time goes in v4:
time: 490 us; the launch traced here: 488 us
  Pallas kernels  355 us (72%)
  blocking collectives  109 us (22%)
  starting transfers between devices  17 us (3%)
  waiting for transfers between devices  6.2 us (1%)
    all_to_all x11, blocking collectives, everyone(): lax.all_to_all(copies, axis, 0, 0, axis_index_groups=groups, tiled=True)  109 us
    pallas_call x3, Pallas kernels, local(): pl.pallas_call(functools.partial(row_kernel, slots, first, first), out_sh...  108 us
    pallas_call x3, Pallas kernels, local(): pl.pallas_call(functools.partial(col_kernel, slots, first), out_shape=(ve...  103 us
    pallas_call x1, Pallas kernels, local(): pl.pallas_call(functools.partial(label_kernel, slots), out_shape=(vec((rb...  83.9 us
    pallas_call x1, Pallas kernels, local(): pl.pallas_call(functools.partial(build_kernel, dims), out_shape=(pltpu.VM...  57.9 us
    ppermute x11, starting transfers between devices, xor(): lax.ppermute(x, axis, [(i, i ^ k) for i in range(lax.axis_size(axis))])  17 us
  transfers between devices with their start and end apart: 11, of which 6 were waited for; matrix products, arithmetic and copies ran while one was open for 0% of the time, Pallas kernels for 0%

profile of v4, /device:TPU:33, one launch (start us, length us, event | category | flops | bytes accessed | tf_op | source)
XLA Modules:
  0.0 488.4 jit_solution(5739128167808638902)
XLA Ops:
  1.3 57.9 %shard_map.103 = (bf16[3,1024,1024]{2,1,0:T(8,128)(2,1)S(1)}, f32[8,4,1024]{2,1,0:T(4,128)S(1)}, s32[1,7]{1,0:T(1,128)S(4)}, f32[1,5]{1,0:T(1,128)S(4)}, f32[4,1024]{1,0:T(4,128)S(1)}, /*index=5*/f32[4,1024]{1,0:T(4,128)S(1)}) custom-call(f32[1,3]{1,0:T(1,128)} %scale.1, s32[1,3]{1,0:T(1,128)} %row.1, s32[1,3]{1,0:T(1,128)} %col.1, s32[1,1]{1,0:T(1,128)S(6)} %copy.14.count, ...), custom_call_target="tpu_custom_call" | custom-call | tf_op jit(solution)/shard_map/pallas_call | solution.py:493
  59.2 13.7 %all_to_all.55 = f32[8,4,1024]{2,1,0:T(4,128)S(1)} all-to-all(f32[8,4,1024]{2,1,0:T(4,128)S(1)} %get-tuple-element.34), channel_id=1, replica_groups={{0,1,2,3,4,5,6,7},{8,9,10,11,12,13,14,15},{16,17,18,19,20,21,22,23},{24..., dimensions={0} | all-to-all | bytes 262144 | tf_op jit(solution)/shard_map/all_to_all | solution.py:485
  72.9 8.0 %all_to_all.56.parts = f32[4,4,1024]{2,1,0:T(4,128)S(1)} all-to-all(f32[4,4,1024]{2,1,0:T(4,128)S(1)} %broadcast_in_dim.9), channel_id=1, replica_groups={{0,8,16,24},{1,9,17,25},{2,10,18,26},{3,11,19,27},{4,12,20,28},{5,13,21..., dimensions={0} | all-to-all | bytes 131072 | tf_op jit(solution)/shard_map/all_to_all | solution.py:485
  81.0 34.5 %shard_map.104 = (f32[8,4,1024]{2,1,0:T(4,128)S(1)}, f32[4,1024]{1,0:T(4,128)S(1)}) custom-call(s32[1,7]{1,0:T(1,128)S(4)} %get-tuple-element.29.ints, f32[1,5]{1,0:T(1,128)S(4)} %get-tuple-element.30.floats, f32[4,1024]{1,0:T(4,128)S(1)} %get-tuple-element.31.log_a, bf16[1,3,1024,1024]{3,2,1,0:T(8,128)(2,1)} %cost_hbm.15, ...), custom_call_target="tpu_custom_call" | custom-call | tf_op jit(solution)/shard_map/pallas_call | solution.py:555
  115.4 13.6 %all_to_all.57.parts = f32[8,4,1024]{2,1,0:T(4,128)S(1)} all-to-all(f32[8,4,1024]{2,1,0:T(4,128)S(1)} %get-tuple-element.35), channel_id=1, replica_groups=mesh['src'=8,'tgt'=32] {'src'}, dimensions={0} | all-to-all | bytes 262144 | tf_op jit(solution)/shard_map/all_to_all | solution.py:485
  129.1 35.8 %shard_map.105 = (bf16[8,48,256]{2,1,0:T(8,128)(2,1)S(1)}, f32[4,1024]{1,0:T(4,128)S(1)}) custom-call(s32[1,7]{1,0:T(1,128)S(4)} %get-tuple-element.29.ints, f32[1,5]{1,0:T(1,128)S(4)} %get-tuple-element.30.floats, f32[4,1024]{1,0:T(4,128)S(1)} %get-tuple-element.33.log_b.rest_1_, bf16[1,3,1024,1024]{3,2,1,0:T(8,128)(2,1)} %cost_hbm.15, ...), custom_call_target="tpu_custom_call" | custom-call | tf_op jit(solution)/shard_map/pallas_call | solution.py:565
  164.9 10.4 %all_to_all.58.parts.lab = bf16[8,48,256]{2,1,0:T(8,128)(2,1)S(1)} all-to-all(bf16[8,48,256]{2,1,0:T(8,128)(2,1)S(1)} %get-tuple-element.37), channel_id=1, replica_groups={{0,1,2,3,4,5,6,7},{8,9,10,11,12,13,14,15},{16,17,18,19,20,21,22,23},{24..., dimensions={0} | all-to-all | bytes 393216 | tf_op jit(solution)/shard_map/all_to_all | solution.py:485
  175.3 7.7 %all_to_all.59.parts.rest_0_ = bf16[4,112,256]{2,1,0:T(8,128)(2,1)S(1)} all-to-all(bf16[4,112,256]{2,1,0:T(8,128)(2,1)S(1)} %shard_map.106), channel_id=1, replica_groups={{0,8,16,24},{1,9,17,25},{2,10,18,26},{3,11,19,27},{4,12,20,28},{5,13,21..., dimensions={0} | all-to-all | bytes 458752 | tf_op jit(solution)/shard_map/all_to_all | solution.py:485
  183.0 34.5 %shard_map.107 = (bf16[8,16,256]{2,1,0:T(8,128)(2,1)S(1)}, f32[4,1024]{1,0:T(4,128)S(1)}) custom-call(s32[1,7]{1,0:T(1,128)S(4)} %get-tuple-element.29.ints, f32[1,5]{1,0:T(1,128)S(4)} %get-tuple-element.30.floats, f32[4,1024]{1,0:T(4,128)S(1)} %get-tuple-element.31.log_a, bf16[1,3,1024,1024]{3,2,1,0:T(8,128)(2,1)} %cost_hbm.15, ...), custom_call_target="tpu_custom_call" | custom-call | tf_op jit(solution)/shard_map/pallas_call | solution.py:555
  217.5 11.9 %all_to_all.60.parts = bf16[8,16,256]{2,1,0:T(8,128)(2,1)S(1)} all-to-all(bf16[8,16,256]{2,1,0:T(8,128)(2,1)S(1)} %get-tuple-element.39), channel_id=1, replica_groups=mesh['src'=8,'tgt'=32] {'src'}, dimensions={0} | all-to-all | bytes 131072 | tf_op jit(solution)/shard_map/all_to_all | solution.py:485
  229.4 35.8 %shard_map.108 = (bf16[8,16,256]{2,1,0:T(8,128)(2,1)S(1)}, f32[4,1024]{1,0:T(4,128)S(1)}) custom-call(s32[1,7]{1,0:T(1,128)S(4)} %get-tuple-element.29.ints, f32[1,5]{1,0:T(1,128)S(4)} %get-tuple-element.30.floats, f32[4,1024]{1,0:T(4,128)S(1)} %get-tuple-element.33.log_b.rest_1_, bf16[1,3,1024,1024]{3,2,1,0:T(8,128)(2,1)} %cost_hbm.15, ...), custom_call_target="tpu_custom_call" | custom-call | tf_op jit(solution)/shard_map/pallas_call | solution.py:565
  265.2 8.6 %all_to_all.61.parts = bf16[8,16,256]{2,1,0:T(8,128)(2,1)S(1)} all-to-all(bf16[8,16,256]{2,1,0:T(8,128)(2,1)S(1)} %get-tuple-element.41), channel_id=1, replica_groups={{0,1,2,3,4,5,6,7},{8,9,10,11,12,13,14,15},{16,17,18,19,20,21,22,23},{24..., dimensions={0} | all-to-all | bytes 131072 | tf_op jit(solution)/shard_map/all_to_all | solution.py:485
  273.9 7.7 %all_to_all.62.parts.rest_1_ = bf16[4,112,256]{2,1,0:T(8,128)(2,1)S(1)} all-to-all(bf16[4,112,256]{2,1,0:T(8,128)(2,1)S(1)} %shard_map.109), channel_id=1, replica_groups={{0,8,16,24},{1,9,17,25},{2,10,18,26},{3,11,19,27},{4,12,20,28},{5,13,21..., dimensions={0} | all-to-all | bytes 458752 | tf_op jit(solution)/shard_map/all_to_all | solution.py:485
  281.6 34.5 %shard_map.110 = (bf16[8,16,256]{2,1,0:T(8,128)(2,1)S(1)}, f32[4,1024]{1,0:T(4,128)S(1)}) custom-call(s32[1,7]{1,0:T(1,128)S(4)} %get-tuple-element.29.ints, f32[1,5]{1,0:T(1,128)S(4)} %get-tuple-element.30.floats, f32[4,1024]{1,0:T(4,128)S(1)} %get-tuple-element.31.log_a, bf16[1,3,1024,1024]{3,2,1,0:T(8,128)(2,1)} %cost_hbm.15, ...), custom_call_target="tpu_custom_call" | custom-call | tf_op jit(solution)/shard_map/pallas_call | solution.py:555
  316.1 10.6 %all_to_all.63.parts = bf16[8,16,256]{2,1,0:T(8,128)(2,1)S(1)} all-to-all(bf16[8,16,256]{2,1,0:T(8,128)(2,1)S(1)} %get-tuple-element.44), channel_id=1, replica_groups=mesh['src'=8,'tgt'=32] {'src'}, dimensions={0} | all-to-all | bytes 131072 | tf_op jit(solution)/shard_map/all_to_all | solution.py:485
  326.7 36.6 %shard_map.111 = (bf16[8,16,256]{2,1,0:T(8,128)(2,1)S(1)}, f32[4,1024]{1,0:T(4,128)}) custom-call(s32[1,7]{1,0:T(1,128)S(4)} %get-tuple-element.29.ints, f32[1,5]{1,0:T(1,128)S(4)} %get-tuple-element.30.floats, f32[4,1024]{1,0:T(4,128)S(1)} %get-tuple-element.33.log_b.rest_1_, bf16[1,3,1024,1024]{3,2,1,0:T(8,128)(2,1)} %cost_hbm.15, ...), custom_call_target="tpu_custom_call" | custom-call | tf_op jit(solution)/shard_map/pallas_call | solution.py:565
  363.2 8.6 %all_to_all.64.parts = bf16[8,16,256]{2,1,0:T(8,128)(2,1)S(1)} all-to-all(bf16[8,16,256]{2,1,0:T(8,128)(2,1)S(1)} %get-tuple-element.45), channel_id=1, replica_groups={{0,1,2,3,4,5,6,7},{8,9,10,11,12,13,14,15},{16,17,18,19,20,21,22,23},{24..., dimensions={0} | all-to-all | bytes 131072 | tf_op jit(solution)/shard_map/all_to_all | solution.py:485
  371.8 7.7 %all_to_all.65.rest_2_ = bf16[4,80,256]{2,1,0:T(8,128)(2,1)S(1)} all-to-all(bf16[4,80,256]{2,1,0:T(8,128)(2,1)S(1)} %shard_map.112), channel_id=1, replica_groups={{0,8,16,24},{1,9,17,25},{2,10,18,26},{3,11,19,27},{4,12,20,28},{5,13,21..., dimensions={0} | all-to-all | bytes 327680 | tf_op jit(solution)/shard_map/all_to_all | solution.py:485
  379.5 83.9 %shard_map.113 = (f32[4,1024]{1,0:T(4,128)S(1)}, f32[4,72,512]{2,1,0:T(8,128)S(1)}, f32[4,72,512]{2,1,0:T(8,128)S(1)}) custom-call(s32[1,7]{1,0:T(1,128)S(4)} %get-tuple-element.29.ints, f32[1,5]{1,0:T(1,128)S(4)} %get-tuple-element.30.floats, f32[4,1024]{1,0:T(4,128)S(1)} %get-tuple-element.31.log_a, bf16[1,3,1024,1024]{3,2,1,0:T(8,128)(2,1)} %cost_hbm.15, ...), custom_call_target="tpu_custom_call" | custom-call | tf_op jit(solution)/shard_map/pallas_call | solution.py:577
  463.5 3.7 collective-permute-start
  467.2 1.6 collective-permute-done.got
  469.1 1.5 collective-permute-start.2
  470.6 2.3 collective-permute-start.3
  472.9 1.8 collective-permute-done.2.rest_2_
  474.7 1.7 collective-permute-done.3.rest_3_
  476.6 2.4 collective-permute-start.6
  479.0 0.9 collective-permute-start.4
  479.9 1.9 collective-permute-start.7
  481.8 1.7 collective-permute-start.10
  483.8 2.4 collective-permute-start.9
  486.3 0.6 copy.13
  487.5 0.8 shard_map.116
  (20 shorter events, 1.5 us)
Async XLA Ops:
  80.9 48.1 %copy-start = (bf16[128,64]{0,1:T(8,128)(2,1)S(1)}, bf16[128,64]{0,1:T(8,128)(2,1)}, u32[]{:S(2)}) copy-start(bf16[128,64]{0,1:T(8,128)(2,1)} %param.15) | copy-start | bytes 49156
  463.5 5.3 %collective-permute-start = (f32[4,72,512]{2,1,0:T(8,128)S(1)}, f32[4,72,512]{2,1,0:T(8,128)S(1)}, u32[]{:S(2)}, u32[]{:S(2)}) collective-permute-start(f32[4,72,512]{2,1,0:T(8,128)S(1)} %get-tuple-element.48), channel_id=1, source_target_pairs={{0,32},{32,0},{64,96},{96,64},{128,160},{160,128},{192,224},{224,1... | collective-permute-start | bytes 1769480 | tf_op jit(solution)/shard_map/ppermute | solution.py:471
  469.0 3.9 collective-permute-start.1
  469.1 5.7 %collective-permute-start.2 = (bf16[80,512]{1,0:T(8,128)(2,1)S(1)}, bf16[80,512]{1,0:T(8,128)(2,1)S(1)}, u32[]{:S(2)}, u32[]{:S(2)}) collective-permute-start(bf16[80,512]{1,0:T(8,128)(2,1)S(1)} %get-tuple-element.51), channel_id=1, source_target_pairs={{0,128},{32,160},{64,192},{96,224},{128,0},{160,32},{192,64},{224,... | collective-permute-start | bytes 245768 | tf_op jit(solution)/shard_map/ppermute | solution.py:471
  470.6 5.9 %collective-permute-start.3 = (bf16[80,512]{1,0:T(8,128)(2,1)S(1)}, bf16[80,512]{1,0:T(8,128)(2,1)S(1)}, u32[]{:S(2)}, u32[]{:S(2)}) collective-permute-start(bf16[80,512]{1,0:T(8,128)(2,1)S(1)} %get-tuple-element.52), channel_id=1, source_target_pairs={{0,192},{32,224},{64,128},{96,160},{128,64},{160,96},{192,0},{224,... | collective-permute-start | bytes 245768 | tf_op jit(solution)/shard_map/ppermute | solution.py:471
  476.6 5.2 %collective-permute-start.6 = (bf16[80,512]{1,0:T(8,128)(2,1)S(1)}, bf16[80,512]{1,0:T(8,128)(2,1)S(1)}, u32[]{:S(2)}, u32[]{:S(2)}) collective-permute-start(bf16[80,512]{1,0:T(8,128)(2,1)S(1)} %shard_map.115.refs_0_), channel_id=1, source_target_pairs={{0,192},{32,224},{64,128},{96,160},{128,64},{160,96},{192,0},{224,... | collective-permute-start | bytes 245768 | tf_op jit(solution)/shard_map/ppermute | solution.py:471
  479.0 4.8 collective-permute-start.5
  479.0 7.2 %collective-permute-start.4 = (bf16[80,512]{1,0:T(8,128)(2,1)S(1)}, bf16[80,512]{1,0:T(8,128)(2,1)S(1)}, u32[]{:S(2)}, u32[]{:S(2)}) collective-permute-start(bf16[80,512]{1,0:T(8,128)(2,1)S(1)} %shard_map.115.refs_0_), channel_id=1, source_target_pairs={{0,64},{32,96},{64,0},{96,32},{128,192},{160,224},{192,128},{224,1... | collective-permute-start | bytes 245768 | tf_op jit(solution)/shard_map/ppermute | solution.py:471
  479.9 6.9 %collective-permute-start.7 = (bf16[80,512]{1,0:T(8,128)(2,1)S(1)}, bf16[80,512]{1,0:T(8,128)(2,1)S(1)}, u32[]{:S(2)}, u32[]{:S(2)}) collective-permute-start(bf16[80,512]{1,0:T(8,128)(2,1)S(1)} %shard_map.115.refs_0_), channel_id=1, source_target_pairs={{0,32},{32,0},{64,96},{96,64},{128,160},{160,128},{192,224},{224,1... | collective-permute-start | bytes 245768 | tf_op jit(solution)/shard_map/ppermute | solution.py:471
  481.8 5.1 %collective-permute-start.10 = (bf16[80,512]{1,0:T(8,128)(2,1)S(1)}, bf16[80,512]{1,0:T(8,128)(2,1)S(1)}, u32[]{:S(2)}, u32[]{:S(2)}) collective-permute-start(bf16[80,512]{1,0:T(8,128)(2,1)S(1)} %collective-permute-done.6.refs_3_), channel_id=1, source_target_pairs={{0,32},{32,0},{64,96},{96,64},{128,160},{160,128},{192,224},{224,1... | collective-permute-start | bytes 245768 | tf_op jit(solution)/shard_map/ppermute | solution.py:471
  483.8 3.4 collective-permute-start.9
  486.3 1.3 collective-permute-start.8

commit v5 on v4

--- a/solution.py
+++ b/solution.py
@@ -12,9 +12,9 @@
 NEG = -1e30
 LOG2E = 1.4426950408889634
 TO2 = LOG2E / EPS
+PART = 256
 INNER = 8
 FLAT = (16, 256)
-SHARE = ((0, 1, 2), (3, 4, 5), (6, 7))
 LIMIT = 40 * 1024 * 1024
 F32, BF16 = jnp.float32, jnp.bfloat16
 
@@ -77,9 +77,9 @@
     return (other - scale * tile) / EPS
 
 
-def slow_lse(slots, cost_hbm, cost_v, sem, other8, out8, other_ref, l_ref, rows_mode):
+def slow_lse(slots, cost_hbm, cost_v, sem, other8, out8, other_ref, l_ref, rows_mode, start=0):
     l_ref[...] = jnp.full(l_ref.shape, NEG, F32)
-    chunks = out8.shape[0]
+    chunks, out_chunks = other8.shape[0], out8.shape[0]
     for s in range(slots.total):
         out_at, other_at = (slots.row[s], slots.col[s]) if rows_mode else (slots.col[s], slots.row[s])
 
@@ -90,11 +90,11 @@
             copy.wait()
             chunked(other_ref[pl.ds(other_at, 1), :], other8)
 
-            @pl.loop(0, chunks)
+            @pl.loop(0, out_chunks)
             def _(i):
                 def step(j, carry):
                     m, total = carry
-                    z = tile_z(cost_v, slots.scale[s], other8, i, j, rows_mode)
+                    z = tile_z(cost_v, slots.scale[s], other8, start + i, j, rows_mode)
                     top = jnp.maximum(m, jnp.max(z, axis=0, keepdims=True))
                     total = total * jnp.exp(m - top) + jnp.sum(jnp.exp(z - top), axis=0, keepdims=True)
                     return top, total
@@ -103,7 +103,7 @@
                 m, total = lax.fori_loop(0, chunks, step, first)
                 out8[pl.ds(i, 1), :] = m + jnp.log(total)
 
-            new = jnp.concatenate([out8[c : c + 1, :] for c in range(chunks)], axis=1)
+            new = jnp.concatenate([out8[c : c + 1, :] for c in range(out_chunks)], axis=1)
             old = l_ref[pl.ds(out_at, 1), :]
             top = jnp.maximum(old, new)
             l_ref[pl.ds(out_at, 1), :] = top + jnp.log(jnp.exp(old - top) + jnp.exp(new - top))
@@ -153,11 +153,40 @@
 
 
 def build_kernel(
-    dims, scale, row, col, count, log_a, log_b, cost_hbm,
+    dims, count, scale_hbm, row_hbm, col_hbm, a_hbm, b_hbm, cost_hbm,
     k_ref, copies_ref, ints, floats, a_ref, b_ref,
     l_ref, cost_v, sums, zero, other8, out8, stat, sems,
+    scale, row, col, log_a, log_b, small_sems, tall,
 ):
     rb, cb, total = dims
+    small = [
+        pltpu.make_async_copy(a, b, small_sems.at[i])
+        for i, (a, b) in enumerate(
+            ((scale_hbm, scale), (row_hbm, row), (col_hbm, col), (a_hbm, log_a), (b_hbm, log_b))
+        )
+    ]
+    parts = cost_v.shape[1] // PART
+    copies = [
+        [
+            pltpu.make_async_copy(
+                cost_hbm.at[0, s, pl.ds(h * PART, PART)], cost_v.at[s, pl.ds(h * PART, PART)], sems.at[s, h]
+            )
+            for h in range(parts)
+        ]
+        for s in range(total)
+    ]
+    copies[0][0].start()
+    for copy in small:
+        copy.start()
+    for s in range(total):
+
+        @pl.when(s < count[0, 0])
+        def _():
+            for h in range(0 if s else 1, parts):
+                copies[s][h].start()
+
+    for copy in small[:3]:
+        copy.wait()
     src, tgt = lax.axis_index("src"), lax.axis_index("tgt")
     for s in range(total):
         ints[0, s] = row[0, s] - src * rb
@@ -165,62 +194,52 @@
         floats[0, s] = scale[0, s]
     ints[0, 2 * total] = count[0, 0]
     slots = Slots(ints, floats, total)
-    half = cost_v.shape[1] // 2
-    copies = [
-        [
-            pltpu.make_async_copy(
-                cost_hbm.at[0, s, pl.ds(h * half, half)], cost_v.at[s, pl.ds(h * half, half)], sems.at[s, h]
-            )
-            for h in range(2)
-        ]
-        for s in range(total)
-    ]
-    for s in range(total):
-
-        @pl.when(slots.live[s])
-        def _():
-            for h in range(2):
-                copies[s][h].start()
-
-    tile = cost_v.shape[2]
+    chunk, tile = 32, cost_v.shape[2]
+
+    def build(shift, wait):
+        sums[...] = jnp.zeros(sums.shape, F32)
+        floats[0, total] = jnp.float32(0.0) if shift is None else shift
+        stat[1] = jnp.float32(0.0)
+        stat[2] = jnp.float32(jnp.inf)
+        for s in range(total):
+
+            @pl.when(slots.live[s])
+            def _():
+                for h in range(parts):
+                    if wait:
+                        copies[s][h].wait()
+
+                    @pl.loop(0, PART // chunk, unroll=2)
+                    def _(i):
+                        here = pl.ds(pl.multiple_of(h * PART + i * chunk, chunk), chunk)
+                        x = cost_v[s, here, :].astype(F32) * (-TO2 * slots.scale[s])
+                        if shift is not None:
+                            x = x + shift * TO2
+                        e = jnp.exp2(x)
+                        k_ref[s, here, :] = e.astype(BF16)
+                        tall[here, :] = tree_sum([e[:, c * 128 : (c + 1) * 128] for c in range(tile // 128)])
+
+                wide = tall[...]
+                hi = wide.astype(BF16)
+                low = (wide - hi.astype(F32)).astype(BF16)
+                ones = jnp.ones((16, 128), BF16)
+                part = (k_row(ones, hi) + k_row(ones, low))[0:1]
+                at = pl.ds(slots.row[s], 1)
+                sums[at, :] = sums[at, :] + part
+                stat[1] = jnp.maximum(stat[1], jnp.max(part))
+                stat[2] = jnp.minimum(stat[2], jnp.min(part))
+
+        l_ref[...] = to_log(sums[...], floats[0, total])
+        floats[0, total + 1] = stat[1]
+        return sums_fine(stat[2], stat[1], stat[1])
+
+    fine = build(None, True)
+    for copy in small[3:]:
+        copy.wait()
     for r in range(rb):
         a_ref[r : r + 1, :] = log_a[r * tile : (r + 1) * tile].reshape(1, tile)
     for c in range(cb):
         b_ref[c : c + 1, :] = log_b[c * tile : (c + 1) * tile].reshape(1, tile)
-    chunk = 32
-    ones = jnp.ones((16, cost_v.shape[2]), BF16)
-
-    def build(shift, wait):
-        sums[...] = jnp.zeros(sums.shape, F32)
-        floats[0, total] = shift
-        stat[1] = jnp.float32(0.0)
-        stat[2] = jnp.float32(jnp.inf)
-        for s in range(total):
-
-            @pl.when(slots.live[s])
-            def _():
-                for h in range(2):
-                    if wait:
-                        copies[s][h].wait()
-
-                    @pl.loop(0, half // chunk, unroll=2)
-                    def _(i):
-                        here = pl.ds(pl.multiple_of(h * half + i * chunk, chunk), chunk)
-                        x = cost_v[s, here, :].astype(F32)
-                        x = x * (-TO2 * slots.scale[s]) + shift * TO2
-                        k_ref[s, here, :] = jnp.exp2(x).astype(BF16)
-
-                part = k_row(ones, k_ref[s])[0:1]
-                at = pl.ds(slots.row[s], 1)
-                sums[at, :] = sums[at, :] + part
-                stat[1] = jnp.maximum(stat[1], jnp.max(part))
-                stat[2] = jnp.minimum(stat[2], jnp.min(part))
-
-        l_ref[...] = to_log(sums[...], shift)
-        floats[0, total + 1] = stat[1]
-        return sums_fine(stat[2], stat[1], stat[1])
-
-    fine = build(jnp.float32(0.0), True)
 
     @pl.when(jnp.logical_not(fine))
     def _():
@@ -233,7 +252,7 @@
                     here = pl.ds(pl.multiple_of(i * chunk, chunk), chunk)
                     return jnp.minimum(low, jnp.min(cost_v[s, here, :].astype(F32)))
 
-                low = lax.fori_loop(0, 2 * half // chunk, lowest, jnp.float32(jnp.inf))
+                low = lax.fori_loop(0, tile // chunk, lowest, jnp.float32(jnp.inf))
                 stat[0] = jnp.minimum(stat[0], low * slots.scale[s])
 
         shifted = build(stat[0], False)
@@ -246,9 +265,9 @@
     send_copies(l_ref, copies_ref)
 
 
-def row_kernel(total, first, with_labels, ints, floats, log_b, cost_hbm, k_ref, parts, log_a, f, *rest):
-    prev, rest = (None, rest) if first else (rest[0], rest[1:])
-    lab, rest = (rest[0], rest[1:]) if with_labels else (None, rest)
+def row_kernel(total, first, ints, floats, log_b, cost_hbm, k_ref, parts, log_a, f, *rest):
+    prev, lab = (None, rest[0]) if first else (rest[0], None)
+    rest = rest[1:]
     copies_ref, g, l_ref, flat, sums, stat, cost_v, other8, out8, sem = rest
     slots = Slots(ints, floats, total)
     new_potential(g, log_b, parts, prev, flat)
@@ -275,20 +294,20 @@
         slow_lse(slots, cost_hbm, cost_v, sem, other8, out8, g, l_ref, True)
 
     send_relative(l_ref, f, log_a, flat, copies_ref)
-    if with_labels:
+    if first:
         half = lab.shape[0] // 2
         for k in range(copies_ref.shape[0]):
             copies_ref[k, flat.shape[0] :] = jnp.concatenate([lab[:half], lab[half:]], axis=1)
 
 
-def relay_kernel(share, parts, lab, copies_ref):
-    rows = FLAT[0]
-    total = tree_sum([parts[k, :rows].astype(F32) for k in range(parts.shape[0])]).astype(BF16)
-    high = lab.shape[1] - rows
-    for k in range(copies_ref.shape[0]):
-        copies_ref[k, :rows] = total
-        for i, p in enumerate(share):
-            copies_ref[k, rows + i * high : rows + (i + 1) * high] = lab[p, rows:]
+def relay_kernel(parts, out):
+    rows, count = FLAT[0], parts.shape[0]
+    total = tree_sum([parts[k, :rows].astype(F32) for k in range(count)]).astype(BF16)
+    high = parts.shape[1] - rows
+    for k in range(out.shape[0]):
+        out[k, :rows] = total
+        for p in range(count):
+            out[k, rows + p * high : rows + (p + 1) * high] = parts[p, rows:]
 
 
 def col_kernel(total, first, ints, floats, log_a, cost_hbm, k_ref, parts, *rest):
@@ -324,35 +343,37 @@
         send_relative(l_ref, g, log_b, flat, copies_ref)
 
 
-def label_kernel(total, ints, floats, log_a, cost_hbm, k_ref, prev, *rest):
-    boxes, rest = rest[: len(SHARE)], rest[len(SHARE) :]
-    f_out, keep, send, acc, l_ref, flat, lab_v, sums, stat, cost_v, other8, out8, sem = rest
+def label_kernel(total, own, ints, floats, log_a, cost_hbm, k_ref, prev, parts, box, *rest):
+    (f_out,), rest = (rest[:1], rest[1:]) if own else ((None,), rest)
+    out, f, row, acc, l_ref, flat, lab_v, sums, stat, cost_v, other8, out8, sem = rest
     slots = Slots(ints, floats, total)
-    classes = acc.shape[1]
-    new_potential(f_out, log_a, boxes[-1], prev, flat)
+    classes, width = acc.shape[1], acc.shape[2]
+    new_potential(f, log_a, parts, prev, flat)
     sums[...] = jnp.zeros(sums.shape, F32)
     acc[...] = jnp.zeros(acc.shape, F32)
     stat[0] = jnp.float32(0.0)
     stat[1] = jnp.float32(jnp.inf)
     stat[2] = slots.high
     high = classes // 2
+    core = slots.src % 2
+    half = core if own else 1 - core
+    lanes = pl.ds(pl.multiple_of(half * width, width), width)
 
     def label_piece(block, p):
-        box = [i for i, share in enumerate(SHARE) if p in share][0]
-        at = FLAT[0] + SHARE[box].index(p) * high
-        both = boxes[box][block, at : at + high]
+        at = FLAT[0] + p * high
+        both = box[block, at : at + high]
         return jnp.concatenate([both[:, :128], both[:, 128:]], axis=0)
 
     for s in range(slots.total):
 
         @pl.when(slots.live[s])
         def _():
-            u = jnp.exp2(f_out[pl.ds(slots.row[s], 1), :] * TO2)
+            u = jnp.exp2(f[pl.ds(slots.row[s], 1), :] * TO2)
             lab = jnp.concatenate([label_piece(slots.row[s], p) for p in range(INNER)], axis=1)
             weighted = lab.astype(F32) * u
             hi = weighted.astype(BF16)
             low = (weighted - hi.astype(F32)).astype(BF16)
-            res = k_col(jnp.concatenate([hi, low, split_rows(u)], axis=0), k_ref[s])
+            res = k_col(jnp.concatenate([hi, low, split_rows(u)], axis=0), k_ref[s, :, lanes])
             part = jnp.sum(res[2 * classes :], axis=0, keepdims=True)
             at = pl.ds(slots.col[s], 1)
             sums[at, :] = sums[at, :] + part
@@ -365,10 +386,10 @@
 
     @pl.when(jnp.logical_not(sums_fine(stat[1], stat[0], stat[2])))
     def _():
-        slow_lse(slots, cost_hbm, cost_v, sem, other8, out8, f_out, l_ref, False)
+        chunks = width // 128
+        slow_lse(slots, cost_hbm, cost_v, sem, other8, out8, f, l_ref, False, half * chunks)
         acc[...] = jnp.zeros(acc.shape, F32)
         sums[...] = jnp.ones(sums.shape, F32)
-        chunks = cost_v.shape[0] // 128
         for s in range(slots.total):
 
             @pl.when(slots.live[s])
@@ -376,39 +397,28 @@
                 copy = pltpu.make_async_copy(cost_hbm.at[0, s], cost_v, sem)
                 copy.start()
                 copy.wait()
-                chunked(f_out[pl.ds(slots.row[s], 1), :], other8)
+                chunked(f[pl.ds(slots.row[s], 1), :], other8)
                 chunked(l_ref[pl.ds(slots.col[s], 1), :], out8)
                 for p in range(INNER):
                     lab_v[p] = label_piece(slots.row[s], p)
 
-                @pl.loop(0, chunks * chunks)
+                @pl.loop(0, chunks * INNER)
                 def _(ij):
-                    i, j = ij // chunks, ij % chunks
+                    i, j = ij // INNER, ij % INNER
                     here = pl.ds(pl.multiple_of(i * 128, 128), 128)
-                    z = tile_z(cost_v, slots.scale[s], other8, i, j, False)
+                    z = tile_z(cost_v, slots.scale[s], other8, half * chunks + i, j, False)
                     p = jnp.exp(z - out8[pl.ds(i, 1), :]).astype(BF16)
                     term = jnp.dot(lab_v[j], p, preferred_element_type=F32)
                     acc[slots.col[s], :, here] = acc[slots.col[s], :, here] + term
 
-    core = slots.src % 2
-    width = keep.shape[2]
     for c in range(acc.shape[0]):
-        total = sums[c : c + 1, :]
-        inv = jnp.where(total > 0, 1.0 / jnp.maximum(total, 1e-38), 0.0)
-        for half in range(2):
-            here = slice(half * width, (half + 1) * width)
-            mean = acc[c, :, here] * inv[:, here]
-            tail = jnp.broadcast_to(l_ref[c : c + 1, here], (8, width))
-
-            @pl.when(core == half)
-            def _():
-                keep[c, :classes] = mean
-                keep[c, classes:] = tail
-
-            @pl.when(core != half)
-            def _():
-                send[c, :classes] = mean
-                send[c, classes:] = tail
+        mass = sums[c : c + 1, :]
+        out[c, :classes] = acc[c] * jnp.where(mass > 0, 1.0 / jnp.maximum(mass, 1e-38), 0.0)
+        out[c, classes:] = jnp.broadcast_to(l_ref[c : c + 1, :], (8, width))
+    if own:
+        for r in range(f.shape[0]):
+            row[:, r * f.shape[1] : (r + 1) * f.shape[1]] = f[r : r + 1, :]
+        f_out[...] = row[...].reshape(f_out.shape)
 
 
 def merge_kernel(keep, got, *outs):
@@ -500,7 +510,7 @@
             pltpu.VMEM((rb, tile), F32),
             pltpu.VMEM((cb, tile), F32),
         ),
-        in_specs=[SM] * 4 + [VM] * 2 + [HB],
+        in_specs=[SM] + [HB] * 6,
         out_specs=(VM, VM, SM, SM, VM, VM),
         scratch_shapes=[
             rows,
@@ -510,14 +520,21 @@
             chunks,
             chunks,
             pltpu.SMEM((3,), F32),
-            pltpu.SemaphoreType.DMA((slots, 2)),
+            pltpu.SemaphoreType.DMA((slots, tile // PART)),
+            pltpu.SMEM((1, slots), F32),
+            pltpu.SMEM((1, slots), jnp.int32),
+            pltpu.SMEM((1, slots), jnp.int32),
+            pltpu.VMEM((rb * tile,), F32),
+            pltpu.VMEM((cb * tile,), F32),
+            pltpu.SemaphoreType.DMA((5,)),
+            pltpu.VMEM((tile, 128), F32),
         ],
         compiler_params=PARAMS,
     )(
+        device_block_count,
         in_hbm(cost_scale),
         in_hbm(slot_block_row),
         in_hbm(slot_block_column),
-        device_block_count,
         in_hbm(log_a),
         in_hbm(log_b),
         cost,
@@ -528,27 +545,27 @@
 
     flat = pltpu.VMEM(FLAT, F32)
     sent = functools.partial(jax.ShapeDtypeStruct, dtype=BF16)
-    lab_t, boxes = labels.T, []
-    f_pot = g_pot = lab_z = None
+    lab_t = labels.T
+    f_pot = g_pot = box = None
     for step in range(ITERS):
-        along = everyone(row_l, "tgt", along_z)
-        if step == 0:
-            part = lse([along[z] for z in range(INNER)])
-            copies = jnp.broadcast_to(part[None], (outer,) + part.shape)
+        if step < 2:
+            along = everyone(row_l, "tgt", along_z)
+            if step == 0:
+                part = lse([along[z] for z in range(INNER)])
+                copies = jnp.broadcast_to(part[None], (outer,) + part.shape)
+            else:
+                high = FLAT[0] + INNER * (along.shape[1] - FLAT[0])
+                copies = pl.pallas_call(
+                    relay_kernel,
+                    out_shape=sent((outer, high, FLAT[1])),
+                    in_specs=[VM],
+                    out_specs=VM,
+                    compiler_params=PARAMS,
+                )(along)
+            row_parts = everyone(copies, "tgt", along_x)
+            box = row_parts if step else None
         else:
-            lab_z = along if step == 1 else lab_z
-            share = SHARE[step - 1]
-            high = FLAT[0] + len(share) * (lab_z.shape[1] - FLAT[0])
-            copies = pl.pallas_call(
-                functools.partial(relay_kernel, share),
-                out_shape=sent((outer, high, FLAT[1])),
-                in_specs=[VM] * 2,
-                out_specs=VM,
-                compiler_params=PARAMS,
-            )(along, lab_z)
-        row_parts = everyone(copies, "tgt", along_x)
-        if step:
-            boxes.append(row_parts)
+            row_parts = everyone(row_l, "tgt")
         if step == ITERS - 1:
             break
         first = step == 0
@@ -562,32 +579,47 @@
         )(*scalars, log_a, cost, k_all, row_parts, *(() if first else (f_pot, log_b, g_pot)))
         col_parts = everyone(col_l, "src")
         extra = FLAT[0] * lab_t.size // (FLAT[0] * FLAT[1]) if first else 0
-        row_l, g_pot = pl.pallas_call(
-            functools.partial(row_kernel, slots, first, first),
-            out_shape=(sent((INNER, FLAT[0] + extra, FLAT[1])), vec((cb, tile))),
+        last = step == ITERS - 2
+        row_l, *g_out = pl.pallas_call(
+            functools.partial(row_kernel, slots, first),
+            out_shape=(sent((INNER if first else n_tgt, FLAT[0] + extra, FLAT[1])), vec((cb, tile)))[: 1 if last else 2],
             in_specs=common + [VM] * 4,
-            out_specs=(VM, VM),
-            scratch_shapes=[rows, flat, rows] + work,
+            out_specs=(VM, VM)[: 1 if last else 2],
+            scratch_shapes=[cols] * last + [rows, flat, rows] + work,
             compiler_params=PARAMS,
         )(*scalars, log_b, cost, k_all, col_parts, log_a, f_pot, lab_t if first else g_pot)
+        g_pot = g_out[0] if g_out else None
 
     width = cb * tile // n_src
+    piece = jax.ShapeDtypeStruct((classes + 16, width), BF16)
     half = vec((cb, classes + 8, width))
-    piece = jax.ShapeDtypeStruct((classes + 16, width), BF16)
-    f_pot, keep, send = pl.pallas_call(
-        functools.partial(label_kernel, slots),
-        out_shape=(vec((rb, tile)), half, half),
-        in_specs=common + [VM] * (1 + len(SHARE)),
-        out_specs=(VM,) * 3,
-        scratch_shapes=[
-            pltpu.VMEM((cb, classes, tile), F32),
-            cols,
-            flat,
-            pltpu.VMEM((INNER, classes, 128), BF16),
-            cols,
-        ] + work,
-        compiler_params=PARAMS,
-    )(*scalars, log_a, cost, k_all, f_pot, *boxes)
+    half_cols = pltpu.VMEM((cb, width), F32)
+
+    def label_call(own):
+        return pl.pallas_call(
+            functools.partial(label_kernel, slots, own),
+            out_shape=((vec((rb * tile,)),) if own else ()) + (half,),
+            in_specs=common + [VM] * 3,
+            out_specs=(VM,) * (1 + own),
+            scratch_shapes=[
+                rows,
+                pltpu.VMEM((1, rb * tile), F32),
+                pltpu.VMEM((cb, classes, width), F32),
+                half_cols,
+                flat,
+                pltpu.VMEM((INNER, classes, 128), BF16),
+                half_cols,
+            ]
+            + work[:3]
+            + [pltpu.VMEM((width // 128, 128), F32), work[4]],
+            cost_estimate=pl.CostEstimate(
+                flops=slots * tile * tile * 150, bytes_accessed=slots * tile * tile, transcendentals=slots * tile
+            ),
+            compiler_params=PARAMS,
+        )(*scalars, log_a, cost, k_all, f_pot, row_parts, box)
+
+    got = xor(label_call(False)[0], "src", 1)
+    f_pot, keep = label_call(True)
     n_y = n_src // 2
     pieces = pl.pallas_call(
         merge_kernel,
@@ -595,7 +627,7 @@
         in_specs=[VM] * 2,
         out_specs=(VM,) * n_y,
         compiler_params=PARAMS,
-    )(keep, xor(send, "src", 1))
+    )(keep, got)
     pieces = [pieces[0]] + [xor(pieces[q], "src", 2 * q) for q in range(1, n_y)]
     done = pl.pallas_call(
         combine_kernel,
@@ -615,7 +647,7 @@
         scratch_shapes=[pltpu.VMEM((1, cb * tile), F32)],
         compiler_params=PARAMS,
     )(*pieces)
-    return f_pot.reshape(-1), g_pot, out.T
+    return f_pot, g_pot, out.T
 
 
 def solution(mesh):

time: 490 us -> 493 us (level)
  the two profiles are of different devices: /device:TPU:33 before, /device:TPU:1 now
where the time goes in v5:
time: 493 us; the launch traced here: 486 us
  Pallas kernels  362 us (73%)
  blocking collectives  107 us (22%)
  starting transfers between devices  8.5 us (2%)
  waiting for transfers between devices  7.08 us (1%)
    pallas_call x3, Pallas kernels, local(): pl.pallas_call(functools.partial(row_kernel, slots, first), out_shape=(se...  108 us
    all_to_all x9, blocking collectives, everyone(): lax.all_to_all(copies, axis, 0, 0, axis_index_groups=groups, tiled=True)  107 us
    pallas_call x3, Pallas kernels, local(): pl.pallas_call(functools.partial(col_kernel, slots, first), out_shape=(ve...  103 us
    pallas_call x2, Pallas kernels, label_call(): pl.pallas_call(functools.partial(label_kernel, slots, own), out_shape=((v...  95.1 us
    pallas_call x1, Pallas kernels, local(): pl.pallas_call(functools.partial(build_kernel, dims), out_shape=(pltpu.VM...  54.6 us
  transfers between devices with their start and end apart: 11, of which 5 were waited for; matrix products, arithmetic and copies ran while one was open for 0% of the time, Pallas kernels for 10%

profile of v5, /device:TPU:1, one launch (start us, length us, event | category | flops | bytes accessed | tf_op | source)
XLA Modules:
  0.0 485.7 jit_solution(13982822632430413128)
XLA Ops:
  1.3 54.6 %shard_map.103 = (bf16[3,1024,1024]{2,1,0:T(8,128)(2,1)S(1)}, f32[8,4,1024]{2,1,0:T(4,128)S(1)}, s32[1,7]{1,0:T(1,128)S(4)}, f32[1,5]{1,0:T(1,128)S(4)}, f32[4,1024]{1,0:T(4,128)S(1)}, /*index=5*/f32[4,1024]{1,0:T(4,128)S(1)}) custom-call(s32[1,1]{1,0:T(1,128)S(6)} %copy.11.count, f32[1,3]{1,0:T(1,128)} %scale_hbm.1, s32[1,3]{1,0:T(1,128)} %row_hbm.1, ...), custom_call_target="tpu_custom_call" | custom-call | tf_op jit(solution)/shard_map/pallas_call | solution.py:503
  55.9 10.3 %all_to_all.45 = f32[8,4,1024]{2,1,0:T(4,128)S(1)} all-to-all(f32[8,4,1024]{2,1,0:T(4,128)S(1)} %get-tuple-element.32), channel_id=1, replica_groups={{0,1,2,3,4,5,6,7},{8,9,10,11,12,13,14,15},{16,17,18,19,20,21,22,23},{24..., dimensions={0} | all-to-all | bytes 262144 | tf_op jit(solution)/shard_map/all_to_all | solution.py:495
  66.3 15.0 %all_to_all.46.parts = f32[4,4,1024]{2,1,0:T(4,128)S(1)} all-to-all(f32[4,4,1024]{2,1,0:T(4,128)S(1)} %broadcast_in_dim.9), channel_id=1, replica_groups={{0,8,16,24},{1,9,17,25},{2,10,18,26},{3,11,19,27},{4,12,20,28},{5,13,21..., dimensions={0} | all-to-all | bytes 131072 | tf_op jit(solution)/shard_map/all_to_all | solution.py:495
  81.3 34.5 %shard_map.104 = (f32[8,4,1024]{2,1,0:T(4,128)S(1)}, f32[4,1024]{1,0:T(4,128)S(1)}) custom-call(s32[1,7]{1,0:T(1,128)S(4)} %get-tuple-element.27.ints, f32[1,5]{1,0:T(1,128)S(4)} %get-tuple-element.28.floats, f32[4,1024]{1,0:T(4,128)S(1)} %get-tuple-element.29.log_a, bf16[1,3,1024,1024]{3,2,1,0:T(8,128)(2,1)} %cost_hbm.17, ...), custom_call_target="tpu_custom_call" | custom-call | tf_op jit(solution)/shard_map/pallas_call | solution.py:572
  115.8 9.0 %all_to_all.47.parts = f32[8,4,1024]{2,1,0:T(4,128)S(1)} all-to-all(f32[8,4,1024]{2,1,0:T(4,128)S(1)} %get-tuple-element.33), channel_id=1, replica_groups=mesh['src'=8,'tgt'=32] {'src'}, dimensions={0} | all-to-all | bytes 262144 | tf_op jit(solution)/shard_map/all_to_all | solution.py:495
  124.8 35.8 %shard_map.105 = (bf16[8,48,256]{2,1,0:T(8,128)(2,1)S(1)}, f32[4,1024]{1,0:T(4,128)S(1)}) custom-call(s32[1,7]{1,0:T(1,128)S(4)} %get-tuple-element.27.ints, f32[1,5]{1,0:T(1,128)S(4)} %get-tuple-element.28.floats, f32[4,1024]{1,0:T(4,128)S(1)} %get-tuple-element.31.log_b.rest_1_, bf16[1,3,1024,1024]{3,2,1,0:T(8,128)(2,1)} %cost_hbm.17, ...), custom_call_target="tpu_custom_call" | custom-call | tf_op jit(solution)/shard_map/pallas_call | solution.py:583
  160.6 11.0 %all_to_all.48.parts = bf16[8,48,256]{2,1,0:T(8,128)(2,1)S(1)} all-to-all(bf16[8,48,256]{2,1,0:T(8,128)(2,1)S(1)} %get-tuple-element.35), channel_id=1, replica_groups={{0,1,2,3,4,5,6,7},{8,9,10,11,12,13,14,15},{16,17,18,19,20,21,22,23},{24..., dimensions={0} | all-to-all | bytes 393216 | tf_op jit(solution)/shard_map/all_to_all | solution.py:495
  171.7 15.1 %all_to_all.49.parts.box = bf16[4,272,256]{2,1,0:T(8,128)(2,1)S(1)} all-to-all(bf16[4,272,256]{2,1,0:T(8,128)(2,1)S(1)} %shard_map.106), channel_id=1, replica_groups={{0,8,16,24},{1,9,17,25},{2,10,18,26},{3,11,19,27},{4,12,20,28},{5,13,21..., dimensions={0} | all-to-all | bytes 1114112 | tf_op jit(solution)/shard_map/all_to_all | solution.py:495
  186.8 34.5 %shard_map.107 = (bf16[8,16,256]{2,1,0:T(8,128)(2,1)S(1)}, f32[4,1024]{1,0:T(4,128)S(1)}) custom-call(s32[1,7]{1,0:T(1,128)S(4)} %get-tuple-element.27.ints, f32[1,5]{1,0:T(1,128)S(4)} %get-tuple-element.28.floats, f32[4,1024]{1,0:T(4,128)S(1)} %get-tuple-element.29.log_a, bf16[1,3,1024,1024]{3,2,1,0:T(8,128)(2,1)} %cost_hbm.17, ...), custom_call_target="tpu_custom_call" | custom-call | tf_op jit(solution)/shard_map/pallas_call | solution.py:572
  221.3 8.9 %all_to_all.50.parts = bf16[8,16,256]{2,1,0:T(8,128)(2,1)S(1)} all-to-all(bf16[8,16,256]{2,1,0:T(8,128)(2,1)S(1)} %get-tuple-element.37), channel_id=1, replica_groups=mesh['src'=8,'tgt'=32] {'src'}, dimensions={0} | all-to-all | bytes 131072 | tf_op jit(solution)/shard_map/all_to_all | solution.py:495
  230.2 35.8 %shard_map.108 = (bf16[32,16,256]{2,1,0:T(8,128)(2,1)S(1)}, f32[4,1024]{1,0:T(4,128)S(1)}) custom-call(s32[1,7]{1,0:T(1,128)S(4)} %get-tuple-element.27.ints, f32[1,5]{1,0:T(1,128)S(4)} %get-tuple-element.28.floats, f32[4,1024]{1,0:T(4,128)S(1)} %get-tuple-element.31.log_b.rest_1_, bf16[1,3,1024,1024]{3,2,1,0:T(8,128)(2,1)} %cost_hbm.17, ...), custom_call_target="tpu_custom_call" | custom-call | tf_op jit(solution)/shard_map/pallas_call | solution.py:583
  266.0 12.8 %all_to_all.51.parts = bf16[32,16,256]{2,1,0:T(8,128)(2,1)S(1)} all-to-all(bf16[32,16,256]{2,1,0:T(8,128)(2,1)S(1)} %get-tuple-element.39), channel_id=1, replica_groups=mesh['src'=8,'tgt'=32] {'tgt'}, dimensions={0} | all-to-all | bytes 524288 | tf_op jit(solution)/shard_map/all_to_all | solution.py:495
  278.8 34.5 %shard_map.109 = (bf16[8,16,256]{2,1,0:T(8,128)(2,1)S(1)}, f32[4,1024]{1,0:T(4,128)S(1)}) custom-call(s32[1,7]{1,0:T(1,128)S(4)} %get-tuple-element.27.ints, f32[1,5]{1,0:T(1,128)S(4)} %get-tuple-element.28.floats, f32[4,1024]{1,0:T(4,128)S(1)} %get-tuple-element.29.log_a, bf16[1,3,1024,1024]{3,2,1,0:T(8,128)(2,1)} %cost_hbm.17, ...), custom_call_target="tpu_custom_call" | custom-call | tf_op jit(solution)/shard_map/pallas_call | solution.py:572
  313.3 6.9 %all_to_all.52.parts = bf16[8,16,256]{2,1,0:T(8,128)(2,1)S(1)} all-to-all(bf16[8,16,256]{2,1,0:T(8,128)(2,1)S(1)} %get-tuple-element.42), channel_id=1, replica_groups=mesh['src'=8,'tgt'=32] {'src'}, dimensions={0} | all-to-all | bytes 131072 | tf_op jit(solution)/shard_map/all_to_all | solution.py:495
  320.2 36.0 %shard_map.110 = bf16[32,16,256]{2,1,0:T(8,128)(2,1)S(1)} custom-call(s32[1,7]{1,0:T(1,128)S(4)} %get-tuple-element.27.ints, f32[1,5]{1,0:T(1,128)S(4)} %get-tuple-element.28.floats, f32[4,1024]{1,0:T(4,128)S(1)} %get-tuple-element.31.log_b.rest_1_, bf16[1,3,1024,1024]{3,2,1,0:T(8,128)(2,1)} %cost_hbm.17, ...), custom_call_target="tpu_custom_call" | custom-call | tf_op jit(solution)/shard_map/pallas_call | solution.py:583
  356.2 17.5 %all_to_all.53.parts = bf16[32,16,256]{2,1,0:T(8,128)(2,1)S(1)} all-to-all(bf16[32,16,256]{2,1,0:T(8,128)(2,1)S(1)} %shard_map.110), channel_id=1, replica_groups=mesh['src'=8,'tgt'=32] {'tgt'}, dimensions={0} | all-to-all | bytes 524288 | tf_op jit(solution)/shard_map/all_to_all | solution.py:495
  373.8 47.3 %shard_map.112 = f32[4,72,512]{2,1,0:T(8,128)S(1)} custom-call(s32[1,7]{1,0:T(1,128)S(4)} %get-tuple-element.27.ints, f32[1,5]{1,0:T(1,128)S(4)} %get-tuple-element.28.floats, f32[4,1024]{1,0:T(4,128)S(1)} %get-tuple-element.29.log_a, bf16[1,3,1024,1024]{3,2,1,0:T(8,128)(2,1)} %cost_hbm.17, bf16[3,1024,1024]{2,1,0:T(8,128)(2,1)S(1)} %get-tuple-element.30.k_ref, ...), custom_call_target="tpu_custom_call" | custom-call | flops 471859200 | bytes 3145728 | tf_op jit(solution)/shard_map/pallas_call | solution.py:599
  421.2 47.8 %shard_map.111 = (f32[4096]{0:T(1024)}, f32[4,72,512]{2,1,0:T(8,128)S(1)}) custom-call(s32[1,7]{1,0:T(1,128)S(4)} %get-tuple-element.27.ints, f32[1,5]{1,0:T(1,128)S(4)} %get-tuple-element.28.floats, f32[4,1024]{1,0:T(4,128)S(1)} %get-tuple-element.29.log_a, bf16[1,3,1024,1024]{3,2,1,0:T(8,128)(2,1)} %cost_hbm.17, ...), custom_call_target="tpu_custom_call" | custom-call | flops 471859200 | bytes 3145728 | tf_op jit(solution)/shard_map/pallas_call | solution.py:599
  469.0 0.2 shard_map.113
  469.2 0.4 collective-permute-start.1
  469.6 0.4 collective-permute-start.2
  470.0 3.2 collective-permute-start.3
  473.1 1.3 collective-permute-done.2.rest_2_
  474.4 0.8 collective-permute-done.3.rest_3_
  475.4 0.4 collective-permute-start.4
  475.8 3.3 collective-permute-start.5
  479.0 0.3 collective-permute-start.6
  479.3 0.5 collective-permute-start.8
  479.9 1.9 collective-permute-done.5.refs_2_
  481.7 1.8 collective-permute-done.6.refs_3_
  483.6 1.3 collective-permute-done.10.refs_7_
  484.8 0.8 shard_map.115
  (16 shorter events, 0.4 us)
Async XLA Ops:
  81.3 43.5 %copy-start = (bf16[128,64]{0,1:T(8,128)(2,1)S(1)}, bf16[128,64]{0,1:T(8,128)(2,1)}, u32[]{:S(2)}) copy-start(bf16[128,64]{0,1:T(8,128)(2,1)} %param.15) | copy-start | bytes 49156
  421.1 48.0 %collective-permute-start = (f32[4,72,512]{2,1,0:T(8,128)S(1)}, f32[4,72,512]{2,1,0:T(8,128)S(1)}, u32[]{:S(2)}, u32[]{:S(2)}) collective-permute-start(f32[4,72,512]{2,1,0:T(8,128)S(1)} %shard_map.112), channel_id=1, source_target_pairs={{0,32},{32,0},{64,96},{96,64},{128,160},{160,128},{192,224},{224,1... | collective-permute-start | bytes 1769480 | tf_op jit(solution)/shard_map/ppermute | solution.py:481
  469.2 3.9 collective-permute-start.1
  469.6 4.8 collective-permute-start.2
  470.0 5.3 %collective-permute-start.3 = (bf16[80,512]{1,0:T(8,128)(2,1)S(1)}, bf16[80,512]{1,0:T(8,128)(2,1)S(1)}, u32[]{:S(2)}, u32[]{:S(2)}) collective-permute-start(bf16[80,512]{1,0:T(8,128)(2,1)S(1)} %get-tuple-element.48), channel_id=1, source_target_pairs={{0,192},{32,224},{64,128},{96,160},{128,64},{160,96},{192,0},{224,... | collective-permute-start | bytes 245768 | tf_op jit(solution)/shard_map/ppermute | solution.py:481
  475.4 4.0 collective-permute-start.4
  475.8 6.0 %collective-permute-start.5 = (bf16[80,512]{1,0:T(8,128)(2,1)S(1)}, bf16[80,512]{1,0:T(8,128)(2,1)S(1)}, u32[]{:S(2)}, u32[]{:S(2)}) collective-permute-start(bf16[80,512]{1,0:T(8,128)(2,1)S(1)} %shard_map.114.refs_0_), channel_id=1, source_target_pairs={{0,128},{32,160},{64,192},{96,224},{128,0},{160,32},{192,64},{224,... | collective-permute-start | bytes 245768 | tf_op jit(solution)/shard_map/ppermute | solution.py:481
  479.0 4.5 collective-permute-start.6
  479.3 4.2 collective-permute-start.7
  479.3 4.2 collective-permute-start.8
  481.7 1.8 collective-permute-start.9
  483.5 1.3 collective-permute-start.10

commit v6 on v5

--- a/solution.py
+++ b/solution.py
@@ -55,6 +55,18 @@
 
 def k_row(lhs, k_block):
     return lax.dot_general(lhs, k_block, (((1,), (1,)), ((), ())), preferred_element_type=F32)
+
+
+def fold_lanes(x):
+    return tree_sum([x[:, c * 128 : (c + 1) * 128] for c in range(x.shape[1] // 128)])
+
+
+def fold_rows(tall):
+    wide = tall[...]
+    hi = wide.astype(BF16)
+    low = (wide - hi.astype(F32)).astype(BF16)
+    ones = jnp.ones((16, 128), BF16)
+    return (k_row(ones, hi) + k_row(ones, low))[0:1]
 
 
 def k_col(lhs, k_block):
@@ -217,13 +229,9 @@
                             x = x + shift * TO2
                         e = jnp.exp2(x)
                         k_ref[s, here, :] = e.astype(BF16)
-                        tall[here, :] = tree_sum([e[:, c * 128 : (c + 1) * 128] for c in range(tile // 128)])
-
-                wide = tall[...]
-                hi = wide.astype(BF16)
-                low = (wide - hi.astype(F32)).astype(BF16)
-                ones = jnp.ones((16, 128), BF16)
-                part = (k_row(ones, hi) + k_row(ones, low))[0:1]
+                        tall[here, :] = fold_lanes(e)
+
+                part = fold_rows(tall)
                 at = pl.ds(slots.row[s], 1)
                 sums[at, :] = sums[at, :] + part
                 stat[1] = jnp.maximum(stat[1], jnp.max(part))
@@ -268,7 +276,7 @@
 def row_kernel(total, first, ints, floats, log_b, cost_hbm, k_ref, parts, log_a, f, *rest):
     prev, lab = (None, rest[0]) if first else (rest[0], None)
     rest = rest[1:]
-    copies_ref, g, l_ref, flat, sums, stat, cost_v, other8, out8, sem = rest
+    copies_ref, g, l_ref, flat, tall, sums, stat, cost_v, other8, out8, sem = rest
     slots = Slots(ints, floats, total)
     new_potential(g, log_b, parts, prev, flat)
     sums[...] = jnp.zeros(sums.shape, F32)
@@ -280,7 +288,13 @@
         @pl.when(slots.live[s])
         def _():
             v = jnp.exp2(g[pl.ds(slots.col[s], 1), :] * TO2)
-            part = jnp.sum(k_row(split_rows(v), k_ref[s]), axis=0, keepdims=True)
+
+            @pl.loop(0, tall.shape[0] // 32, unroll=2)
+            def _(i):
+                here = pl.ds(pl.multiple_of(i * 32, 32), 32)
+                tall[here, :] = fold_lanes(k_ref[s, here, :].astype(F32) * v)
+
+            part = fold_rows(tall)
             at = pl.ds(slots.row[s], 1)
             sums[at, :] = sums[at, :] + part
             stat[0] = jnp.maximum(stat[0], jnp.max(part))
@@ -344,8 +358,8 @@
 
 
 def label_kernel(total, own, ints, floats, log_a, cost_hbm, k_ref, prev, parts, box, *rest):
-    (f_out,), rest = (rest[:1], rest[1:]) if own else ((None,), rest)
-    out, f, row, acc, l_ref, flat, lab_v, sums, stat, cost_v, other8, out8, sem = rest
+    (f, out), rest = (rest[:2] if own else rest[1::-1]), rest[2:]
+    acc, l_ref, flat, lab_v, sums, stat, cost_v, other8, out8, sem = rest
     slots = Slots(ints, floats, total)
     classes, width = acc.shape[1], acc.shape[2]
     new_potential(f, log_a, parts, prev, flat)
@@ -415,10 +429,6 @@
         mass = sums[c : c + 1, :]
         out[c, :classes] = acc[c] * jnp.where(mass > 0, 1.0 / jnp.maximum(mass, 1e-38), 0.0)
         out[c, classes:] = jnp.broadcast_to(l_ref[c : c + 1, :], (8, width))
-    if own:
-        for r in range(f.shape[0]):
-            row[:, r * f.shape[1] : (r + 1) * f.shape[1]] = f[r : r + 1, :]
-        f_out[...] = row[...].reshape(f_out.shape)
 
 
 def merge_kernel(keep, got, *outs):
@@ -585,7 +595,7 @@
             out_shape=(sent((INNER if first else n_tgt, FLAT[0] + extra, FLAT[1])), vec((cb, tile)))[: 1 if last else 2],
             in_specs=common + [VM] * 4,
             out_specs=(VM, VM)[: 1 if last else 2],
-            scratch_shapes=[cols] * last + [rows, flat, rows] + work,
+            scratch_shapes=[cols] * last + [rows, flat, pltpu.VMEM((tile, 128), F32), rows] + work,
             compiler_params=PARAMS,
         )(*scalars, log_b, cost, k_all, col_parts, log_a, f_pot, lab_t if first else g_pot)
         g_pot = g_out[0] if g_out else None
@@ -598,12 +608,11 @@
     def label_call(own):
         return pl.pallas_call(
             functools.partial(label_kernel, slots, own),
-            out_shape=((vec((rb * tile,)),) if own else ()) + (half,),
+            out_shape=(vec((rb, tile)), half) if own else (half,),
             in_specs=common + [VM] * 3,
             out_specs=(VM,) * (1 + own),
-            scratch_shapes=[
-                rows,
-                pltpu.VMEM((1, rb * tile), F32),
+            scratch_shapes=[rows] * (not own)
+            + [
                 pltpu.VMEM((cb, classes, width), F32),
                 half_cols,
                 flat,
@@ -647,7 +656,7 @@
         scratch_shapes=[pltpu.VMEM((1, cb * tile), F32)],
         compiler_params=PARAMS,
     )(*pieces)
-    return f_pot, g_pot, out.T
+    return f_pot.reshape(-1), g_pot, out.T
 
 
 def solution(mesh):

time: 493 us -> 492 us (level); the launches traced: 486 us -> 491 us
  starting transfers between devices: 8.5 us -> 14.2 us
    ppermute x11, starting transfers between devices: 8.5 us -> 14.2 us  [xor(): lax.ppermute(x, axis, [(i, i ^ k) for i in range(lax.axis_size(axis))])]
  transfers between devices with their start and end apart: 11 -> 11, of which waited for: 5 -> 3; matrix products, arithmetic and copies ran while one was open for 0% -> 0% of each run, Pallas kernels for 10% -> 10%
where the time goes in v6:
time: 492 us; the launch traced here: 491 us
  Pallas kernels  362 us (74%)
  blocking collectives  106 us (22%)
  starting transfers between devices  14.2 us (3%)
  waiting for transfers between devices  6.48 us (1%)
    pallas_call x3, Pallas kernels, local(): pl.pallas_call(functools.partial(row_kernel, slots, first), out_shape=(se...  108 us
    all_to_all x9, blocking collectives, everyone(): lax.all_to_all(copies, axis, 0, 0, axis_index_groups=groups, tiled=True)  106 us
    pallas_call x3, Pallas kernels, local(): pl.pallas_call(functools.partial(col_kernel, slots, first), out_shape=(ve...  103 us
    pallas_call x2, Pallas kernels, label_call(): pl.pallas_call(functools.partial(label_kernel, slots, own), out_shape=(ve...  94.7 us
    pallas_call x1, Pallas kernels, local(): pl.pallas_call(functools.partial(build_kernel, dims), out_shape=(pltpu.VM...  54.6 us
    ppermute x11, starting transfers between devices, xor(): lax.ppermute(x, axis, [(i, i ^ k) for i in range(lax.axis_size(axis))])  14.2 us
  transfers between devices with their start and end apart: 11, of which 3 were waited for; matrix products, arithmetic and copies ran while one was open for 0% of the time, Pallas kernels for 10%

profile of v6, /device:TPU:1, one launch (start us, length us, event | category | flops | bytes accessed | tf_op | source)
XLA Modules:
  0.0 490.8 jit_solution(6702549063449063798)
XLA Ops:
  1.3 54.6 %shard_map.103 = (bf16[3,1024,1024]{2,1,0:T(8,128)(2,1)S(1)}, f32[8,4,1024]{2,1,0:T(4,128)S(1)}, s32[1,7]{1,0:T(1,128)S(4)}, f32[1,5]{1,0:T(1,128)S(4)}, f32[4,1024]{1,0:T(4,128)S(1)}, /*index=5*/f32[4,1024]{1,0:T(4,128)S(1)}) custom-call(s32[1,1]{1,0:T(1,128)S(6)} %copy.14.count, f32[1,3]{1,0:T(1,128)} %scale_hbm.1, s32[1,3]{1,0:T(1,128)} %row_hbm.1, ...), custom_call_target="tpu_custom_call" | custom-call | tf_op jit(solution)/shard_map/pallas_call | solution.py:513
  55.9 17.0 %all_to_all.45 = f32[8,4,1024]{2,1,0:T(4,128)S(1)} all-to-all(f32[8,4,1024]{2,1,0:T(4,128)S(1)} %get-tuple-element.32), channel_id=1, replica_groups={{0,1,2,3,4,5,6,7},{8,9,10,11,12,13,14,15},{16,17,18,19,20,21,22,23},{24..., dimensions={0} | all-to-all | bytes 262144 | tf_op jit(solution)/shard_map/all_to_all | solution.py:505
  73.0 7.1 %all_to_all.46.parts = f32[4,4,1024]{2,1,0:T(4,128)S(1)} all-to-all(f32[4,4,1024]{2,1,0:T(4,128)S(1)} %broadcast_in_dim.9), channel_id=1, replica_groups={{0,8,16,24},{1,9,17,25},{2,10,18,26},{3,11,19,27},{4,12,20,28},{5,13,21..., dimensions={0} | all-to-all | bytes 131072 | tf_op jit(solution)/shard_map/all_to_all | solution.py:505
  80.1 34.5 %shard_map.104 = (f32[8,4,1024]{2,1,0:T(4,128)S(1)}, f32[4,1024]{1,0:T(4,128)S(1)}) custom-call(s32[1,7]{1,0:T(1,128)S(4)} %get-tuple-element.27.ints, f32[1,5]{1,0:T(1,128)S(4)} %get-tuple-element.28.floats, f32[4,1024]{1,0:T(4,128)S(1)} %get-tuple-element.29.log_a, bf16[1,3,1024,1024]{3,2,1,0:T(8,128)(2,1)} %cost_hbm.17, ...), custom_call_target="tpu_custom_call" | custom-call | tf_op jit(solution)/shard_map/pallas_call | solution.py:582
  114.6 12.0 %all_to_all.47.parts = f32[8,4,1024]{2,1,0:T(4,128)S(1)} all-to-all(f32[8,4,1024]{2,1,0:T(4,128)S(1)} %get-tuple-element.33), channel_id=1, replica_groups=mesh['src'=8,'tgt'=32] {'src'}, dimensions={0} | all-to-all | bytes 262144 | tf_op jit(solution)/shard_map/all_to_all | solution.py:505
  126.6 36.1 %shard_map.105 = (bf16[8,48,256]{2,1,0:T(8,128)(2,1)S(1)}, f32[4,1024]{1,0:T(4,128)S(1)}) custom-call(s32[1,7]{1,0:T(1,128)S(4)} %get-tuple-element.27.ints, f32[1,5]{1,0:T(1,128)S(4)} %get-tuple-element.28.floats, f32[4,1024]{1,0:T(4,128)S(1)} %get-tuple-element.31.log_b.rest_1_, bf16[1,3,1024,1024]{3,2,1,0:T(8,128)(2,1)} %cost_hbm.17, ...), custom_call_target="tpu_custom_call" | custom-call | tf_op jit(solution)/shard_map/pallas_call | solution.py:593
  162.7 13.3 %all_to_all.48.parts = bf16[8,48,256]{2,1,0:T(8,128)(2,1)S(1)} all-to-all(bf16[8,48,256]{2,1,0:T(8,128)(2,1)S(1)} %get-tuple-element.35), channel_id=1, replica_groups={{0,1,2,3,4,5,6,7},{8,9,10,11,12,13,14,15},{16,17,18,19,20,21,22,23},{24..., dimensions={0} | all-to-all | bytes 393216 | tf_op jit(solution)/shard_map/all_to_all | solution.py:505
  176.0 11.8 %all_to_all.49.parts.box = bf16[4,272,256]{2,1,0:T(8,128)(2,1)S(1)} all-to-all(bf16[4,272,256]{2,1,0:T(8,128)(2,1)S(1)} %shard_map.106), channel_id=1, replica_groups={{0,8,16,24},{1,9,17,25},{2,10,18,26},{3,11,19,27},{4,12,20,28},{5,13,21..., dimensions={0} | all-to-all | bytes 1114112 | tf_op jit(solution)/shard_map/all_to_all | solution.py:505
  187.8 34.5 %shard_map.107 = (bf16[8,16,256]{2,1,0:T(8,128)(2,1)S(1)}, f32[4,1024]{1,0:T(4,128)S(1)}) custom-call(s32[1,7]{1,0:T(1,128)S(4)} %get-tuple-element.27.ints, f32[1,5]{1,0:T(1,128)S(4)} %get-tuple-element.28.floats, f32[4,1024]{1,0:T(4,128)S(1)} %get-tuple-element.29.log_a, bf16[1,3,1024,1024]{3,2,1,0:T(8,128)(2,1)} %cost_hbm.17, ...), custom_call_target="tpu_custom_call" | custom-call | tf_op jit(solution)/shard_map/pallas_call | solution.py:582
  222.3 7.7 %all_to_all.50.parts = bf16[8,16,256]{2,1,0:T(8,128)(2,1)S(1)} all-to-all(bf16[8,16,256]{2,1,0:T(8,128)(2,1)S(1)} %get-tuple-element.37), channel_id=1, replica_groups=mesh['src'=8,'tgt'=32] {'src'}, dimensions={0} | all-to-all | bytes 131072 | tf_op jit(solution)/shard_map/all_to_all | solution.py:505
  230.0 36.1 %shard_map.108 = (bf16[32,16,256]{2,1,0:T(8,128)(2,1)S(1)}, f32[4,1024]{1,0:T(4,128)S(1)}) custom-call(s32[1,7]{1,0:T(1,128)S(4)} %get-tuple-element.27.ints, f32[1,5]{1,0:T(1,128)S(4)} %get-tuple-element.28.floats, f32[4,1024]{1,0:T(4,128)S(1)} %get-tuple-element.31.log_b.rest_1_, bf16[1,3,1024,1024]{3,2,1,0:T(8,128)(2,1)} %cost_hbm.17, ...), custom_call_target="tpu_custom_call" | custom-call | tf_op jit(solution)/shard_map/pallas_call | solution.py:593
  266.1 12.7 %all_to_all.51.parts = bf16[32,16,256]{2,1,0:T(8,128)(2,1)S(1)} all-to-all(bf16[32,16,256]{2,1,0:T(8,128)(2,1)S(1)} %get-tuple-element.39), channel_id=1, replica_groups=mesh['src'=8,'tgt'=32] {'tgt'}, dimensions={0} | all-to-all | bytes 524288 | tf_op jit(solution)/shard_map/all_to_all | solution.py:505
  278.8 34.5 %shard_map.109 = (bf16[8,16,256]{2,1,0:T(8,128)(2,1)S(1)}, f32[4,1024]{1,0:T(4,128)S(1)}) custom-call(s32[1,7]{1,0:T(1,128)S(4)} %get-tuple-element.27.ints, f32[1,5]{1,0:T(1,128)S(4)} %get-tuple-element.28.floats, f32[4,1024]{1,0:T(4,128)S(1)} %get-tuple-element.29.log_a, bf16[1,3,1024,1024]{3,2,1,0:T(8,128)(2,1)} %cost_hbm.17, ...), custom_call_target="tpu_custom_call" | custom-call | tf_op jit(solution)/shard_map/pallas_call | solution.py:582
  313.3 10.6 %all_to_all.52.parts = bf16[8,16,256]{2,1,0:T(8,128)(2,1)S(1)} all-to-all(bf16[8,16,256]{2,1,0:T(8,128)(2,1)S(1)} %get-tuple-element.42), channel_id=1, replica_groups=mesh['src'=8,'tgt'=32] {'src'}, dimensions={0} | all-to-all | bytes 131072 | tf_op jit(solution)/shard_map/all_to_all | solution.py:505
  323.8 36.1 %shard_map.110 = bf16[32,16,256]{2,1,0:T(8,128)(2,1)S(1)} custom-call(s32[1,7]{1,0:T(1,128)S(4)} %get-tuple-element.27.ints, f32[1,5]{1,0:T(1,128)S(4)} %get-tuple-element.28.floats, f32[4,1024]{1,0:T(4,128)S(1)} %get-tuple-element.31.log_b.rest_1_, bf16[1,3,1024,1024]{3,2,1,0:T(8,128)(2,1)} %cost_hbm.17, ...), custom_call_target="tpu_custom_call" | custom-call | tf_op jit(solution)/shard_map/pallas_call | solution.py:593
  360.0 13.6 %all_to_all.53.parts = bf16[32,16,256]{2,1,0:T(8,128)(2,1)S(1)} all-to-all(bf16[32,16,256]{2,1,0:T(8,128)(2,1)S(1)} %shard_map.110), channel_id=1, replica_groups=mesh['src'=8,'tgt'=32] {'tgt'}, dimensions={0} | all-to-all | bytes 524288 | tf_op jit(solution)/shard_map/all_to_all | solution.py:505
  373.5 47.5 %shard_map.112 = f32[4,72,512]{2,1,0:T(8,128)S(1)} custom-call(s32[1,7]{1,0:T(1,128)S(4)} %get-tuple-element.27.ints, f32[1,5]{1,0:T(1,128)S(4)} %get-tuple-element.28.floats, f32[4,1024]{1,0:T(4,128)S(1)} %get-tuple-element.29.log_a, bf16[1,3,1024,1024]{3,2,1,0:T(8,128)(2,1)} %cost_hbm.17, bf16[3,1024,1024]{2,1,0:T(8,128)(2,1)S(1)} %get-tuple-element.30.k_ref, ...), custom_call_target="tpu_custom_call" | custom-call | flops 471859200 | bytes 3145728 | tf_op jit(solution)/shard_map/pallas_call | solution.py:609
  421.1 47.3 %shard_map.111 = (f32[4,1024]{1,0:T(4,128)S(1)}, f32[4,72,512]{2,1,0:T(8,128)S(1)}) custom-call(s32[1,7]{1,0:T(1,128)S(4)} %get-tuple-element.27.ints, f32[1,5]{1,0:T(1,128)S(4)} %get-tuple-element.28.floats, f32[4,1024]{1,0:T(4,128)S(1)} %get-tuple-element.29.log_a, bf16[1,3,1024,1024]{3,2,1,0:T(8,128)(2,1)} %cost_hbm.17, ...), custom_call_target="tpu_custom_call" | custom-call | flops 471859200 | bytes 3145728 | tf_op jit(solution)/shard_map/pallas_call | solution.py:609
  468.7 4.7 collective-permute-start.2
  473.4 0.2 collective-permute-start.3
  473.6 4.3 collective-permute-done.2.rest_2_
  477.9 1.9 collective-permute-done.3.rest_3_
  479.9 0.2 collective-permute-start.4
  480.1 2.0 collective-permute-start.5
  482.1 1.8 collective-permute-start.6
  483.8 1.3 collective-permute-start.7
  485.1 0.6 collective-permute-start.8
  485.7 1.8 collective-permute-start.9
  487.5 1.6 collective-permute-start.10
  489.0 0.6 copy.13
  489.6 0.3 collective-permute-done.10.refs_7_
  490.0 0.8 shard_map.115
  (17 shorter events, 0.6 us)
Async XLA Ops:
  80.1 46.5 %copy-start = (bf16[128,64]{0,1:T(8,128)(2,1)S(1)}, bf16[128,64]{0,1:T(8,128)(2,1)}, u32[]{:S(2)}) copy-start(bf16[128,64]{0,1:T(8,128)(2,1)} %param.15) | copy-start | bytes 49156
  421.0 47.4 %collective-permute-start = (f32[4,72,512]{2,1,0:T(8,128)S(1)}, f32[4,72,512]{2,1,0:T(8,128)S(1)}, u32[]{:S(2)}, u32[]{:S(2)}) collective-permute-start(f32[4,72,512]{2,1,0:T(8,128)S(1)} %shard_map.112), channel_id=1, source_target_pairs={{0,32},{32,0},{64,96},{96,64},{128,160},{160,128},{192,224},{224,1... | collective-permute-start | bytes 1769480 | tf_op jit(solution)/shard_map/ppermute | solution.py:491
  468.6 5.0 %collective-permute-start.1 = (bf16[80,512]{1,0:T(8,128)(2,1)S(1)}, bf16[80,512]{1,0:T(8,128)(2,1)S(1)}, u32[]{:S(2)}, u32[]{:S(2)}) collective-permute-start(bf16[80,512]{1,0:T(8,128)(2,1)S(1)} %get-tuple-element.46), channel_id=1, source_target_pairs={{0,64},{32,96},{64,0},{96,32},{128,192},{160,224},{192,128},{224,1... | collective-permute-start | bytes 245768 | tf_op jit(solution)/shard_map/ppermute | solution.py:491
  468.7 9.2 %collective-permute-start.2 = (bf16[80,512]{1,0:T(8,128)(2,1)S(1)}, bf16[80,512]{1,0:T(8,128)(2,1)S(1)}, u32[]{:S(2)}, u32[]{:S(2)}) collective-permute-start(bf16[80,512]{1,0:T(8,128)(2,1)S(1)} %get-tuple-element.47), channel_id=1, source_target_pairs={{0,128},{32,160},{64,192},{96,224},{128,0},{160,32},{192,64},{224,... | collective-permute-start | bytes 245768 | tf_op jit(solution)/shard_map/ppermute | solution.py:491
  473.4 6.3 %collective-permute-start.3 = (bf16[80,512]{1,0:T(8,128)(2,1)S(1)}, bf16[80,512]{1,0:T(8,128)(2,1)S(1)}, u32[]{:S(2)}, u32[]{:S(2)}) collective-permute-start(bf16[80,512]{1,0:T(8,128)(2,1)S(1)} %get-tuple-element.48), channel_id=1, source_target_pairs={{0,192},{32,224},{64,128},{96,160},{128,64},{160,96},{192,0},{224,... | collective-permute-start | bytes 245768 | tf_op jit(solution)/shard_map/ppermute | solution.py:491
  479.9 5.3 %collective-permute-start.4 = (bf16[80,512]{1,0:T(8,128)(2,1)S(1)}, bf16[80,512]{1,0:T(8,128)(2,1)S(1)}, u32[]{:S(2)}, u32[]{:S(2)}) collective-permute-start(bf16[80,512]{1,0:T(8,128)(2,1)S(1)} %shard_map.114.refs_0_), channel_id=1, source_target_pairs={{0,64},{32,96},{64,0},{96,32},{128,192},{160,224},{192,128},{224,1... | collective-permute-start | bytes 245768 | tf_op jit(solution)/shard_map/ppermute | solution.py:491
  480.1 5.6 %collective-permute-start.5 = (bf16[80,512]{1,0:T(8,128)(2,1)S(1)}, bf16[80,512]{1,0:T(8,128)(2,1)S(1)}, u32[]{:S(2)}, u32[]{:S(2)}) collective-permute-start(bf16[80,512]{1,0:T(8,128)(2,1)S(1)} %shard_map.114.refs_0_), channel_id=1, source_target_pairs={{0,128},{32,160},{64,192},{96,224},{128,0},{160,32},{192,64},{224,... | collective-permute-start | bytes 245768 | tf_op jit(solution)/shard_map/ppermute | solution.py:491
  482.1 5.4 %collective-permute-start.6 = (bf16[80,512]{1,0:T(8,128)(2,1)S(1)}, bf16[80,512]{1,0:T(8,128)(2,1)S(1)}, u32[]{:S(2)}, u32[]{:S(2)}) collective-permute-start(bf16[80,512]{1,0:T(8,128)(2,1)S(1)} %shard_map.114.refs_0_), channel_id=1, source_target_pairs={{0,192},{32,224},{64,128},{96,160},{128,64},{160,96},{192,0},{224,... | collective-permute-start | bytes 245768 | tf_op jit(solution)/shard_map/ppermute | solution.py:491
  483.8 5.8 %collective-permute-start.7 = (bf16[80,512]{1,0:T(8,128)(2,1)S(1)}, bf16[80,512]{1,0:T(8,128)(2,1)S(1)}, u32[]{:S(2)}, u32[]{:S(2)}) collective-permute-start(bf16[80,512]{1,0:T(8,128)(2,1)S(1)} %shard_map.114.refs_0_), channel_id=1, source_target_pairs={{0,32},{32,0},{64,96},{96,64},{128,160},{160,128},{192,224},{224,1... | collective-permute-start | bytes 245768 | tf_op jit(solution)/shard_map/ppermute | solution.py:491
  485.1 4.5 collective-permute-start.8
  485.7 3.9 collective-permute-start.9
  487.5 2.5 collective-permute-start.10

commit v7 on v6

--- a/solution.py
+++ b/solution.py
@@ -14,6 +14,7 @@
 TO2 = LOG2E / EPS
 PART = 256
 INNER = 8
+MIDDLE = 116.0
 FLAT = (16, 256)
 LIMIT = 40 * 1024 * 1024
 F32, BF16 = jnp.float32, jnp.bfloat16
@@ -139,25 +140,35 @@
         copies_ref[k] = l_ref[...]
 
 
+def send_flat(x, flat, copies_ref):
+    count, width = x.shape[0], flat.shape[1]
+    for c in range(x.shape[1] // width):
+        flat[c * count : (c + 1) * count, :] = x[:, c * width : (c + 1) * width]
+    x = flat[...].astype(BF16)
+    for k in range(copies_ref.shape[0]):
+        copies_ref[k, : flat.shape[0]] = x
+
+
 def send_relative(l_ref, pot, log_mass, flat, copies_ref):
-    rel = jnp.exp(l_ref[...] + pot[...] / EPS - log_mass[...])
-    count, width = rel.shape[0], flat.shape[1]
-    for c in range(rel.shape[1] // width):
-        flat[c * count : (c + 1) * count, :] = rel[:, c * width : (c + 1) * width]
-    rel = flat[...].astype(BF16)
-    for k in range(copies_ref.shape[0]):
-        copies_ref[k, : flat.shape[0]] = rel
+    send_flat(jnp.exp(l_ref[...] + pot[...] / EPS - log_mass[...]), flat, copies_ref)
 
 
 def new_potential(out, log_mass, parts, prev, flat):
-    if prev is None:
+    if parts.dtype == F32:
         out[...] = EPS * log_mass[...] - EPS * lse([parts[k] for k in range(parts.shape[0])])
         return
-    flat[...] = tree_sum([parts[k, : flat.shape[0]].astype(F32) for k in range(parts.shape[0])])
+    parts = [parts[k, : flat.shape[0]].astype(F32) for k in range(parts.shape[0])]
+    if prev is None:
+        top = functools.reduce(jnp.maximum, parts)
+        inv = 1.0 / top
+        flat[...] = MIDDLE + 2.0 * jnp.log(top) + jnp.log(tree_sum([(p * inv) * (p * inv) for p in parts]))
+    else:
+        flat[...] = jnp.log(tree_sum(parts))
     count, width = out.shape[0], flat.shape[1]
     for c in range(out.shape[1] // width):
         here = slice(c * width, (c + 1) * width)
-        out[:, here] = prev[:, here] - EPS * jnp.log(flat[c * count : (c + 1) * count, :])
+        base = EPS * log_mass[:, here] if prev is None else prev[:, here]
+        out[:, here] = base - EPS * flat[c * count : (c + 1) * count, :]
 
 
 def sums_fine(low, high, others):
@@ -168,7 +179,7 @@
     dims, count, scale_hbm, row_hbm, col_hbm, a_hbm, b_hbm, cost_hbm,
     k_ref, copies_ref, ints, floats, a_ref, b_ref,
     l_ref, cost_v, sums, zero, other8, out8, stat, sems,
-    scale, row, col, log_a, log_b, small_sems, tall,
+    scale, row, col, log_a, log_b, small_sems, tall, flat,
 ):
     rb, cb, total = dims
     small = [
@@ -270,13 +281,13 @@
             zero[...] = jnp.zeros(zero.shape, F32)
             slow_lse(slots, cost_hbm, cost_v.at[0], sems.at[0, 0], other8, out8, zero, l_ref, True)
 
-    send_copies(l_ref, copies_ref)
+    send_flat(jnp.exp((l_ref[...] - MIDDLE) / 2), flat, copies_ref)
 
 
 def row_kernel(total, first, ints, floats, log_b, cost_hbm, k_ref, parts, log_a, f, *rest):
     prev, lab = (None, rest[0]) if first else (rest[0], None)
     rest = rest[1:]
-    copies_ref, g, l_ref, flat, tall, sums, stat, cost_v, other8, out8, sem = rest
+    copies_ref, g, l_ref, flat, sums, stat, cost_v, other8, out8, sem = rest
     slots = Slots(ints, floats, total)
     new_potential(g, log_b, parts, prev, flat)
     sums[...] = jnp.zeros(sums.shape, F32)
@@ -288,13 +299,7 @@
         @pl.when(slots.live[s])
         def _():
             v = jnp.exp2(g[pl.ds(slots.col[s], 1), :] * TO2)
-
-            @pl.loop(0, tall.shape[0] // 32, unroll=2)
-            def _(i):
-                here = pl.ds(pl.multiple_of(i * 32, 32), 32)
-                tall[here, :] = fold_lanes(k_ref[s, here, :].astype(F32) * v)
-
-            part = fold_rows(tall)
+            part = jnp.sum(k_row(split_rows(v), k_ref[s]), axis=0, keepdims=True)
             at = pl.ds(slots.row[s], 1)
             sums[at, :] = sums[at, :] + part
             stat[0] = jnp.maximum(stat[0], jnp.max(part))
@@ -506,6 +511,7 @@
 
     cost = in_hbm(cost)
     vec = functools.partial(jax.ShapeDtypeStruct, dtype=F32)
+    sent = functools.partial(jax.ShapeDtypeStruct, dtype=BF16)
     chunks = pltpu.VMEM((tile // 128, 128), F32)
     work = [pltpu.SMEM((3,), F32), pltpu.VMEM((tile, tile), BF16), chunks, chunks, pltpu.SemaphoreType.DMA]
     rows, cols = pltpu.VMEM((rb, tile), F32), pltpu.VMEM((cb, tile), F32)
@@ -514,7 +520,7 @@
         functools.partial(build_kernel, dims),
         out_shape=(
             pltpu.VMEM((slots, tile, tile), BF16),
-            vec((INNER, rb, tile)),
+            sent((n_tgt,) + FLAT),
             pltpu.SMEM((1, 2 * slots + 1), jnp.int32),
             pltpu.SMEM((1, slots + 2), F32),
             pltpu.VMEM((rb, tile), F32),
@@ -538,6 +544,7 @@
             pltpu.VMEM((cb * tile,), F32),
             pltpu.SemaphoreType.DMA((5,)),
             pltpu.VMEM((tile, 128), F32),
+            pltpu.VMEM(FLAT, F32),
         ],
         compiler_params=PARAMS,
     )(
@@ -554,26 +561,20 @@
     common = [SM] * 2 + [VM, HB, VM]
 
     flat = pltpu.VMEM(FLAT, F32)
-    sent = functools.partial(jax.ShapeDtypeStruct, dtype=BF16)
     lab_t = labels.T
     f_pot = g_pot = box = None
     for step in range(ITERS):
-        if step < 2:
+        if step == 1:
             along = everyone(row_l, "tgt", along_z)
-            if step == 0:
-                part = lse([along[z] for z in range(INNER)])
-                copies = jnp.broadcast_to(part[None], (outer,) + part.shape)
-            else:
-                high = FLAT[0] + INNER * (along.shape[1] - FLAT[0])
-                copies = pl.pallas_call(
-                    relay_kernel,
-                    out_shape=sent((outer, high, FLAT[1])),
-                    in_specs=[VM],
-                    out_specs=VM,
-                    compiler_params=PARAMS,
-                )(along)
-            row_parts = everyone(copies, "tgt", along_x)
-            box = row_parts if step else None
+            high = FLAT[0] + INNER * (along.shape[1] - FLAT[0])
+            copies = pl.pallas_call(
+                relay_kernel,
+                out_shape=sent((outer, high, FLAT[1])),
+                in_specs=[VM],
+                out_specs=VM,
+                compiler_params=PARAMS,
+            )(along)
+            row_parts = box = everyone(copies, "tgt", along_x)
         else:
             row_parts = everyone(row_l, "tgt")
         if step == ITERS - 1:
@@ -595,7 +596,7 @@
             out_shape=(sent((INNER if first else n_tgt, FLAT[0] + extra, FLAT[1])), vec((cb, tile)))[: 1 if last else 2],
             in_specs=common + [VM] * 4,
             out_specs=(VM, VM)[: 1 if last else 2],
-            scratch_shapes=[cols] * last + [rows, flat, pltpu.VMEM((tile, 128), F32), rows] + work,
+            scratch_shapes=[cols] * last + [rows, flat, rows] + work,
             compiler_params=PARAMS,
         )(*scalars, log_b, cost, k_all, col_parts, log_a, f_pot, lab_t if first else g_pot)
         g_pot = g_out[0] if g_out else None

time: 492 us -> 489 us (level); the launches traced: 491 us -> 481 us
  Pallas kernels: 362 us -> 242 us
  blocking collectives: 106 us -> 191 us
  starting transfers between devices: 14.2 us -> 39.1 us
    all_to_all x9 -> x8, blocking collectives: 106 us -> 191 us  [everyone(): lax.all_to_all(copies, axis, 0, 0, axis_index_groups=groups, tiled=True)]
    pallas_call x3, Pallas kernels: 108 us -> 71.9 us  [local(): pl.pallas_call(functools.partial(row_kernel, slots, first), out_shape=(se...]
    pallas_call x3, Pallas kernels: 103 us -> 69.2 us  [local(): pl.pallas_call(functools.partial(col_kernel, slots, first), out_shape=(ve...]
    pallas_call x2, Pallas kernels: 94.7 us -> 63.1 us  [label_call(): pl.pallas_call(functools.partial(label_kernel, slots, own), out_shape=(ve...]
    ppermute x11, starting transfers between devices: 14.2 us -> 39.1 us  [xor(): lax.ppermute(x, axis, [(i, i ^ k) for i in range(lax.axis_size(axis))])]
    pallas_call x1, Pallas kernels: 54.6 us -> 36.8 us  [local(): pl.pallas_call(functools.partial(build_kernel, dims), out_shape=(pltpu.VM...]
  transfers between devices with their start and end apart: 11 -> 11, of which waited for: 3 -> 5; matrix products, arithmetic and copies ran while one was open for 0% -> 0% of each run, Pallas kernels for 10% -> 7%
where the time goes in v7:
time: 489 us; the launch traced here: 481 us
  Pallas kernels  242 us (49%)
  blocking collectives  191 us (39%)
  starting transfers between devices  39.1 us (8%)
  waiting for transfers between devices  6.48 us (1%)
    all_to_all x8, blocking collectives, everyone(): lax.all_to_all(copies, axis, 0, 0, axis_index_groups=groups, tiled=True)  191 us
    pallas_call x3, Pallas kernels, local(): pl.pallas_call(functools.partial(row_kernel, slots, first), out_shape=(se...  71.9 us
    pallas_call x3, Pallas kernels, local(): pl.pallas_call(functools.partial(col_kernel, slots, first), out_shape=(ve...  69.2 us
    pallas_call x2, Pallas kernels, label_call(): pl.pallas_call(functools.partial(label_kernel, slots, own), out_shape=(ve...  63.1 us
    ppermute x11, starting transfers between devices, xor(): lax.ppermute(x, axis, [(i, i ^ k) for i in range(lax.axis_size(axis))])  39.1 us
    pallas_call x1, Pallas kernels, local(): pl.pallas_call(functools.partial(build_kernel, dims), out_shape=(pltpu.VM...  36.8 us
  transfers between devices with their start and end apart: 11, of which 5 were waited for; matrix products, arithmetic and copies ran while one was open for 0% of the time, Pallas kernels for 7%

profile of v7, /device:TPU:1, one launch (start us, length us, event | category | flops | bytes accessed | tf_op | source)
XLA Modules:
  0.0 481.2 jit_solution(11527281977557354378)
XLA Ops:
  1.3 36.8 %shard_map.103 = (bf16[3,1024,1024]{2,1,0:T(8,128)(2,1)S(1)}, bf16[32,16,256]{2,1,0:T(8,128)(2,1)S(1)}, s32[1,7]{1,0:T(1,128)S(4)}, f32[1,5]{1,0:T(1,128)S(4)}, ...) custom-call(s32[1,1]{1,0:T(1,128)S(6)} %copy.14.count, f32[1,3]{1,0:T(1,128)} %scale_hbm.1, s32[1,3]{1,0:T(1,128)} %row_hbm.1, ...), custom_call_target="tpu_custom_call" | custom-call | tf_op jit(solution)/shard_map/pallas_call | solution.py:519
  38.1 37.9 %all_to_all.40.parts = bf16[32,16,256]{2,1,0:T(8,128)(2,1)S(1)} all-to-all(bf16[32,16,256]{2,1,0:T(8,128)(2,1)S(1)} %get-tuple-element.32), channel_id=1, replica_groups=mesh['src'=8,'tgt'=32] {'tgt'}, dimensions={0} | all-to-all | bytes 524288 | tf_op jit(solution)/shard_map/all_to_all | solution.py:510
  76.1 23.1 %shard_map.104 = (f32[8,4,1024]{2,1,0:T(4,128)S(1)}, f32[4,1024]{1,0:T(4,128)S(1)}) custom-call(s32[1,7]{1,0:T(1,128)S(4)} %get-tuple-element.27.ints, f32[1,5]{1,0:T(1,128)S(4)} %get-tuple-element.28.floats, f32[4,1024]{1,0:T(4,128)S(1)} %get-tuple-element.29.log_a, bf16[1,3,1024,1024]{3,2,1,0:T(8,128)(2,1)} %cost_hbm.17, ...), custom_call_target="tpu_custom_call" | custom-call | tf_op jit(solution)/shard_map/pallas_call | solution.py:583
  99.2 22.7 %all_to_all.41.parts = f32[8,4,1024]{2,1,0:T(4,128)S(1)} all-to-all(f32[8,4,1024]{2,1,0:T(4,128)S(1)} %get-tuple-element.33), channel_id=1, replica_groups=mesh['src'=8,'tgt'=32] {'src'}, dimensions={0} | all-to-all | bytes 262144 | tf_op jit(solution)/shard_map/all_to_all | solution.py:510
  121.9 23.9 %shard_map.105 = (bf16[8,48,256]{2,1,0:T(8,128)(2,1)S(1)}, f32[4,1024]{1,0:T(4,128)S(1)}) custom-call(s32[1,7]{1,0:T(1,128)S(4)} %get-tuple-element.27.ints, f32[1,5]{1,0:T(1,128)S(4)} %get-tuple-element.28.floats, f32[4,1024]{1,0:T(4,128)S(1)} %get-tuple-element.31.log_b.rest_1_, bf16[1,3,1024,1024]{3,2,1,0:T(8,128)(2,1)} %cost_hbm.17, ...), custom_call_target="tpu_custom_call" | custom-call | tf_op jit(solution)/shard_map/pallas_call | solution.py:594
  145.8 24.0 %all_to_all.42.parts = bf16[8,48,256]{2,1,0:T(8,128)(2,1)S(1)} all-to-all(bf16[8,48,256]{2,1,0:T(8,128)(2,1)S(1)} %get-tuple-element.35), channel_id=1, replica_groups={{0,1,2,3,4,5,6,7},{8,9,10,11,12,13,14,15},{16,17,18,19,20,21,22,23},{24..., dimensions={0} | all-to-all | bytes 393216 | tf_op jit(solution)/shard_map/all_to_all | solution.py:510
  169.9 10.7 %all_to_all.43.parts.box = bf16[4,272,256]{2,1,0:T(8,128)(2,1)S(1)} all-to-all(bf16[4,272,256]{2,1,0:T(8,128)(2,1)S(1)} %shard_map.106), channel_id=1, replica_groups={{0,8,16,24},{1,9,17,25},{2,10,18,26},{3,11,19,27},{4,12,20,28},{5,13,21..., dimensions={0} | all-to-all | bytes 1114112 | tf_op jit(solution)/shard_map/all_to_all | solution.py:510
  180.6 23.0 %shard_map.107 = (bf16[8,16,256]{2,1,0:T(8,128)(2,1)S(1)}, f32[4,1024]{1,0:T(4,128)S(1)}) custom-call(s32[1,7]{1,0:T(1,128)S(4)} %get-tuple-element.27.ints, f32[1,5]{1,0:T(1,128)S(4)} %get-tuple-element.28.floats, f32[4,1024]{1,0:T(4,128)S(1)} %get-tuple-element.29.log_a, bf16[1,3,1024,1024]{3,2,1,0:T(8,128)(2,1)} %cost_hbm.17, ...), custom_call_target="tpu_custom_call" | custom-call | tf_op jit(solution)/shard_map/pallas_call | solution.py:583
  203.6 19.3 %all_to_all.44.parts = bf16[8,16,256]{2,1,0:T(8,128)(2,1)S(1)} all-to-all(bf16[8,16,256]{2,1,0:T(8,128)(2,1)S(1)} %get-tuple-element.37), channel_id=1, replica_groups=mesh['src'=8,'tgt'=32] {'src'}, dimensions={0} | all-to-all | bytes 131072 | tf_op jit(solution)/shard_map/all_to_all | solution.py:510
  223.0 23.9 %shard_map.108 = (bf16[32,16,256]{2,1,0:T(8,128)(2,1)S(1)}, f32[4,1024]{1,0:T(4,128)S(1)}) custom-call(s32[1,7]{1,0:T(1,128)S(4)} %get-tuple-element.27.ints, f32[1,5]{1,0:T(1,128)S(4)} %get-tuple-element.28.floats, f32[4,1024]{1,0:T(4,128)S(1)} %get-tuple-element.31.log_b.rest_1_, bf16[1,3,1024,1024]{3,2,1,0:T(8,128)(2,1)} %cost_hbm.17, ...), custom_call_target="tpu_custom_call" | custom-call | tf_op jit(solution)/shard_map/pallas_call | solution.py:594
  246.9 28.9 %all_to_all.45.parts = bf16[32,16,256]{2,1,0:T(8,128)(2,1)S(1)} all-to-all(bf16[32,16,256]{2,1,0:T(8,128)(2,1)S(1)} %get-tuple-element.39), channel_id=1, replica_groups=mesh['src'=8,'tgt'=32] {'tgt'}, dimensions={0} | all-to-all | bytes 524288 | tf_op jit(solution)/shard_map/all_to_all | solution.py:510
  275.8 23.1 %shard_map.109 = (bf16[8,16,256]{2,1,0:T(8,128)(2,1)S(1)}, f32[4,1024]{1,0:T(4,128)S(1)}) custom-call(s32[1,7]{1,0:T(1,128)S(4)} %get-tuple-element.27.ints, f32[1,5]{1,0:T(1,128)S(4)} %get-tuple-element.28.floats, f32[4,1024]{1,0:T(4,128)S(1)} %get-tuple-element.29.log_a, bf16[1,3,1024,1024]{3,2,1,0:T(8,128)(2,1)} %cost_hbm.17, ...), custom_call_target="tpu_custom_call" | custom-call | tf_op jit(solution)/shard_map/pallas_call | solution.py:583
  298.8 19.5 %all_to_all.46.parts = bf16[8,16,256]{2,1,0:T(8,128)(2,1)S(1)} all-to-all(bf16[8,16,256]{2,1,0:T(8,128)(2,1)S(1)} %get-tuple-element.42), channel_id=1, replica_groups=mesh['src'=8,'tgt'=32] {'src'}, dimensions={0} | all-to-all | bytes 131072 | tf_op jit(solution)/shard_map/all_to_all | solution.py:510
  318.3 24.1 %shard_map.110 = bf16[32,16,256]{2,1,0:T(8,128)(2,1)S(1)} custom-call(s32[1,7]{1,0:T(1,128)S(4)} %get-tuple-element.27.ints, f32[1,5]{1,0:T(1,128)S(4)} %get-tuple-element.28.floats, f32[4,1024]{1,0:T(4,128)S(1)} %get-tuple-element.31.log_b.rest_1_, bf16[1,3,1024,1024]{3,2,1,0:T(8,128)(2,1)} %cost_hbm.17, ...), custom_call_target="tpu_custom_call" | custom-call | tf_op jit(solution)/shard_map/pallas_call | solution.py:594
  342.4 28.4 %all_to_all.47.parts = bf16[32,16,256]{2,1,0:T(8,128)(2,1)S(1)} all-to-all(bf16[32,16,256]{2,1,0:T(8,128)(2,1)S(1)} %shard_map.110), channel_id=1, replica_groups=mesh['src'=8,'tgt'=32] {'tgt'}, dimensions={0} | all-to-all | bytes 524288 | tf_op jit(solution)/shard_map/all_to_all | solution.py:510
  370.8 31.6 %shard_map.112 = f32[4,72,512]{2,1,0:T(8,128)S(1)} custom-call(s32[1,7]{1,0:T(1,128)S(4)} %get-tuple-element.27.ints, f32[1,5]{1,0:T(1,128)S(4)} %get-tuple-element.28.floats, f32[4,1024]{1,0:T(4,128)S(1)} %get-tuple-element.29.log_a, bf16[1,3,1024,1024]{3,2,1,0:T(8,128)(2,1)} %cost_hbm.17, bf16[3,1024,1024]{2,1,0:T(8,128)(2,1)S(1)} %get-tuple-element.30.k_ref, ...), custom_call_target="tpu_custom_call" | custom-call | flops 471859200 | bytes 3145728 | tf_op jit(solution)/shard_map/pallas_call | solution.py:610
  402.4 3.7 collective-permute-start
  406.1 31.6 %shard_map.111 = (f32[4,1024]{1,0:T(4,128)S(1)}, f32[4,72,512]{2,1,0:T(8,128)S(1)}) custom-call(s32[1,7]{1,0:T(1,128)S(4)} %get-tuple-element.27.ints, f32[1,5]{1,0:T(1,128)S(4)} %get-tuple-element.28.floats, f32[4,1024]{1,0:T(4,128)S(1)} %get-tuple-element.29.log_a, bf16[1,3,1024,1024]{3,2,1,0:T(8,128)(2,1)} %cost_hbm.17, ...), custom_call_target="tpu_custom_call" | custom-call | flops 471859200 | bytes 3145728 | tf_op jit(solution)/shard_map/pallas_call | solution.py:610
  437.7 0.2 shard_map.113
  437.8 28.4 %collective-permute-start.1 = (bf16[80,512]{1,0:T(8,128)(2,1)S(1)}, bf16[80,512]{1,0:T(8,128)(2,1)S(1)}, u32[]{:S(2)}, u32[]{:S(2)}) collective-permute-start(bf16[80,512]{1,0:T(8,128)(2,1)S(1)} %get-tuple-element.46), channel_id=1, source_target_pairs={{0,64},{32,96},{64,0},{96,32},{128,192},{160,224},{192,128},{224,1... | collective-permute-start | bytes 245768 | tf_op jit(solution)/shard_map/ppermute | solution.py:496
  466.2 0.5 collective-permute-start.2
  466.8 1.9 collective-permute-start.3
  468.7 2.4 collective-permute-done.2.rest_2_
  471.1 0.8 collective-permute-done.3.rest_3_
  472.1 2.5 collective-permute-start.5
  474.6 1.4 collective-permute-start.6
  476.0 0.5 collective-permute-start.8
  476.5 0.8 collective-permute-done.5.refs_2_
  477.3 1.8 collective-permute-done.6.refs_3_
  479.1 0.6 copy.13
  479.8 0.7 collective-permute-done.10.refs_7_
  480.4 0.8 shard_map.115
  (14 shorter events, 0.3 us)
Async XLA Ops:
  76.1 45.8 %copy-start = (bf16[128,64]{0,1:T(8,128)(2,1)S(1)}, bf16[128,64]{0,1:T(8,128)(2,1)}, u32[]{:S(2)}) copy-start(bf16[128,64]{0,1:T(8,128)(2,1)} %param.15) | copy-start | bytes 49156
  402.4 35.3 %collective-permute-start = (f32[4,72,512]{2,1,0:T(8,128)S(1)}, f32[4,72,512]{2,1,0:T(8,128)S(1)}, u32[]{:S(2)}, u32[]{:S(2)}) collective-permute-start(f32[4,72,512]{2,1,0:T(8,128)S(1)} %shard_map.112), channel_id=1, source_target_pairs={{0,32},{32,0},{64,96},{96,64},{128,160},{160,128},{192,224},{224,1... | collective-permute-start | bytes 1769480 | tf_op jit(solution)/shard_map/ppermute | solution.py:496
  437.8 30.9 %collective-permute-start.1 = (bf16[80,512]{1,0:T(8,128)(2,1)S(1)}, bf16[80,512]{1,0:T(8,128)(2,1)S(1)}, u32[]{:S(2)}, u32[]{:S(2)}) collective-permute-start(bf16[80,512]{1,0:T(8,128)(2,1)S(1)} %get-tuple-element.46), channel_id=1, source_target_pairs={{0,64},{32,96},{64,0},{96,32},{128,192},{160,224},{192,128},{224,1... | collective-permute-start | bytes 245768 | tf_op jit(solution)/shard_map/ppermute | solution.py:496
  466.2 4.9 %collective-permute-start.2 = (bf16[80,512]{1,0:T(8,128)(2,1)S(1)}, bf16[80,512]{1,0:T(8,128)(2,1)S(1)}, u32[]{:S(2)}, u32[]{:S(2)}) collective-permute-start(bf16[80,512]{1,0:T(8,128)(2,1)S(1)} %get-tuple-element.47), channel_id=1, source_target_pairs={{0,128},{32,160},{64,192},{96,224},{128,0},{160,32},{192,64},{224,... | collective-permute-start | bytes 245768 | tf_op jit(solution)/shard_map/ppermute | solution.py:496
  466.8 5.1 %collective-permute-start.3 = (bf16[80,512]{1,0:T(8,128)(2,1)S(1)}, bf16[80,512]{1,0:T(8,128)(2,1)S(1)}, u32[]{:S(2)}, u32[]{:S(2)}) collective-permute-start(bf16[80,512]{1,0:T(8,128)(2,1)S(1)} %get-tuple-element.48), channel_id=1, source_target_pairs={{0,192},{32,224},{64,128},{96,160},{128,64},{160,96},{192,0},{224,... | collective-permute-start | bytes 245768 | tf_op jit(solution)/shard_map/ppermute | solution.py:496
  472.0 4.0 collective-permute-start.4
  472.1 5.2 %collective-permute-start.5 = (bf16[80,512]{1,0:T(8,128)(2,1)S(1)}, bf16[80,512]{1,0:T(8,128)(2,1)S(1)}, u32[]{:S(2)}, u32[]{:S(2)}) collective-permute-start(bf16[80,512]{1,0:T(8,128)(2,1)S(1)} %shard_map.114.refs_0_), channel_id=1, source_target_pairs={{0,128},{32,160},{64,192},{96,224},{128,0},{160,32},{192,64},{224,... | collective-permute-start | bytes 245768 | tf_op jit(solution)/shard_map/ppermute | solution.py:496
  474.6 4.5 collective-permute-start.6
  476.0 3.8 collective-permute-start.7
  476.0 3.8 collective-permute-start.8
  477.3 2.4 collective-permute-start.9
  479.1 1.3 collective-permute-start.10

commit v8 on v7

--- a/solution.py
+++ b/solution.py
@@ -217,7 +217,7 @@
         floats[0, s] = scale[0, s]
     ints[0, 2 * total] = count[0, 0]
     slots = Slots(ints, floats, total)
-    chunk, tile = 32, cost_v.shape[2]
+    chunk, tile = 16, cost_v.shape[2]
 
     def build(shift, wait):
         sums[...] = jnp.zeros(sums.shape, F32)
@@ -232,7 +232,7 @@
                     if wait:
                         copies[s][h].wait()
 
-                    @pl.loop(0, PART // chunk, unroll=2)
+                    @pl.loop(0, PART // chunk, unroll=4)
                     def _(i):
                         here = pl.ds(pl.multiple_of(h * PART + i * chunk, chunk), chunk)
                         x = cost_v[s, here, :].astype(F32) * (-TO2 * slots.scale[s])
@@ -465,8 +465,8 @@
     out[classes:] = split_rows(EPS * mass - EPS * total)
 
 
-def assemble_kernel(order, *refs):
-    pieces, (g_out, out, row) = refs[: len(order)], refs[len(order) :]
+def assemble_kernel(order, f, *refs):
+    pieces, (f_out, g_out, out, row, f_row) = refs[: len(order)], refs[len(order) :]
     src = lax.axis_index("src")
     classes, width = out.shape[0], pieces[0].shape[1]
     for k, piece in zip(order, pieces):
@@ -474,6 +474,10 @@
         out[:, here] = piece[:classes]
         row[:, here] = tail_row(piece[...])
     g_out[...] = row[...].reshape(g_out.shape)
+    tile = f.shape[1]
+    for r in range(f.shape[0]):
+        f_row[:, r * tile : (r + 1) * tile] = f[r : r + 1, :]
+    f_out[...] = f_row[...].reshape(f_out.shape)
 
 
 VM = pl.BlockSpec(memory_space=pltpu.VMEM)
@@ -638,7 +642,8 @@
         out_specs=(VM,) * n_y,
         compiler_params=PARAMS,
     )(keep, got)
-    pieces = [pieces[0]] + [xor(pieces[q], "src", 2 * q) for q in range(1, n_y)]
+    far_first = (2, 1, 3)
+    pieces = [pieces[0]] + [xor(pieces[q], "src", 2 * q) for q in far_first]
     done = pl.pallas_call(
         combine_kernel,
         out_shape=piece,
@@ -646,18 +651,19 @@
         out_specs=VM,
         compiler_params=PARAMS,
     )(log_b, *pieces)
-    pieces = [done] + [xor(done, "src", 2 * q) for q in range(1, n_y)]
+    pieces = [done] + [xor(done, "src", 2 * q) for q in far_first]
     pieces = pieces + [xor(p, "src", 1) for p in pieces]
-    order = tuple(2 * q for q in range(n_y)) + tuple(2 * q + 1 for q in range(n_y))
-    g_pot, out = pl.pallas_call(
+    order = (0,) + tuple(2 * q for q in far_first)
+    order = order + tuple(k + 1 for k in order)
+    f_pot, g_pot, out = pl.pallas_call(
         functools.partial(assemble_kernel, order),
-        out_shape=(vec((cb * tile,)), jax.ShapeDtypeStruct((classes, cb * tile), BF16)),
-        in_specs=[VM] * n_src,
-        out_specs=(VM, VM),
-        scratch_shapes=[pltpu.VMEM((1, cb * tile), F32)],
+        out_shape=(vec((rb * tile,)), vec((cb * tile,)), jax.ShapeDtypeStruct((classes, cb * tile), BF16)),
+        in_specs=[VM] * (1 + n_src),
+        out_specs=(VM,) * 3,
+        scratch_shapes=[pltpu.VMEM((1, cb * tile), F32), pltpu.VMEM((1, rb * tile), F32)],
         compiler_params=PARAMS,
-    )(*pieces)
-    return f_pot.reshape(-1), g_pot, out.T
+    )(f_pot, *pieces)
+    return f_pot, g_pot, out.T
 
 
 def solution(mesh):

time: 489 us -> 500 us (1.022); the launches traced: 481 us -> 500 us
  Pallas kernels: 242 us -> 82.3 us
  blocking collectives: 191 us -> 332 us
  starting transfers between devices: 39.1 us -> 77.6 us
    all_to_all x8, blocking collectives: 191 us -> 332 us  [everyone(): lax.all_to_all(copies, axis, 0, 0, axis_index_groups=groups, tiled=True)]
    pallas_call x3, Pallas kernels: 71.9 us -> 2.78 us  [local(): pl.pallas_call(functools.partial(row_kernel, slots, first), out_shape=(se...]
    ppermute x11, starting transfers between devices: 39.1 us -> 77.6 us  [xor(): lax.ppermute(x, axis, [(i, i ^ k) for i in range(lax.axis_size(axis))])]
    pallas_call x3, Pallas kernels: 69.2 us -> 34.8 us  [local(): pl.pallas_call(functools.partial(col_kernel, slots, first), out_shape=(ve...]
    pallas_call x2, Pallas kernels: 63.1 us -> 31.7 us  [label_call(): pl.pallas_call(functools.partial(label_kernel, slots, own), out_shape=(ve...]
    pallas_call x1, Pallas kernels: 36.8 us -> 11.8 us  [local(): pl.pallas_call(functools.partial(build_kernel, dims), out_shape=(pltpu.VM...]
  transfers between devices with their start and end apart: 11 -> 11, of which waited for: 5 -> 3; matrix products, arithmetic and copies ran while one was open for 0% -> 0% of each run, Pallas kernels for 7% -> 3%
where the time goes in v8:
time: 500 us
  blocking collectives  332 us (66%)
  Pallas kernels  82.3 us (16%)
  starting transfers between devices  77.6 us (16%)
  waiting for transfers between devices  6.31 us (1%)
    all_to_all x8, blocking collectives, everyone(): lax.all_to_all(copies, axis, 0, 0, axis_index_groups=groups, tiled=True)  332 us
    ppermute x11, starting transfers between devices, xor(): lax.ppermute(x, axis, [(i, i ^ k) for i in range(lax.axis_size(axis))])  77.6 us
    pallas_call x3, Pallas kernels, local(): pl.pallas_call(functools.partial(col_kernel, slots, first), out_shape=(ve...  34.8 us
    pallas_call x2, Pallas kernels, label_call(): pl.pallas_call(functools.partial(label_kernel, slots, own), out_shape=(ve...  31.7 us
    pallas_call x1, Pallas kernels, local(): pl.pallas_call(functools.partial(build_kernel, dims), out_shape=(pltpu.VM...  11.8 us
  transfers between devices with their start and end apart: 11, of which 3 were waited for; matrix products, arithmetic and copies ran while one was open for 0% of the time, Pallas kernels for 3%

profile of v8, /device:TPU:1, one launch (start us, length us, event | category | flops | bytes accessed | tf_op | source)
XLA Modules:
  0.0 499.9 jit_solution(14785787212916410488)
XLA Ops:
  1.3 11.8 %shard_map.103 = (bf16[3,1024,1024]{2,1,0:T(8,128)(2,1)S(1)}, bf16[32,16,256]{2,1,0:T(8,128)(2,1)S(1)}, s32[1,7]{1,0:T(1,128)S(4)}, f32[1,5]{1,0:T(1,128)S(4)}, ...) custom-call(s32[1,1]{1,0:T(1,128)S(6)} %copy.11.count, f32[1,3]{1,0:T(1,128)} %scale_hbm.1, s32[1,3]{1,0:T(1,128)} %row_hbm.1, ...), custom_call_target="tpu_custom_call" | custom-call | tf_op jit(solution)/shard_map/pallas_call | solution.py:523
  13.1 75.3 %all_to_all.40.parts = bf16[32,16,256]{2,1,0:T(8,128)(2,1)S(1)} all-to-all(bf16[32,16,256]{2,1,0:T(8,128)(2,1)S(1)} %get-tuple-element.33), channel_id=1, replica_groups=mesh['src'=8,'tgt'=32] {'tgt'}, dimensions={0} | all-to-all | bytes 524288 | tf_op jit(solution)/shard_map/all_to_all | solution.py:514
  88.3 11.7 %shard_map.104 = (f32[8,4,1024]{2,1,0:T(4,128)S(1)}, f32[4,1024]{1,0:T(4,128)S(1)}) custom-call(s32[1,7]{1,0:T(1,128)S(4)} %get-tuple-element.28.ints, f32[1,5]{1,0:T(1,128)S(4)} %get-tuple-element.29.floats, f32[4,1024]{1,0:T(4,128)S(1)} %get-tuple-element.30.log_a, bf16[1,3,1024,1024]{3,2,1,0:T(8,128)(2,1)} %cost_hbm.17, ...), custom_call_target="tpu_custom_call" | custom-call | tf_op jit(solution)/shard_map/pallas_call | solution.py:587
  100.0 35.7 %all_to_all.41.parts = f32[8,4,1024]{2,1,0:T(4,128)S(1)} all-to-all(f32[8,4,1024]{2,1,0:T(4,128)S(1)} %get-tuple-element.34), channel_id=1, replica_groups=mesh['src'=8,'tgt'=32] {'src'}, dimensions={0} | all-to-all | bytes 262144 | tf_op jit(solution)/shard_map/all_to_all | solution.py:514
  135.7 0.9 shard_map.105
  136.6 46.8 %all_to_all.42.parts = bf16[8,48,256]{2,1,0:T(8,128)(2,1)S(1)} all-to-all(bf16[8,48,256]{2,1,0:T(8,128)(2,1)S(1)} %get-tuple-element.36), channel_id=1, replica_groups={{0,1,2,3,4,5,6,7},{8,9,10,11,12,13,14,15},{16,17,18,19,20,21,22,23},{24..., dimensions={0} | all-to-all | bytes 393216 | tf_op jit(solution)/shard_map/all_to_all | solution.py:514
  183.4 9.8 %all_to_all.43.parts.box = bf16[4,272,256]{2,1,0:T(8,128)(2,1)S(1)} all-to-all(bf16[4,272,256]{2,1,0:T(8,128)(2,1)S(1)} %shard_map.106), channel_id=1, replica_groups={{0,8,16,24},{1,9,17,25},{2,10,18,26},{3,11,19,27},{4,12,20,28},{5,13,21..., dimensions={0} | all-to-all | bytes 1114112 | tf_op jit(solution)/shard_map/all_to_all | solution.py:514
  193.3 11.5 %shard_map.107 = (bf16[8,16,256]{2,1,0:T(8,128)(2,1)S(1)}, f32[4,1024]{1,0:T(4,128)S(1)}) custom-call(s32[1,7]{1,0:T(1,128)S(4)} %get-tuple-element.28.ints, f32[1,5]{1,0:T(1,128)S(4)} %get-tuple-element.29.floats, f32[4,1024]{1,0:T(4,128)S(1)} %get-tuple-element.30.log_a, bf16[1,3,1024,1024]{3,2,1,0:T(8,128)(2,1)} %cost_hbm.17, ...), custom_call_target="tpu_custom_call" | custom-call | tf_op jit(solution)/shard_map/pallas_call | solution.py:587
  204.8 35.2 %all_to_all.44.parts = bf16[8,16,256]{2,1,0:T(8,128)(2,1)S(1)} all-to-all(bf16[8,16,256]{2,1,0:T(8,128)(2,1)S(1)} %get-tuple-element.38), channel_id=1, replica_groups=mesh['src'=8,'tgt'=32] {'src'}, dimensions={0} | all-to-all | bytes 131072 | tf_op jit(solution)/shard_map/all_to_all | solution.py:514
  240.0 0.9 shard_map.108
  240.9 45.9 %all_to_all.45.parts = bf16[32,16,256]{2,1,0:T(8,128)(2,1)S(1)} all-to-all(bf16[32,16,256]{2,1,0:T(8,128)(2,1)S(1)} %get-tuple-element.40), channel_id=1, replica_groups=mesh['src'=8,'tgt'=32] {'tgt'}, dimensions={0} | all-to-all | bytes 524288 | tf_op jit(solution)/shard_map/all_to_all | solution.py:514
  286.8 11.6 %shard_map.109 = (bf16[8,16,256]{2,1,0:T(8,128)(2,1)S(1)}, f32[4,1024]{1,0:T(4,128)S(1)}) custom-call(s32[1,7]{1,0:T(1,128)S(4)} %get-tuple-element.28.ints, f32[1,5]{1,0:T(1,128)S(4)} %get-tuple-element.29.floats, f32[4,1024]{1,0:T(4,128)S(1)} %get-tuple-element.30.log_a, bf16[1,3,1024,1024]{3,2,1,0:T(8,128)(2,1)} %cost_hbm.17, ...), custom_call_target="tpu_custom_call" | custom-call | tf_op jit(solution)/shard_map/pallas_call | solution.py:587
  298.4 34.0 %all_to_all.46.parts = bf16[8,16,256]{2,1,0:T(8,128)(2,1)S(1)} all-to-all(bf16[8,16,256]{2,1,0:T(8,128)(2,1)S(1)} %get-tuple-element.43), channel_id=1, replica_groups=mesh['src'=8,'tgt'=32] {'src'}, dimensions={0} | all-to-all | bytes 131072 | tf_op jit(solution)/shard_map/all_to_all | solution.py:514
  332.4 1.0 shard_map.110
  333.5 49.6 %all_to_all.47.parts = bf16[32,16,256]{2,1,0:T(8,128)(2,1)S(1)} all-to-all(bf16[32,16,256]{2,1,0:T(8,128)(2,1)S(1)} %shard_map.110), channel_id=1, replica_groups=mesh['src'=8,'tgt'=32] {'tgt'}, dimensions={0} | all-to-all | bytes 524288 | tf_op jit(solution)/shard_map/all_to_all | solution.py:514
  383.0 15.9 %shard_map.112 = f32[4,72,512]{2,1,0:T(8,128)S(1)} custom-call(s32[1,7]{1,0:T(1,128)S(4)} %get-tuple-element.28.ints, f32[1,5]{1,0:T(1,128)S(4)} %get-tuple-element.29.floats, f32[4,1024]{1,0:T(4,128)S(1)} %get-tuple-element.30.log_a, bf16[1,3,1024,1024]{3,2,1,0:T(8,128)(2,1)} %cost_hbm.17, bf16[3,1024,1024]{2,1,0:T(8,128)(2,1)S(1)} %get-tuple-element.31.k_ref, ...), custom_call_target="tpu_custom_call" | custom-call | flops 471859200 | bytes 3145728 | tf_op jit(solution)/shard_map/pallas_call | solution.py:614
  398.9 19.5 %collective-permute-start = (f32[4,72,512]{2,1,0:T(8,128)S(1)}, f32[4,72,512]{2,1,0:T(8,128)S(1)}, u32[]{:S(2)}, u32[]{:S(2)}) collective-permute-start(f32[4,72,512]{2,1,0:T(8,128)S(1)} %shard_map.112), channel_id=1, source_target_pairs={{0,32},{32,0},{64,96},{96,64},{128,160},{160,128},{192,224},{224,1... | collective-permute-start | bytes 1769480 | tf_op jit(solution)/shard_map/ppermute | solution.py:500
  418.4 15.9 %shard_map.111 = (f32[4,1024]{1,0:T(4,128)S(1)}, f32[4,72,512]{2,1,0:T(8,128)S(1)}) custom-call(s32[1,7]{1,0:T(1,128)S(4)} %get-tuple-element.28.ints, f32[1,5]{1,0:T(1,128)S(4)} %get-tuple-element.29.floats, f32[4,1024]{1,0:T(4,128)S(1)} %get-tuple-element.30.log_a, bf16[1,3,1024,1024]{3,2,1,0:T(8,128)(2,1)} %cost_hbm.17, ...), custom_call_target="tpu_custom_call" | custom-call | flops 471859200 | bytes 3145728 | tf_op jit(solution)/shard_map/pallas_call | solution.py:614
  434.3 0.2 shard_map.113
  434.5 16.4 %collective-permute-start.1 = (bf16[80,512]{1,0:T(8,128)(2,1)S(1)}, bf16[80,512]{1,0:T(8,128)(2,1)S(1)}, u32[]{:S(2)}, u32[]{:S(2)}) collective-permute-start(bf16[80,512]{1,0:T(8,128)(2,1)S(1)} %get-tuple-element.47), channel_id=1, source_target_pairs={{0,128},{32,160},{64,192},{96,224},{128,0},{160,32},{192,64},{224,... | collective-permute-start | bytes 245768 | tf_op jit(solution)/shard_map/ppermute | solution.py:500
  450.8 28.6 %collective-permute-start.2 = (bf16[80,512]{1,0:T(8,128)(2,1)S(1)}, bf16[80,512]{1,0:T(8,128)(2,1)S(1)}, u32[]{:S(2)}, u32[]{:S(2)}) collective-permute-start(bf16[80,512]{1,0:T(8,128)(2,1)S(1)} %get-tuple-element.48), channel_id=1, source_target_pairs={{0,64},{32,96},{64,0},{96,32},{128,192},{160,224},{192,128},{224,1... | collective-permute-start | bytes 245768 | tf_op jit(solution)/shard_map/ppermute | solution.py:500
  479.4 2.7 collective-permute-done.2.rest_2_
  482.1 2.7 collective-permute-done.3.rest_3_
  484.8 0.1 shard_map.114.refs_0_
  485.0 0.3 collective-permute-start.5
  485.3 3.0 collective-permute-start.6
  488.2 5.2 %collective-permute-start.7 = (bf16[80,512]{1,0:T(8,128)(2,1)S(1)}, bf16[80,512]{1,0:T(8,128)(2,1)S(1)}, u32[]{:S(2)}, u32[]{:S(2)}) collective-permute-start(bf16[80,512]{1,0:T(8,128)(2,1)S(1)} %shard_map.114.refs_0_), channel_id=1, source_target_pairs={{0,32},{32,0},{64,96},{96,64},{128,160},{160,128},{192,224},{224,1... | collective-permute-start | bytes 245768 | tf_op jit(solution)/shard_map/ppermute | solution.py:500
  493.5 1.1 collective-permute-start.8
  494.6 2.0 collective-permute-start.9
  496.6 1.5 collective-permute-start.10
  498.1 0.9 collective-permute-done.10.refs_7_
  499.0 0.9 shard_map.115
  (13 shorter events, 0.2 us)
Async XLA Ops:
  88.3 47.3 %copy-start = (bf16[128,64]{0,1:T(8,128)(2,1)S(1)}, bf16[128,64]{0,1:T(8,128)(2,1)}, u32[]{:S(2)}) copy-start(bf16[128,64]{0,1:T(8,128)(2,1)} %param.15) | copy-start | bytes 49156
  398.9 35.4 %collective-permute-start = (f32[4,72,512]{2,1,0:T(8,128)S(1)}, f32[4,72,512]{2,1,0:T(8,128)S(1)}, u32[]{:S(2)}, u32[]{:S(2)}) collective-permute-start(f32[4,72,512]{2,1,0:T(8,128)S(1)} %shard_map.112), channel_id=1, source_target_pairs={{0,32},{32,0},{64,96},{96,64},{128,160},{160,128},{192,224},{224,1... | collective-permute-start | bytes 1769480 | tf_op jit(solution)/shard_map/ppermute | solution.py:500
  434.5 45.0 %collective-permute-start.1 = (bf16[80,512]{1,0:T(8,128)(2,1)S(1)}, bf16[80,512]{1,0:T(8,128)(2,1)S(1)}, u32[]{:S(2)}, u32[]{:S(2)}) collective-permute-start(bf16[80,512]{1,0:T(8,128)(2,1)S(1)} %get-tuple-element.47), channel_id=1, source_target_pairs={{0,128},{32,160},{64,192},{96,224},{128,0},{160,32},{192,64},{224,... | collective-permute-start | bytes 245768 | tf_op jit(solution)/shard_map/ppermute | solution.py:500
  450.8 31.3 %collective-permute-start.2 = (bf16[80,512]{1,0:T(8,128)(2,1)S(1)}, bf16[80,512]{1,0:T(8,128)(2,1)S(1)}, u32[]{:S(2)}, u32[]{:S(2)}) collective-permute-start(bf16[80,512]{1,0:T(8,128)(2,1)S(1)} %get-tuple-element.48), channel_id=1, source_target_pairs={{0,64},{32,96},{64,0},{96,32},{128,192},{160,224},{192,128},{224,1... | collective-permute-start | bytes 245768 | tf_op jit(solution)/shard_map/ppermute | solution.py:500
  479.4 5.4 %collective-permute-start.3 = (bf16[80,512]{1,0:T(8,128)(2,1)S(1)}, bf16[80,512]{1,0:T(8,128)(2,1)S(1)}, u32[]{:S(2)}, u32[]{:S(2)}) collective-permute-start(bf16[80,512]{1,0:T(8,128)(2,1)S(1)} %get-tuple-element.49), channel_id=1, source_target_pairs={{0,192},{32,224},{64,128},{96,160},{128,64},{160,96},{192,0},{224,... | collective-permute-start | bytes 245768 | tf_op jit(solution)/shard_map/ppermute | solution.py:500
  484.9 8.6 %collective-permute-start.4 = (bf16[80,512]{1,0:T(8,128)(2,1)S(1)}, bf16[80,512]{1,0:T(8,128)(2,1)S(1)}, u32[]{:S(2)}, u32[]{:S(2)}) collective-permute-start(bf16[80,512]{1,0:T(8,128)(2,1)S(1)} %shard_map.114.refs_0_), channel_id=1, source_target_pairs={{0,128},{32,160},{64,192},{96,224},{128,0},{160,32},{192,64},{224,... | collective-permute-start | bytes 245768 | tf_op jit(solution)/shard_map/ppermute | solution.py:500
  485.0 9.6 %collective-permute-start.5 = (bf16[80,512]{1,0:T(8,128)(2,1)S(1)}, bf16[80,512]{1,0:T(8,128)(2,1)S(1)}, u32[]{:S(2)}, u32[]{:S(2)}) collective-permute-start(bf16[80,512]{1,0:T(8,128)(2,1)S(1)} %shard_map.114.refs_0_), channel_id=1, source_target_pairs={{0,64},{32,96},{64,0},{96,32},{128,192},{160,224},{192,128},{224,1... | collective-permute-start | bytes 245768 | tf_op jit(solution)/shard_map/ppermute | solution.py:500
  485.3 11.3 %collective-permute-start.6 = (bf16[80,512]{1,0:T(8,128)(2,1)S(1)}, bf16[80,512]{1,0:T(8,128)(2,1)S(1)}, u32[]{:S(2)}, u32[]{:S(2)}) collective-permute-start(bf16[80,512]{1,0:T(8,128)(2,1)S(1)} %shard_map.114.refs_0_), channel_id=1, source_target_pairs={{0,192},{32,224},{64,128},{96,160},{128,64},{160,96},{192,0},{224,... | collective-permute-start | bytes 245768 | tf_op jit(solution)/shard_map/ppermute | solution.py:500
  488.2 9.9 %collective-permute-start.7 = (bf16[80,512]{1,0:T(8,128)(2,1)S(1)}, bf16[80,512]{1,0:T(8,128)(2,1)S(1)}, u32[]{:S(2)}, u32[]{:S(2)}) collective-permute-start(bf16[80,512]{1,0:T(8,128)(2,1)S(1)} %shard_map.114.refs_0_), channel_id=1, source_target_pairs={{0,32},{32,0},{64,96},{96,64},{128,160},{160,128},{192,224},{224,1... | collective-permute-start | bytes 245768 | tf_op jit(solution)/shard_map/ppermute | solution.py:500
  493.5 4.7 collective-permute-start.8
  494.6 3.6 collective-permute-start.9
  496.6 2.5 collective-permute-start.10

commit v9 on v8

--- a/solution.py
+++ b/solution.py
@@ -171,8 +171,26 @@
         out[:, here] = base - EPS * flat[c * count : (c + 1) * count, :]
 
 
-def sums_fine(low, high, others):
-    return (low >= 2.0**-80 * jnp.maximum(others, 1.0)) & (high <= 2.0**100)
+def clear_stat(stat):
+    stat[0:1, :] = jnp.zeros((1, stat.shape[1]), F32)
+    stat[1:2, :] = jnp.full((1, stat.shape[1]), jnp.inf, F32)
+    stat[2:3, :] = jnp.zeros((1, stat.shape[1]), F32)
+
+
+def note_stat(stat, part, other=None):
+    here = slice(0, part.shape[1])
+    stat[0:1, here] = jnp.maximum(stat[0:1, here], jnp.where(part <= 2.0**100, part, jnp.inf))
+    stat[1:2, here] = jnp.minimum(stat[1:2, here], part)
+    if other is not None:
+        stat[2:3, :] = jnp.maximum(stat[2:3, :], other)
+
+
+def sums_fine(stat, high=None):
+    top = jnp.max(stat[0:1, :], axis=1, keepdims=True)
+    low = jnp.min(stat[1:2, :], axis=1, keepdims=True)
+    others = top if high is None else jnp.maximum(jnp.max(stat[2:3, :], axis=1, keepdims=True), high)
+    fine = (low >= 2.0**-80 * jnp.maximum(others, 1.0)) & (top <= 2.0**100)
+    return jnp.max(jnp.where(fine, 0.0, 1.0)) < 0.5
 
 
 def build_kernel(
@@ -222,8 +240,7 @@
     def build(shift, wait):
         sums[...] = jnp.zeros(sums.shape, F32)
         floats[0, total] = jnp.float32(0.0) if shift is None else shift
-        stat[1] = jnp.float32(0.0)
-        stat[2] = jnp.float32(jnp.inf)
+        clear_stat(stat)
         for s in range(total):
 
             @pl.when(slots.live[s])
@@ -245,12 +262,11 @@
                 part = fold_rows(tall)
                 at = pl.ds(slots.row[s], 1)
                 sums[at, :] = sums[at, :] + part
-                stat[1] = jnp.maximum(stat[1], jnp.max(part))
-                stat[2] = jnp.minimum(stat[2], jnp.min(part))
+                note_stat(stat, part)
 
         l_ref[...] = to_log(sums[...], floats[0, total])
-        floats[0, total + 1] = stat[1]
-        return sums_fine(stat[2], stat[1], stat[1])
+        floats[0, total + 1] = jnp.max(stat[0:1, :])
+        return sums_fine(stat)
 
     fine = build(None, True)
     for copy in small[3:]:
@@ -262,7 +278,7 @@
 
     @pl.when(jnp.logical_not(fine))
     def _():
-        stat[0] = jnp.float32(jnp.inf)
+        floats[0, total] = jnp.float32(jnp.inf)
         for s in range(total):
 
             @pl.when(slots.live[s])
@@ -272,9 +288,9 @@
                     return jnp.minimum(low, jnp.min(cost_v[s, here, :].astype(F32)))
 
                 low = lax.fori_loop(0, tile // chunk, lowest, jnp.float32(jnp.inf))
-                stat[0] = jnp.minimum(stat[0], low * slots.scale[s])
-
-        shifted = build(stat[0], False)
+                floats[0, total] = jnp.minimum(floats[0, total], low * slots.scale[s])
+
+        shifted = build(floats[0, total], False)
 
         @pl.when(jnp.logical_not(shifted))
         def _():
@@ -291,9 +307,7 @@
     slots = Slots(ints, floats, total)
     new_potential(g, log_b, parts, prev, flat)
     sums[...] = jnp.zeros(sums.shape, F32)
-    stat[0] = jnp.float32(0.0)
-    stat[1] = jnp.float32(jnp.inf)
-    stat[2] = slots.high
+    clear_stat(stat)
     for s in range(slots.total):
 
         @pl.when(slots.live[s])
@@ -302,13 +316,11 @@
             part = jnp.sum(k_row(split_rows(v), k_ref[s]), axis=0, keepdims=True)
             at = pl.ds(slots.row[s], 1)
             sums[at, :] = sums[at, :] + part
-            stat[0] = jnp.maximum(stat[0], jnp.max(part))
-            stat[1] = jnp.minimum(stat[1], jnp.min(part))
-            stat[2] = jnp.maximum(stat[2], jnp.max(v))
+            note_stat(stat, part, v)
 
     l_ref[...] = to_log(sums[...], slots.shift)
 
-    @pl.when(jnp.logical_not(sums_fine(stat[1], stat[0], stat[2])))
+    @pl.when(jnp.logical_not(sums_fine(stat, slots.high)))
     def _():
         slow_lse(slots, cost_hbm, cost_v, sem, other8, out8, g, l_ref, True)
 
@@ -335,9 +347,7 @@
     slots = Slots(ints, floats, total)
     new_potential(f, log_a, parts, prev, flat)
     sums[...] = jnp.zeros(sums.shape, F32)
-    stat[0] = jnp.float32(0.0)
-    stat[1] = jnp.float32(jnp.inf)
-    stat[2] = slots.high
+    clear_stat(stat)
     for s in range(slots.total):
 
         @pl.when(slots.live[s])
@@ -346,13 +356,11 @@
             part = jnp.sum(k_col(split_rows(u), k_ref[s]), axis=0, keepdims=True)
             at = pl.ds(slots.col[s], 1)
             sums[at, :] = sums[at, :] + part
-            stat[0] = jnp.maximum(stat[0], jnp.max(part))
-            stat[1] = jnp.minimum(stat[1], jnp.min(part))
-            stat[2] = jnp.maximum(stat[2], jnp.max(u))
+            note_stat(stat, part, u)
 
     l_ref[...] = to_log(sums[...], slots.shift)
 
-    @pl.when(jnp.logical_not(sums_fine(stat[1], stat[0], stat[2])))
+    @pl.when(jnp.logical_not(sums_fine(stat, slots.high)))
     def _():
         slow_lse(slots, cost_hbm, cost_v, sem, other8, out8, f, l_ref, False)
 
@@ -370,9 +378,7 @@
     new_potential(f, log_a, parts, prev, flat)
     sums[...] = jnp.zeros(sums.shape, F32)
     acc[...] = jnp.zeros(acc.shape, F32)
-    stat[0] = jnp.float32(0.0)
-    stat[1] = jnp.float32(jnp.inf)
-    stat[2] = slots.high
+    clear_stat(stat)
     high = classes // 2
     core = slots.src % 2
     half = core if own else 1 - core
@@ -397,13 +403,11 @@
             at = pl.ds(slots.col[s], 1)
             sums[at, :] = sums[at, :] + part
             acc[slots.col[s]] = acc[slots.col[s]] + (res[:classes] + res[classes : 2 * classes])
-            stat[0] = jnp.maximum(stat[0], jnp.max(part))
-            stat[1] = jnp.minimum(stat[1], jnp.min(part))
-            stat[2] = jnp.maximum(stat[2], jnp.max(u))
+            note_stat(stat, part, u)
 
     l_ref[...] = to_log(sums[...], slots.shift)
 
-    @pl.when(jnp.logical_not(sums_fine(stat[1], stat[0], stat[2])))
+    @pl.when(jnp.logical_not(sums_fine(stat, slots.high)))
     def _():
         chunks = width // 128
         slow_lse(slots, cost_hbm, cost_v, sem, other8, out8, f, l_ref, False, half * chunks)
@@ -517,7 +521,7 @@
     vec = functools.partial(jax.ShapeDtypeStruct, dtype=F32)
     sent = functools.partial(jax.ShapeDtypeStruct, dtype=BF16)
     chunks = pltpu.VMEM((tile // 128, 128), F32)
-    work = [pltpu.SMEM((3,), F32), pltpu.VMEM((tile, tile), BF16), chunks, chunks, pltpu.SemaphoreType.DMA]
+    work = [pltpu.VMEM((3, tile), F32), pltpu.VMEM((tile, tile), BF16), chunks, chunks, pltpu.SemaphoreType.DMA]
     rows, cols = pltpu.VMEM((rb, tile), F32), pltpu.VMEM((cb, tile), F32)
 
     k_all, row_l, ints, floats, log_a, log_b = pl.pallas_call(
@@ -539,7 +543,7 @@
             cols,
             chunks,
             chunks,
-            pltpu.SMEM((3,), F32),
+            pltpu.VMEM((3, tile), F32),
             pltpu.SemaphoreType.DMA((slots, tile // PART)),
             pltpu.SMEM((1, slots), F32),
             pltpu.SMEM((1, slots), jnp.int32),

time: 500 us -> 497 us (level)
  Pallas kernels: 82.3 us -> 249 us
  blocking collectives: 332 us -> 194 us
  starting transfers between devices: 77.6 us -> 47 us
    all_to_all x8, blocking collectives: 332 us -> 194 us  [everyone(): lax.all_to_all(copies, axis, 0, 0, axis_index_groups=groups, tiled=True)]
    pallas_call x3, Pallas kernels: 2.78 us -> 71.6 us  [local(): pl.pallas_call(functools.partial(row_kernel, slots, first), out_shape=(se...]
    pallas_call x3, Pallas kernels: 34.8 us -> 68.9 us  [local(): pl.pallas_call(functools.partial(col_kernel, slots, first), out_shape=(ve...]
    pallas_call x1, Pallas kernels: 11.8 us -> 44.3 us  [local(): pl.pallas_call(functools.partial(build_kernel, dims), out_shape=(pltpu.VM...]
    pallas_call x2, Pallas kernels: 31.7 us -> 62.9 us  [label_call(): pl.pallas_call(functools.partial(label_kernel, slots, own), out_shape=(ve...]
    ppermute x11, starting transfers between devices: 77.6 us -> 47 us  [xor(): lax.ppermute(x, axis, [(i, i ^ k) for i in range(lax.axis_size(axis))])]
  transfers between devices with their start and end apart: 11 -> 11, of which waited for: 3 -> 5; matrix products, arithmetic and copies ran while one was open for 0% -> 0% of each run, Pallas kernels for 3% -> 6%
where the time goes in v9:
time: 497 us
  Pallas kernels  249 us (50%)
  blocking collectives  194 us (39%)
  starting transfers between devices  47 us (9%)
  waiting for transfers between devices  5.05 us (1%)
    all_to_all x8, blocking collectives, everyone(): lax.all_to_all(copies, axis, 0, 0, axis_index_groups=groups, tiled=True)  194 us
    pallas_call x3, Pallas kernels, local(): pl.pallas_call(functools.partial(row_kernel, slots, first), out_shape=(se...  71.6 us
    pallas_call x3, Pallas kernels, local(): pl.pallas_call(functools.partial(col_kernel, slots, first), out_shape=(ve...  68.9 us
    pallas_call x2, Pallas kernels, label_call(): pl.pallas_call(functools.partial(label_kernel, slots, own), out_shape=(ve...  62.9 us
    ppermute x11, starting transfers between devices, xor(): lax.ppermute(x, axis, [(i, i ^ k) for i in range(lax.axis_size(axis))])  47 us
    pallas_call x1, Pallas kernels, local(): pl.pallas_call(functools.partial(build_kernel, dims), out_shape=(pltpu.VM...  44.3 us
  transfers between devices with their start and end apart: 11, of which 5 were waited for; matrix products, arithmetic and copies ran while one was open for 0% of the time, Pallas kernels for 6%

profile of v9, /device:TPU:1, one launch (start us, length us, event | category | flops | bytes accessed | tf_op | source)
XLA Modules:
  0.0 496.5 jit_solution(9441614375208373799)
XLA Ops:
  1.3 44.3 %shard_map.103 = (bf16[3,1024,1024]{2,1,0:T(8,128)(2,1)S(1)}, bf16[32,16,256]{2,1,0:T(8,128)(2,1)S(1)}, s32[1,7]{1,0:T(1,128)S(4)}, f32[1,5]{1,0:T(1,128)S(4)}, ...) custom-call(s32[1,1]{1,0:T(1,128)S(6)} %copy.11.count, f32[1,3]{1,0:T(1,128)} %scale_hbm.1, s32[1,3]{1,0:T(1,128)} %row_hbm.1, ...), custom_call_target="tpu_custom_call" | custom-call | tf_op jit(solution)/shard_map/pallas_call | solution.py:527
  45.6 40.7 %all_to_all.40.parts = bf16[32,16,256]{2,1,0:T(8,128)(2,1)S(1)} all-to-all(bf16[32,16,256]{2,1,0:T(8,128)(2,1)S(1)} %get-tuple-element.33), channel_id=1, replica_groups=mesh['src'=8,'tgt'=32] {'tgt'}, dimensions={0} | all-to-all | bytes 524288 | tf_op jit(solution)/shard_map/all_to_all | solution.py:518
  86.3 23.0 %shard_map.104 = (f32[8,4,1024]{2,1,0:T(4,128)S(1)}, f32[4,1024]{1,0:T(4,128)S(1)}) custom-call(s32[1,7]{1,0:T(1,128)S(4)} %get-tuple-element.28.ints, f32[1,5]{1,0:T(1,128)S(4)} %get-tuple-element.29.floats, f32[4,1024]{1,0:T(4,128)S(1)} %get-tuple-element.30.log_a, bf16[1,3,1024,1024]{3,2,1,0:T(8,128)(2,1)} %cost_hbm.17, ...), custom_call_target="tpu_custom_call" | custom-call | tf_op jit(solution)/shard_map/pallas_call | solution.py:591
  109.3 26.4 %all_to_all.41.parts = f32[8,4,1024]{2,1,0:T(4,128)S(1)} all-to-all(f32[8,4,1024]{2,1,0:T(4,128)S(1)} %get-tuple-element.34), channel_id=1, replica_groups=mesh['src'=8,'tgt'=32] {'src'}, dimensions={0} | all-to-all | bytes 262144 | tf_op jit(solution)/shard_map/all_to_all | solution.py:518
  135.8 23.8 %shard_map.105 = (bf16[8,48,256]{2,1,0:T(8,128)(2,1)S(1)}, f32[4,1024]{1,0:T(4,128)S(1)}) custom-call(s32[1,7]{1,0:T(1,128)S(4)} %get-tuple-element.28.ints, f32[1,5]{1,0:T(1,128)S(4)} %get-tuple-element.29.floats, f32[4,1024]{1,0:T(4,128)S(1)} %get-tuple-element.32.log_b.rest_1_, bf16[1,3,1024,1024]{3,2,1,0:T(8,128)(2,1)} %cost_hbm.17, ...), custom_call_target="tpu_custom_call" | custom-call | tf_op jit(solution)/shard_map/pallas_call | solution.py:602
  159.6 23.1 %all_to_all.42.parts = bf16[8,48,256]{2,1,0:T(8,128)(2,1)S(1)} all-to-all(bf16[8,48,256]{2,1,0:T(8,128)(2,1)S(1)} %get-tuple-element.36), channel_id=1, replica_groups={{0,1,2,3,4,5,6,7},{8,9,10,11,12,13,14,15},{16,17,18,19,20,21,22,23},{24..., dimensions={0} | all-to-all | bytes 393216 | tf_op jit(solution)/shard_map/all_to_all | solution.py:518
  182.8 9.5 %all_to_all.43.parts.box = bf16[4,272,256]{2,1,0:T(8,128)(2,1)S(1)} all-to-all(bf16[4,272,256]{2,1,0:T(8,128)(2,1)S(1)} %shard_map.106), channel_id=1, replica_groups={{0,8,16,24},{1,9,17,25},{2,10,18,26},{3,11,19,27},{4,12,20,28},{5,13,21..., dimensions={0} | all-to-all | bytes 1114112 | tf_op jit(solution)/shard_map/all_to_all | solution.py:518
  192.3 22.9 %shard_map.107 = (bf16[8,16,256]{2,1,0:T(8,128)(2,1)S(1)}, f32[4,1024]{1,0:T(4,128)S(1)}) custom-call(s32[1,7]{1,0:T(1,128)S(4)} %get-tuple-element.28.ints, f32[1,5]{1,0:T(1,128)S(4)} %get-tuple-element.29.floats, f32[4,1024]{1,0:T(4,128)S(1)} %get-tuple-element.30.log_a, bf16[1,3,1024,1024]{3,2,1,0:T(8,128)(2,1)} %cost_hbm.17, ...), custom_call_target="tpu_custom_call" | custom-call | tf_op jit(solution)/shard_map/pallas_call | solution.py:591
  215.2 22.4 %all_to_all.44.parts = bf16[8,16,256]{2,1,0:T(8,128)(2,1)S(1)} all-to-all(bf16[8,16,256]{2,1,0:T(8,128)(2,1)S(1)} %get-tuple-element.38), channel_id=1, replica_groups=mesh['src'=8,'tgt'=32] {'src'}, dimensions={0} | all-to-all | bytes 131072 | tf_op jit(solution)/shard_map/all_to_all | solution.py:518
  237.6 23.8 %shard_map.108 = (bf16[32,16,256]{2,1,0:T(8,128)(2,1)S(1)}, f32[4,1024]{1,0:T(4,128)S(1)}) custom-call(s32[1,7]{1,0:T(1,128)S(4)} %get-tuple-element.28.ints, f32[1,5]{1,0:T(1,128)S(4)} %get-tuple-element.29.floats, f32[4,1024]{1,0:T(4,128)S(1)} %get-tuple-element.32.log_b.rest_1_, bf16[1,3,1024,1024]{3,2,1,0:T(8,128)(2,1)} %cost_hbm.17, ...), custom_call_target="tpu_custom_call" | custom-call | tf_op jit(solution)/shard_map/pallas_call | solution.py:602
  261.4 24.3 %all_to_all.45.parts = bf16[32,16,256]{2,1,0:T(8,128)(2,1)S(1)} all-to-all(bf16[32,16,256]{2,1,0:T(8,128)(2,1)S(1)} %get-tuple-element.40), channel_id=1, replica_groups=mesh['src'=8,'tgt'=32] {'tgt'}, dimensions={0} | all-to-all | bytes 524288 | tf_op jit(solution)/shard_map/all_to_all | solution.py:518
  285.7 23.0 %shard_map.109 = (bf16[8,16,256]{2,1,0:T(8,128)(2,1)S(1)}, f32[4,1024]{1,0:T(4,128)S(1)}) custom-call(s32[1,7]{1,0:T(1,128)S(4)} %get-tuple-element.28.ints, f32[1,5]{1,0:T(1,128)S(4)} %get-tuple-element.29.floats, f32[4,1024]{1,0:T(4,128)S(1)} %get-tuple-element.30.log_a, bf16[1,3,1024,1024]{3,2,1,0:T(8,128)(2,1)} %cost_hbm.17, ...), custom_call_target="tpu_custom_call" | custom-call | tf_op jit(solution)/shard_map/pallas_call | solution.py:591
  308.6 22.0 %all_to_all.46.parts = bf16[8,16,256]{2,1,0:T(8,128)(2,1)S(1)} all-to-all(bf16[8,16,256]{2,1,0:T(8,128)(2,1)S(1)} %get-tuple-element.43), channel_id=1, replica_groups=mesh['src'=8,'tgt'=32] {'src'}, dimensions={0} | all-to-all | bytes 131072 | tf_op jit(solution)/shard_map/all_to_all | solution.py:518
  330.7 24.0 %shard_map.110 = bf16[32,16,256]{2,1,0:T(8,128)(2,1)S(1)} custom-call(s32[1,7]{1,0:T(1,128)S(4)} %get-tuple-element.28.ints, f32[1,5]{1,0:T(1,128)S(4)} %get-tuple-element.29.floats, f32[4,1024]{1,0:T(4,128)S(1)} %get-tuple-element.32.log_b.rest_1_, bf16[1,3,1024,1024]{3,2,1,0:T(8,128)(2,1)} %cost_hbm.17, ...), custom_call_target="tpu_custom_call" | custom-call | tf_op jit(solution)/shard_map/pallas_call | solution.py:602
  354.6 25.7 %all_to_all.47.parts = bf16[32,16,256]{2,1,0:T(8,128)(2,1)S(1)} all-to-all(bf16[32,16,256]{2,1,0:T(8,128)(2,1)S(1)} %shard_map.110), channel_id=1, replica_groups=mesh['src'=8,'tgt'=32] {'tgt'}, dimensions={0} | all-to-all | bytes 524288 | tf_op jit(solution)/shard_map/all_to_all | solution.py:518
  380.3 31.5 %shard_map.112 = f32[4,72,512]{2,1,0:T(8,128)S(1)} custom-call(s32[1,7]{1,0:T(1,128)S(4)} %get-tuple-element.28.ints, f32[1,5]{1,0:T(1,128)S(4)} %get-tuple-element.29.floats, f32[4,1024]{1,0:T(4,128)S(1)} %get-tuple-element.30.log_a, bf16[1,3,1024,1024]{3,2,1,0:T(8,128)(2,1)} %cost_hbm.17, bf16[3,1024,1024]{2,1,0:T(8,128)(2,1)S(1)} %get-tuple-element.31.k_ref, ...), custom_call_target="tpu_custom_call" | custom-call | flops 471859200 | bytes 3145728 | tf_op jit(solution)/shard_map/pallas_call | solution.py:618
  411.8 3.8 collective-permute-start
  415.5 31.5 %shard_map.111 = (f32[4,1024]{1,0:T(4,128)S(1)}, f32[4,72,512]{2,1,0:T(8,128)S(1)}) custom-call(s32[1,7]{1,0:T(1,128)S(4)} %get-tuple-element.28.ints, f32[1,5]{1,0:T(1,128)S(4)} %get-tuple-element.29.floats, f32[4,1024]{1,0:T(4,128)S(1)} %get-tuple-element.30.log_a, bf16[1,3,1024,1024]{3,2,1,0:T(8,128)(2,1)} %cost_hbm.17, ...), custom_call_target="tpu_custom_call" | custom-call | flops 471859200 | bytes 3145728 | tf_op jit(solution)/shard_map/pallas_call | solution.py:618
  447.0 0.2 shard_map.113
  447.2 28.4 %collective-permute-start.1 = (bf16[80,512]{1,0:T(8,128)(2,1)S(1)}, bf16[80,512]{1,0:T(8,128)(2,1)S(1)}, u32[]{:S(2)}, u32[]{:S(2)}) collective-permute-start(bf16[80,512]{1,0:T(8,128)(2,1)S(1)} %get-tuple-element.47), channel_id=1, source_target_pairs={{0,128},{32,160},{64,192},{96,224},{128,0},{160,32},{192,64},{224,... | collective-permute-start | bytes 245768 | tf_op jit(solution)/shard_map/ppermute | solution.py:504
  475.5 0.4 collective-permute-start.3
  475.9 1.4 collective-permute-done.1.rest_1_
  477.4 1.5 collective-permute-done.2.rest_2_
  478.8 1.2 collective-permute-done.3.rest_3_
  480.2 1.3 collective-permute-start.4
  481.4 2.1 collective-permute-start.6
  483.5 8.5 %collective-permute-start.7 = (bf16[80,512]{1,0:T(8,128)(2,1)S(1)}, bf16[80,512]{1,0:T(8,128)(2,1)S(1)}, u32[]{:S(2)}, u32[]{:S(2)}) collective-permute-start(bf16[80,512]{1,0:T(8,128)(2,1)S(1)} %shard_map.114.refs_0_), channel_id=1, source_target_pairs={{0,32},{32,0},{64,96},{96,64},{128,160},{160,128},{192,224},{224,1... | collective-permute-start | bytes 245768 | tf_op jit(solution)/shard_map/ppermute | solution.py:504
  492.0 1.8 collective-permute-start.8
  493.8 0.9 collective-permute-start.10
  494.8 0.4 collective-permute-done.9.refs_6_
  495.1 0.5 collective-permute-done.10.refs_7_
  495.6 0.9 shard_map.115
  (13 shorter events, 0.2 us)
Async XLA Ops:
  86.3 49.5 %copy-start = (bf16[128,64]{0,1:T(8,128)(2,1)S(1)}, bf16[128,64]{0,1:T(8,128)(2,1)}, u32[]{:S(2)}) copy-start(bf16[128,64]{0,1:T(8,128)(2,1)} %param.15) | copy-start | bytes 49156
  411.8 35.2 %collective-permute-start = (f32[4,72,512]{2,1,0:T(8,128)S(1)}, f32[4,72,512]{2,1,0:T(8,128)S(1)}, u32[]{:S(2)}, u32[]{:S(2)}) collective-permute-start(f32[4,72,512]{2,1,0:T(8,128)S(1)} %shard_map.112), channel_id=1, source_target_pairs={{0,32},{32,0},{64,96},{96,64},{128,160},{160,128},{192,224},{224,1... | collective-permute-start | bytes 1769480 | tf_op jit(solution)/shard_map/ppermute | solution.py:504
  447.2 30.2 %collective-permute-start.1 = (bf16[80,512]{1,0:T(8,128)(2,1)S(1)}, bf16[80,512]{1,0:T(8,128)(2,1)S(1)}, u32[]{:S(2)}, u32[]{:S(2)}) collective-permute-start(bf16[80,512]{1,0:T(8,128)(2,1)S(1)} %get-tuple-element.47), channel_id=1, source_target_pairs={{0,128},{32,160},{64,192},{96,224},{128,0},{160,32},{192,64},{224,... | collective-permute-start | bytes 245768 | tf_op jit(solution)/shard_map/ppermute | solution.py:504
  475.5 3.3 collective-permute-start.2
  475.5 4.5 collective-permute-start.3
  480.2 11.8 %collective-permute-start.4 = (bf16[80,512]{1,0:T(8,128)(2,1)S(1)}, bf16[80,512]{1,0:T(8,128)(2,1)S(1)}, u32[]{:S(2)}, u32[]{:S(2)}) collective-permute-start(bf16[80,512]{1,0:T(8,128)(2,1)S(1)} %shard_map.114.refs_0_), channel_id=1, source_target_pairs={{0,128},{32,160},{64,192},{96,224},{128,0},{160,32},{192,64},{224,... | collective-permute-start | bytes 245768 | tf_op jit(solution)/shard_map/ppermute | solution.py:504
  481.4 12.4 %collective-permute-start.5 = (bf16[80,512]{1,0:T(8,128)(2,1)S(1)}, bf16[80,512]{1,0:T(8,128)(2,1)S(1)}, u32[]{:S(2)}, u32[]{:S(2)}) collective-permute-start(bf16[80,512]{1,0:T(8,128)(2,1)S(1)} %shard_map.114.refs_0_), channel_id=1, source_target_pairs={{0,64},{32,96},{64,0},{96,32},{128,192},{160,224},{192,128},{224,1... | collective-permute-start | bytes 245768 | tf_op jit(solution)/shard_map/ppermute | solution.py:504
  481.4 12.4 %collective-permute-start.6 = (bf16[80,512]{1,0:T(8,128)(2,1)S(1)}, bf16[80,512]{1,0:T(8,128)(2,1)S(1)}, u32[]{:S(2)}, u32[]{:S(2)}) collective-permute-start(bf16[80,512]{1,0:T(8,128)(2,1)S(1)} %shard_map.114.refs_0_), channel_id=1, source_target_pairs={{0,192},{32,224},{64,128},{96,160},{128,64},{160,96},{192,0},{224,... | collective-permute-start | bytes 245768 | tf_op jit(solution)/shard_map/ppermute | solution.py:504
  483.5 11.2 %collective-permute-start.7 = (bf16[80,512]{1,0:T(8,128)(2,1)S(1)}, bf16[80,512]{1,0:T(8,128)(2,1)S(1)}, u32[]{:S(2)}, u32[]{:S(2)}) collective-permute-start(bf16[80,512]{1,0:T(8,128)(2,1)S(1)} %shard_map.114.refs_0_), channel_id=1, source_target_pairs={{0,32},{32,0},{64,96},{96,64},{128,160},{160,128},{192,224},{224,1... | collective-permute-start | bytes 245768 | tf_op jit(solution)/shard_map/ppermute | solution.py:504
  492.0 2.8 collective-permute-start.8
  493.8 1.3 collective-permute-start.9
  493.8 1.8 collective-permute-start.10

commit v10 on v9

--- a/solution.py
+++ b/solution.py
@@ -656,7 +656,8 @@
         compiler_params=PARAMS,
     )(log_b, *pieces)
     pieces = [done] + [xor(done, "src", 2 * q) for q in far_first]
-    pieces = pieces + [xor(p, "src", 1) for p in pieces]
+    straight = xor(done, "src", 2 * far_first[-1] + 1)
+    pieces = pieces + [xor(p, "src", 1) for p in pieces[:-1]] + [straight]
     order = (0,) + tuple(2 * q for q in far_first)
     order = order + tuple(k + 1 for k in order)
     f_pot, g_pot, out = pl.pallas_call(

time: 497 us -> 497 us (level); the launches traced: 497 us -> 489 us
  starting transfers between devices: 47 us -> 40.6 us
    ppermute x11, starting transfers between devices: 47 us -> 40.6 us  [xor(): lax.ppermute(x, axis, [(i, i ^ k) for i in range(lax.axis_size(axis))])]
  transfers between devices with their start and end apart: 11 -> 11, of which waited for: 5 -> 4; matrix products, arithmetic and copies ran while one was open for 0% -> 0% of each run, Pallas kernels for 6% -> 6%
where the time goes in v10:
time: 497 us; the launch traced here: 489 us
  Pallas kernels  249 us (50%)
  blocking collectives  193 us (39%)
  starting transfers between devices  40.6 us (8%)
  waiting for transfers between devices  5.1 us (1%)
    all_to_all x8, blocking collectives, everyone(): lax.all_to_all(copies, axis, 0, 0, axis_index_groups=groups, tiled=True)  193 us
    pallas_call x3, Pallas kernels, local(): pl.pallas_call(functools.partial(row_kernel, slots, first), out_shape=(se...  71.6 us
    pallas_call x3, Pallas kernels, local(): pl.pallas_call(functools.partial(col_kernel, slots, first), out_shape=(ve...  68.9 us
    pallas_call x2, Pallas kernels, label_call(): pl.pallas_call(functools.partial(label_kernel, slots, own), out_shape=(ve...  62.9 us
    pallas_call x1, Pallas kernels, local(): pl.pallas_call(functools.partial(build_kernel, dims), out_shape=(pltpu.VM...  44.3 us
    ppermute x11, starting transfers between devices, xor(): lax.ppermute(x, axis, [(i, i ^ k) for i in range(lax.axis_size(axis))])  40.6 us
  transfers between devices with their start and end apart: 11, of which 4 were waited for; matrix products, arithmetic and copies ran while one was open for 0% of the time, Pallas kernels for 6%

profile of v10, /device:TPU:1, one launch (start us, length us, event | category | flops | bytes accessed | tf_op | source)
XLA Modules:
  0.0 488.8 jit_solution(105510831835294873)
XLA Ops:
  1.3 44.3 %shard_map.103 = (bf16[3,1024,1024]{2,1,0:T(8,128)(2,1)S(1)}, bf16[32,16,256]{2,1,0:T(8,128)(2,1)S(1)}, s32[1,7]{1,0:T(1,128)S(4)}, f32[1,5]{1,0:T(1,128)S(4)}, ...) custom-call(s32[1,1]{1,0:T(1,128)S(6)} %copy.11.count, f32[1,3]{1,0:T(1,128)} %scale_hbm.1, s32[1,3]{1,0:T(1,128)} %row_hbm.1, ...), custom_call_target="tpu_custom_call" | custom-call | tf_op jit(solution)/shard_map/pallas_call | solution.py:527
  45.6 42.7 %all_to_all.40.parts = bf16[32,16,256]{2,1,0:T(8,128)(2,1)S(1)} all-to-all(bf16[32,16,256]{2,1,0:T(8,128)(2,1)S(1)} %get-tuple-element.33), channel_id=1, replica_groups=mesh['src'=8,'tgt'=32] {'tgt'}, dimensions={0} | all-to-all | bytes 524288 | tf_op jit(solution)/shard_map/all_to_all | solution.py:518
  88.2 23.0 %shard_map.104 = (f32[8,4,1024]{2,1,0:T(4,128)S(1)}, f32[4,1024]{1,0:T(4,128)S(1)}) custom-call(s32[1,7]{1,0:T(1,128)S(4)} %get-tuple-element.28.ints, f32[1,5]{1,0:T(1,128)S(4)} %get-tuple-element.29.floats, f32[4,1024]{1,0:T(4,128)S(1)} %get-tuple-element.30.log_a, bf16[1,3,1024,1024]{3,2,1,0:T(8,128)(2,1)} %cost_hbm.17, ...), custom_call_target="tpu_custom_call" | custom-call | tf_op jit(solution)/shard_map/pallas_call | solution.py:591
  111.2 20.3 %all_to_all.41.parts = f32[8,4,1024]{2,1,0:T(4,128)S(1)} all-to-all(f32[8,4,1024]{2,1,0:T(4,128)S(1)} %get-tuple-element.34), channel_id=1, replica_groups=mesh['src'=8,'tgt'=32] {'src'}, dimensions={0} | all-to-all | bytes 262144 | tf_op jit(solution)/shard_map/all_to_all | solution.py:518
  131.6 23.8 %shard_map.105 = (bf16[8,48,256]{2,1,0:T(8,128)(2,1)S(1)}, f32[4,1024]{1,0:T(4,128)S(1)}) custom-call(s32[1,7]{1,0:T(1,128)S(4)} %get-tuple-element.28.ints, f32[1,5]{1,0:T(1,128)S(4)} %get-tuple-element.29.floats, f32[4,1024]{1,0:T(4,128)S(1)} %get-tuple-element.32.log_b.rest_1_, bf16[1,3,1024,1024]{3,2,1,0:T(8,128)(2,1)} %cost_hbm.17, ...), custom_call_target="tpu_custom_call" | custom-call | tf_op jit(solution)/shard_map/pallas_call | solution.py:602
  155.4 23.3 %all_to_all.42.parts = bf16[8,48,256]{2,1,0:T(8,128)(2,1)S(1)} all-to-all(bf16[8,48,256]{2,1,0:T(8,128)(2,1)S(1)} %get-tuple-element.36), channel_id=1, replica_groups={{0,1,2,3,4,5,6,7},{8,9,10,11,12,13,14,15},{16,17,18,19,20,21,22,23},{24..., dimensions={0} | all-to-all | bytes 393216 | tf_op jit(solution)/shard_map/all_to_all | solution.py:518
  178.8 12.0 %all_to_all.43.parts.box = bf16[4,272,256]{2,1,0:T(8,128)(2,1)S(1)} all-to-all(bf16[4,272,256]{2,1,0:T(8,128)(2,1)S(1)} %shard_map.106), channel_id=1, replica_groups={{0,8,16,24},{1,9,17,25},{2,10,18,26},{3,11,19,27},{4,12,20,28},{5,13,21..., dimensions={0} | all-to-all | bytes 1114112 | tf_op jit(solution)/shard_map/all_to_all | solution.py:518
  190.7 22.9 %shard_map.107 = (bf16[8,16,256]{2,1,0:T(8,128)(2,1)S(1)}, f32[4,1024]{1,0:T(4,128)S(1)}) custom-call(s32[1,7]{1,0:T(1,128)S(4)} %get-tuple-element.28.ints, f32[1,5]{1,0:T(1,128)S(4)} %get-tuple-element.29.floats, f32[4,1024]{1,0:T(4,128)S(1)} %get-tuple-element.30.log_a, bf16[1,3,1024,1024]{3,2,1,0:T(8,128)(2,1)} %cost_hbm.17, ...), custom_call_target="tpu_custom_call" | custom-call | tf_op jit(solution)/shard_map/pallas_call | solution.py:591
  213.7 18.4 %all_to_all.44.parts = bf16[8,16,256]{2,1,0:T(8,128)(2,1)S(1)} all-to-all(bf16[8,16,256]{2,1,0:T(8,128)(2,1)S(1)} %get-tuple-element.38), channel_id=1, replica_groups=mesh['src'=8,'tgt'=32] {'src'}, dimensions={0} | all-to-all | bytes 131072 | tf_op jit(solution)/shard_map/all_to_all | solution.py:518
  232.1 23.8 %shard_map.108 = (bf16[32,16,256]{2,1,0:T(8,128)(2,1)S(1)}, f32[4,1024]{1,0:T(4,128)S(1)}) custom-call(s32[1,7]{1,0:T(1,128)S(4)} %get-tuple-element.28.ints, f32[1,5]{1,0:T(1,128)S(4)} %get-tuple-element.29.floats, f32[4,1024]{1,0:T(4,128)S(1)} %get-tuple-element.32.log_b.rest_1_, bf16[1,3,1024,1024]{3,2,1,0:T(8,128)(2,1)} %cost_hbm.17, ...), custom_call_target="tpu_custom_call" | custom-call | tf_op jit(solution)/shard_map/pallas_call | solution.py:602
  255.9 28.5 %all_to_all.45.parts = bf16[32,16,256]{2,1,0:T(8,128)(2,1)S(1)} all-to-all(bf16[32,16,256]{2,1,0:T(8,128)(2,1)S(1)} %get-tuple-element.40), channel_id=1, replica_groups=mesh['src'=8,'tgt'=32] {'tgt'}, dimensions={0} | all-to-all | bytes 524288 | tf_op jit(solution)/shard_map/all_to_all | solution.py:518
  284.4 23.0 %shard_map.109 = (bf16[8,16,256]{2,1,0:T(8,128)(2,1)S(1)}, f32[4,1024]{1,0:T(4,128)S(1)}) custom-call(s32[1,7]{1,0:T(1,128)S(4)} %get-tuple-element.28.ints, f32[1,5]{1,0:T(1,128)S(4)} %get-tuple-element.29.floats, f32[4,1024]{1,0:T(4,128)S(1)} %get-tuple-element.30.log_a, bf16[1,3,1024,1024]{3,2,1,0:T(8,128)(2,1)} %cost_hbm.17, ...), custom_call_target="tpu_custom_call" | custom-call | tf_op jit(solution)/shard_map/pallas_call | solution.py:591
  307.3 18.2 %all_to_all.46.parts = bf16[8,16,256]{2,1,0:T(8,128)(2,1)S(1)} all-to-all(bf16[8,16,256]{2,1,0:T(8,128)(2,1)S(1)} %get-tuple-element.43), channel_id=1, replica_groups=mesh['src'=8,'tgt'=32] {'src'}, dimensions={0} | all-to-all | bytes 131072 | tf_op jit(solution)/shard_map/all_to_all | solution.py:518
  325.5 24.0 %shard_map.110 = bf16[32,16,256]{2,1,0:T(8,128)(2,1)S(1)} custom-call(s32[1,7]{1,0:T(1,128)S(4)} %get-tuple-element.28.ints, f32[1,5]{1,0:T(1,128)S(4)} %get-tuple-element.29.floats, f32[4,1024]{1,0:T(4,128)S(1)} %get-tuple-element.32.log_b.rest_1_, bf16[1,3,1024,1024]{3,2,1,0:T(8,128)(2,1)} %cost_hbm.17, ...), custom_call_target="tpu_custom_call" | custom-call | tf_op jit(solution)/shard_map/pallas_call | solution.py:602
  349.5 29.6 %all_to_all.47.parts = bf16[32,16,256]{2,1,0:T(8,128)(2,1)S(1)} all-to-all(bf16[32,16,256]{2,1,0:T(8,128)(2,1)S(1)} %shard_map.110), channel_id=1, replica_groups=mesh['src'=8,'tgt'=32] {'tgt'}, dimensions={0} | all-to-all | bytes 524288 | tf_op jit(solution)/shard_map/all_to_all | solution.py:518
  379.0 31.5 %shard_map.112 = f32[4,72,512]{2,1,0:T(8,128)S(1)} custom-call(s32[1,7]{1,0:T(1,128)S(4)} %get-tuple-element.28.ints, f32[1,5]{1,0:T(1,128)S(4)} %get-tuple-element.29.floats, f32[4,1024]{1,0:T(4,128)S(1)} %get-tuple-element.30.log_a, bf16[1,3,1024,1024]{3,2,1,0:T(8,128)(2,1)} %cost_hbm.17, bf16[3,1024,1024]{2,1,0:T(8,128)(2,1)S(1)} %get-tuple-element.31.k_ref, ...), custom_call_target="tpu_custom_call" | custom-call | flops 471859200 | bytes 3145728 | tf_op jit(solution)/shard_map/pallas_call | solution.py:618
  410.5 3.7 collective-permute-start
  414.2 31.5 %shard_map.111 = (f32[4,1024]{1,0:T(4,128)S(1)}, f32[4,72,512]{2,1,0:T(8,128)S(1)}) custom-call(s32[1,7]{1,0:T(1,128)S(4)} %get-tuple-element.28.ints, f32[1,5]{1,0:T(1,128)S(4)} %get-tuple-element.29.floats, f32[4,1024]{1,0:T(4,128)S(1)} %get-tuple-element.30.log_a, bf16[1,3,1024,1024]{3,2,1,0:T(8,128)(2,1)} %cost_hbm.17, ...), custom_call_target="tpu_custom_call" | custom-call | flops 471859200 | bytes 3145728 | tf_op jit(solution)/shard_map/pallas_call | solution.py:618
  445.7 0.2 shard_map.113
  445.9 27.9 %collective-permute-start.2 = (bf16[80,512]{1,0:T(8,128)(2,1)S(1)}, bf16[80,512]{1,0:T(8,128)(2,1)S(1)}, u32[]{:S(2)}, u32[]{:S(2)}) collective-permute-start(bf16[80,512]{1,0:T(8,128)(2,1)S(1)} %get-tuple-element.48), channel_id=1, source_target_pairs={{0,64},{32,96},{64,0},{96,32},{128,192},{160,224},{192,128},{224,1... | collective-permute-start | bytes 245768 | tf_op jit(solution)/shard_map/ppermute | solution.py:504
  473.9 2.3 collective-permute-start.3
  476.2 0.3 collective-permute-done.2.rest_2_
  476.5 1.9 collective-permute-done.3.rest_3_
  478.4 0.1 shard_map.114.refs_0_
  478.5 2.4 collective-permute-start.4
  480.8 0.6 collective-permute-start.5
  481.5 0.6 collective-permute-start.6
  482.1 2.5 collective-permute-start.10
  484.5 0.5 collective-permute-start.9
  485.0 0.9 collective-permute-done.6.refs_3_
  486.0 2.0 collective-permute-done.10.refs_7_
  487.9 0.9 shard_map.115
  (13 shorter events, 0.2 us)
Async XLA Ops:
  88.2 43.3 %copy-start = (bf16[128,64]{0,1:T(8,128)(2,1)S(1)}, bf16[128,64]{0,1:T(8,128)(2,1)}, u32[]{:S(2)}) copy-start(bf16[128,64]{0,1:T(8,128)(2,1)} %param.15) | copy-start | bytes 49156
  410.5 35.2 %collective-permute-start = (f32[4,72,512]{2,1,0:T(8,128)S(1)}, f32[4,72,512]{2,1,0:T(8,128)S(1)}, u32[]{:S(2)}, u32[]{:S(2)}) collective-permute-start(f32[4,72,512]{2,1,0:T(8,128)S(1)} %shard_map.112), channel_id=1, source_target_pairs={{0,32},{32,0},{64,96},{96,64},{128,160},{160,128},{192,224},{224,1... | collective-permute-start | bytes 1769480 | tf_op jit(solution)/shard_map/ppermute | solution.py:504
  445.8 30.3 %collective-permute-start.1 = (bf16[80,512]{1,0:T(8,128)(2,1)S(1)}, bf16[80,512]{1,0:T(8,128)(2,1)S(1)}, u32[]{:S(2)}, u32[]{:S(2)}) collective-permute-start(bf16[80,512]{1,0:T(8,128)(2,1)S(1)} %get-tuple-element.47), channel_id=1, source_target_pairs={{0,128},{32,160},{64,192},{96,224},{128,0},{160,32},{192,64},{224,... | collective-permute-start | bytes 245768 | tf_op jit(solution)/shard_map/ppermute | solution.py:504
  445.9 30.5 %collective-permute-start.2 = (bf16[80,512]{1,0:T(8,128)(2,1)S(1)}, bf16[80,512]{1,0:T(8,128)(2,1)S(1)}, u32[]{:S(2)}, u32[]{:S(2)}) collective-permute-start(bf16[80,512]{1,0:T(8,128)(2,1)S(1)} %get-tuple-element.48), channel_id=1, source_target_pairs={{0,64},{32,96},{64,0},{96,32},{128,192},{160,224},{192,128},{224,1... | collective-permute-start | bytes 245768 | tf_op jit(solution)/shard_map/ppermute | solution.py:504
  473.9 4.5 collective-permute-start.3
  478.5 6.0 %collective-permute-start.4 = (bf16[80,512]{1,0:T(8,128)(2,1)S(1)}, bf16[80,512]{1,0:T(8,128)(2,1)S(1)}, u32[]{:S(2)}, u32[]{:S(2)}) collective-permute-start(bf16[80,512]{1,0:T(8,128)(2,1)S(1)} %shard_map.114.refs_0_), channel_id=1, source_target_pairs={{0,128},{32,160},{64,192},{96,224},{128,0},{160,32},{192,64},{224,... | collective-permute-start | bytes 245768 | tf_op jit(solution)/shard_map/ppermute | solution.py:504
  480.8 3.7 collective-permute-start.5
  481.5 4.5 collective-permute-start.6
  482.1 3.9 collective-permute-start.7
  482.1 5.9 %collective-permute-start.10 = (bf16[80,512]{1,0:T(8,128)(2,1)S(1)}, bf16[80,512]{1,0:T(8,128)(2,1)S(1)}, u32[]{:S(2)}, u32[]{:S(2)}) collective-permute-start(bf16[80,512]{1,0:T(8,128)(2,1)S(1)} %shard_map.114.refs_0_), channel_id=1, source_target_pairs={{0,224},{32,192},{64,160},{96,128},{128,96},{160,64},{192,32},{224... | collective-permute-start | bytes 245768 | tf_op jit(solution)/shard_map/ppermute | solution.py:504
  484.5 3.4 collective-permute-start.8
  484.5 3.4 collective-permute-start.9

commit v11 on v9

--- a/solution.py
+++ b/solution.py
@@ -15,6 +15,7 @@
 PART = 256
 INNER = 8
 MIDDLE = 116.0
+MIDDLE_COL = -130.0
 FLAT = (16, 256)
 LIMIT = 40 * 1024 * 1024
 F32, BF16 = jnp.float32, jnp.bfloat16
@@ -135,11 +136,6 @@
     return jnp.where(total > 0, jnp.log(jnp.maximum(total, 1e-38)) - shift / EPS, NEG)
 
 
-def send_copies(l_ref, copies_ref):
-    for k in range(copies_ref.shape[0]):
-        copies_ref[k] = l_ref[...]
-
-
 def send_flat(x, flat, copies_ref):
     count, width = x.shape[0], flat.shape[1]
     for c in range(x.shape[1] // width):
@@ -153,15 +149,12 @@
     send_flat(jnp.exp(l_ref[...] + pot[...] / EPS - log_mass[...]), flat, copies_ref)
 
 
-def new_potential(out, log_mass, parts, prev, flat):
-    if parts.dtype == F32:
-        out[...] = EPS * log_mass[...] - EPS * lse([parts[k] for k in range(parts.shape[0])])
-        return
+def new_potential(out, log_mass, parts, prev, flat, middle=MIDDLE):
     parts = [parts[k, : flat.shape[0]].astype(F32) for k in range(parts.shape[0])]
     if prev is None:
         top = functools.reduce(jnp.maximum, parts)
         inv = 1.0 / top
-        flat[...] = MIDDLE + 2.0 * jnp.log(top) + jnp.log(tree_sum([(p * inv) * (p * inv) for p in parts]))
+        flat[...] = middle + 2.0 * jnp.log(top) + jnp.log(tree_sum([(p * inv) * (p * inv) for p in parts]))
     else:
         flat[...] = jnp.log(tree_sum(parts))
     count, width = out.shape[0], flat.shape[1]
@@ -305,7 +298,7 @@
     rest = rest[1:]
     copies_ref, g, l_ref, flat, sums, stat, cost_v, other8, out8, sem = rest
     slots = Slots(ints, floats, total)
-    new_potential(g, log_b, parts, prev, flat)
+    new_potential(g, log_b, parts, prev, flat, MIDDLE_COL)
     sums[...] = jnp.zeros(sums.shape, F32)
     clear_stat(stat)
     for s in range(slots.total):
@@ -365,7 +358,7 @@
         slow_lse(slots, cost_hbm, cost_v, sem, other8, out8, f, l_ref, False)
 
     if first:
-        send_copies(l_ref, copies_ref)
+        send_flat(jnp.exp((l_ref[...] - MIDDLE_COL) / 2), flat, copies_ref)
     else:
         send_relative(l_ref, g, log_b, flat, copies_ref)
 
@@ -590,7 +583,7 @@
         first = step == 0
         col_l, f_pot = pl.pallas_call(
             functools.partial(col_kernel, slots, first),
-            out_shape=(vec((n_src, cb, tile)) if first else sent((n_src,) + FLAT), vec((rb, tile))),
+            out_shape=(sent((n_src,) + FLAT), vec((rb, tile))),
             in_specs=common + [VM] * (1 if first else 4),
             out_specs=(VM, VM),
             scratch_shapes=[cols, flat, cols] + work,

time: 497 us -> 497 us (level)
  Pallas kernels: 249 us -> 371 us
  blocking collectives: 194 us -> 103 us
  starting transfers between devices: 47 us -> 17.5 us
    all_to_all x8, blocking collectives: 194 us -> 103 us  [everyone(): lax.all_to_all(copies, axis, 0, 0, axis_index_groups=groups, tiled=True)]
    pallas_call x3, Pallas kernels: 71.6 us -> 107 us  [local(): pl.pallas_call(functools.partial(row_kernel, slots, first), out_shape=(se...]
    pallas_call x3, Pallas kernels: 68.9 us -> 103 us  [local(): pl.pallas_call(functools.partial(col_kernel, slots, first), out_shape=(se...]
    pallas_call x2, Pallas kernels: 62.9 us -> 94.1 us  [label_call(): pl.pallas_call(functools.partial(label_kernel, slots, own), out_shape=(ve...]
    ppermute x11, starting transfers between devices: 47 us -> 17.5 us  [xor(): lax.ppermute(x, axis, [(i, i ^ k) for i in range(lax.axis_size(axis))])]
    pallas_call x1, Pallas kernels: 44.3 us -> 65.7 us  [local(): pl.pallas_call(functools.partial(build_kernel, dims), out_shape=(pltpu.VM...]
  transfers between devices with their start and end apart: 11 -> 11, of which waited for: 5 -> 3; matrix products, arithmetic and copies ran while one was open for 0% -> 0% of each run, Pallas kernels for 6% -> 9%
where the time goes in v11:
time: 497 us; the launch traced here: 496 us
  Pallas kernels  371 us (75%)
  blocking collectives  103 us (21%)
  starting transfers between devices  17.5 us (4%)
    pallas_call x3, Pallas kernels, local(): pl.pallas_call(functools.partial(row_kernel, slots, first), out_shape=(se...  107 us
    all_to_all x8, blocking collectives, everyone(): lax.all_to_all(copies, axis, 0, 0, axis_index_groups=groups, tiled=True)  103 us
    pallas_call x3, Pallas kernels, local(): pl.pallas_call(functools.partial(col_kernel, slots, first), out_shape=(se...  103 us
    pallas_call x2, Pallas kernels, label_call(): pl.pallas_call(functools.partial(label_kernel, slots, own), out_shape=(ve...  94.1 us
    pallas_call x1, Pallas kernels, local(): pl.pallas_call(functools.partial(build_kernel, dims), out_shape=(pltpu.VM...  65.7 us
    ppermute x11, starting transfers between devices, xor(): lax.ppermute(x, axis, [(i, i ^ k) for i in range(lax.axis_size(axis))])  17.5 us
  transfers between devices with their start and end apart: 11, of which 3 were waited for; matrix products, arithmetic and copies ran while one was open for 0% of the time, Pallas kernels for 9%

profile of v11, /device:TPU:1, one launch (start us, length us, event | category | flops | bytes accessed | tf_op | source)
XLA Modules:
  0.0 496.4 jit_solution(3187223278809466103)
XLA Ops:
  1.3 65.7 %shard_map.103 = (bf16[3,1024,1024]{2,1,0:T(8,128)(2,1)S(1)}, bf16[32,16,256]{2,1,0:T(8,128)(2,1)S(1)}, s32[1,7]{1,0:T(1,128)S(4)}, f32[1,5]{1,0:T(1,128)S(4)}, ...) custom-call(s32[1,1]{1,0:T(1,128)S(6)} %copy.11.count, f32[1,3]{1,0:T(1,128)} %scale_hbm.1, s32[1,3]{1,0:T(1,128)} %row_hbm.1, ...), custom_call_target="tpu_custom_call" | custom-call | tf_op jit(solution)/shard_map/pallas_call | solution.py:520
  66.9 20.6 %all_to_all.40.parts = bf16[32,16,256]{2,1,0:T(8,128)(2,1)S(1)} all-to-all(bf16[32,16,256]{2,1,0:T(8,128)(2,1)S(1)} %get-tuple-element.33), channel_id=1, replica_groups=mesh['src'=8,'tgt'=32] {'tgt'}, dimensions={0} | all-to-all | bytes 524288 | tf_op jit(solution)/shard_map/all_to_all | solution.py:511
  87.6 34.4 %shard_map.104 = (bf16[8,16,256]{2,1,0:T(8,128)(2,1)S(1)}, f32[4,1024]{1,0:T(4,128)S(1)}) custom-call(s32[1,7]{1,0:T(1,128)S(4)} %get-tuple-element.28.ints, f32[1,5]{1,0:T(1,128)S(4)} %get-tuple-element.29.floats, f32[4,1024]{1,0:T(4,128)S(1)} %get-tuple-element.30.log_a, bf16[1,3,1024,1024]{3,2,1,0:T(8,128)(2,1)} %cost_hbm.17, ...), custom_call_target="tpu_custom_call" | custom-call | tf_op jit(solution)/shard_map/pallas_call | solution.py:584
  122.0 11.8 %all_to_all.41.parts = bf16[8,16,256]{2,1,0:T(8,128)(2,1)S(1)} all-to-all(bf16[8,16,256]{2,1,0:T(8,128)(2,1)S(1)} %get-tuple-element.34), channel_id=1, replica_groups=mesh['src'=8,'tgt'=32] {'src'}, dimensions={0} | all-to-all | bytes 131072 | tf_op jit(solution)/shard_map/all_to_all | solution.py:511
  133.7 35.6 %shard_map.105 = (bf16[8,48,256]{2,1,0:T(8,128)(2,1)S(1)}, f32[4,1024]{1,0:T(4,128)S(1)}) custom-call(s32[1,7]{1,0:T(1,128)S(4)} %get-tuple-element.28.ints, f32[1,5]{1,0:T(1,128)S(4)} %get-tuple-element.29.floats, f32[4,1024]{1,0:T(4,128)S(1)} %get-tuple-element.32.log_b.rest_1_, bf16[1,3,1024,1024]{3,2,1,0:T(8,128)(2,1)} %cost_hbm.17, ...), custom_call_target="tpu_custom_call" | custom-call | tf_op jit(solution)/shard_map/pallas_call | solution.py:595
  169.3 14.5 %all_to_all.42.parts = bf16[8,48,256]{2,1,0:T(8,128)(2,1)S(1)} all-to-all(bf16[8,48,256]{2,1,0:T(8,128)(2,1)S(1)} %get-tuple-element.36), channel_id=1, replica_groups={{0,1,2,3,4,5,6,7},{8,9,10,11,12,13,14,15},{16,17,18,19,20,21,22,23},{24..., dimensions={0} | all-to-all | bytes 393216 | tf_op jit(solution)/shard_map/all_to_all | solution.py:511
  183.9 11.1 %all_to_all.43.parts.box = bf16[4,272,256]{2,1,0:T(8,128)(2,1)S(1)} all-to-all(bf16[4,272,256]{2,1,0:T(8,128)(2,1)S(1)} %shard_map.106), channel_id=1, replica_groups={{0,8,16,24},{1,9,17,25},{2,10,18,26},{3,11,19,27},{4,12,20,28},{5,13,21..., dimensions={0} | all-to-all | bytes 1114112 | tf_op jit(solution)/shard_map/all_to_all | solution.py:511
  195.0 34.3 %shard_map.107 = (bf16[8,16,256]{2,1,0:T(8,128)(2,1)S(1)}, f32[4,1024]{1,0:T(4,128)S(1)}) custom-call(s32[1,7]{1,0:T(1,128)S(4)} %get-tuple-element.28.ints, f32[1,5]{1,0:T(1,128)S(4)} %get-tuple-element.29.floats, f32[4,1024]{1,0:T(4,128)S(1)} %get-tuple-element.30.log_a, bf16[1,3,1024,1024]{3,2,1,0:T(8,128)(2,1)} %cost_hbm.17, ...), custom_call_target="tpu_custom_call" | custom-call | tf_op jit(solution)/shard_map/pallas_call | solution.py:584
  229.3 8.2 %all_to_all.44.parts = bf16[8,16,256]{2,1,0:T(8,128)(2,1)S(1)} all-to-all(bf16[8,16,256]{2,1,0:T(8,128)(2,1)S(1)} %get-tuple-element.38), channel_id=1, replica_groups=mesh['src'=8,'tgt'=32] {'src'}, dimensions={0} | all-to-all | bytes 131072 | tf_op jit(solution)/shard_map/all_to_all | solution.py:511
  237.4 35.6 %shard_map.108 = (bf16[32,16,256]{2,1,0:T(8,128)(2,1)S(1)}, f32[4,1024]{1,0:T(4,128)S(1)}) custom-call(s32[1,7]{1,0:T(1,128)S(4)} %get-tuple-element.28.ints, f32[1,5]{1,0:T(1,128)S(4)} %get-tuple-element.29.floats, f32[4,1024]{1,0:T(4,128)S(1)} %get-tuple-element.32.log_b.rest_1_, bf16[1,3,1024,1024]{3,2,1,0:T(8,128)(2,1)} %cost_hbm.17, ...), custom_call_target="tpu_custom_call" | custom-call | tf_op jit(solution)/shard_map/pallas_call | solution.py:595
  273.1 13.1 %all_to_all.45.parts = bf16[32,16,256]{2,1,0:T(8,128)(2,1)S(1)} all-to-all(bf16[32,16,256]{2,1,0:T(8,128)(2,1)S(1)} %get-tuple-element.40), channel_id=1, replica_groups=mesh['src'=8,'tgt'=32] {'tgt'}, dimensions={0} | all-to-all | bytes 524288 | tf_op jit(solution)/shard_map/all_to_all | solution.py:511
  286.2 34.3 %shard_map.109 = (bf16[8,16,256]{2,1,0:T(8,128)(2,1)S(1)}, f32[4,1024]{1,0:T(4,128)S(1)}) custom-call(s32[1,7]{1,0:T(1,128)S(4)} %get-tuple-element.28.ints, f32[1,5]{1,0:T(1,128)S(4)} %get-tuple-element.29.floats, f32[4,1024]{1,0:T(4,128)S(1)} %get-tuple-element.30.log_a, bf16[1,3,1024,1024]{3,2,1,0:T(8,128)(2,1)} %cost_hbm.17, ...), custom_call_target="tpu_custom_call" | custom-call | tf_op jit(solution)/shard_map/pallas_call | solution.py:584
  320.5 9.7 %all_to_all.46.parts = bf16[8,16,256]{2,1,0:T(8,128)(2,1)S(1)} all-to-all(bf16[8,16,256]{2,1,0:T(8,128)(2,1)S(1)} %get-tuple-element.43), channel_id=1, replica_groups=mesh['src'=8,'tgt'=32] {'src'}, dimensions={0} | all-to-all | bytes 131072 | tf_op jit(solution)/shard_map/all_to_all | solution.py:511
  330.3 35.8 %shard_map.110 = bf16[32,16,256]{2,1,0:T(8,128)(2,1)S(1)} custom-call(s32[1,7]{1,0:T(1,128)S(4)} %get-tuple-element.28.ints, f32[1,5]{1,0:T(1,128)S(4)} %get-tuple-element.29.floats, f32[4,1024]{1,0:T(4,128)S(1)} %get-tuple-element.32.log_b.rest_1_, bf16[1,3,1024,1024]{3,2,1,0:T(8,128)(2,1)} %cost_hbm.17, ...), custom_call_target="tpu_custom_call" | custom-call | tf_op jit(solution)/shard_map/pallas_call | solution.py:595
  366.1 14.2 %all_to_all.47.parts = bf16[32,16,256]{2,1,0:T(8,128)(2,1)S(1)} all-to-all(bf16[32,16,256]{2,1,0:T(8,128)(2,1)S(1)} %shard_map.110), channel_id=1, replica_groups=mesh['src'=8,'tgt'=32] {'tgt'}, dimensions={0} | all-to-all | bytes 524288 | tf_op jit(solution)/shard_map/all_to_all | solution.py:511
  380.2 47.1 %shard_map.112 = f32[4,72,512]{2,1,0:T(8,128)S(1)} custom-call(s32[1,7]{1,0:T(1,128)S(4)} %get-tuple-element.28.ints, f32[1,5]{1,0:T(1,128)S(4)} %get-tuple-element.29.floats, f32[4,1024]{1,0:T(4,128)S(1)} %get-tuple-element.30.log_a, bf16[1,3,1024,1024]{3,2,1,0:T(8,128)(2,1)} %cost_hbm.17, bf16[3,1024,1024]{2,1,0:T(8,128)(2,1)S(1)} %get-tuple-element.31.k_ref, ...), custom_call_target="tpu_custom_call" | custom-call | flops 471859200 | bytes 3145728 | tf_op jit(solution)/shard_map/pallas_call | solution.py:611
  427.4 47.1 %shard_map.111 = (f32[4,1024]{1,0:T(4,128)S(1)}, f32[4,72,512]{2,1,0:T(8,128)S(1)}) custom-call(s32[1,7]{1,0:T(1,128)S(4)} %get-tuple-element.28.ints, f32[1,5]{1,0:T(1,128)S(4)} %get-tuple-element.29.floats, f32[4,1024]{1,0:T(4,128)S(1)} %get-tuple-element.30.log_a, bf16[1,3,1024,1024]{3,2,1,0:T(8,128)(2,1)} %cost_hbm.17, ...), custom_call_target="tpu_custom_call" | custom-call | flops 471859200 | bytes 3145728 | tf_op jit(solution)/shard_map/pallas_call | solution.py:611
  474.5 0.2 shard_map.113
  474.6 0.1 collective-permute-start.1
  474.8 3.1 collective-permute-start.3
  478.0 1.6 collective-permute-done.1.rest_1_
  479.6 0.8 collective-permute-done.3.rest_3_
  480.4 0.1 shard_map.114.refs_0_
  480.5 0.7 collective-permute-start.4
  481.2 2.1 collective-permute-start.5
  483.3 0.6 collective-permute-start.6
  483.9 7.3 %collective-permute-start.7 = (bf16[80,512]{1,0:T(8,128)(2,1)S(1)}, bf16[80,512]{1,0:T(8,128)(2,1)S(1)}, u32[]{:S(2)}, u32[]{:S(2)}) collective-permute-start(bf16[80,512]{1,0:T(8,128)(2,1)S(1)} %shard_map.114.refs_0_), channel_id=1, source_target_pairs={{0,32},{32,0},{64,96},{96,64},{128,160},{160,128},{192,224},{224,1... | collective-permute-start | bytes 245768 | tf_op jit(solution)/shard_map/ppermute | solution.py:497
  491.2 1.8 collective-permute-start.8
  493.0 0.4 collective-permute-start.9
  493.4 1.2 collective-permute-start.10
  494.6 0.9 collective-permute-done.10.refs_7_
  495.6 0.9 shard_map.115
  (13 shorter events, 0.2 us)
Async XLA Ops:
  87.6 46.2 %copy-start = (bf16[128,64]{0,1:T(8,128)(2,1)S(1)}, bf16[128,64]{0,1:T(8,128)(2,1)}, u32[]{:S(2)}) copy-start(bf16[128,64]{0,1:T(8,128)(2,1)} %param.15) | copy-start | bytes 49156
  427.3 47.2 %collective-permute-start = (f32[4,72,512]{2,1,0:T(8,128)S(1)}, f32[4,72,512]{2,1,0:T(8,128)S(1)}, u32[]{:S(2)}, u32[]{:S(2)}) collective-permute-start(f32[4,72,512]{2,1,0:T(8,128)S(1)} %shard_map.112), channel_id=1, source_target_pairs={{0,32},{32,0},{64,96},{96,64},{128,160},{160,128},{192,224},{224,1... | collective-permute-start | bytes 1769480 | tf_op jit(solution)/shard_map/ppermute | solution.py:497
  474.6 4.9 collective-permute-start.1
  474.7 4.8 collective-permute-start.2
  474.8 5.6 %collective-permute-start.3 = (bf16[80,512]{1,0:T(8,128)(2,1)S(1)}, bf16[80,512]{1,0:T(8,128)(2,1)S(1)}, u32[]{:S(2)}, u32[]{:S(2)}) collective-permute-start(bf16[80,512]{1,0:T(8,128)(2,1)S(1)} %get-tuple-element.49), channel_id=1, source_target_pairs={{0,192},{32,224},{64,128},{96,160},{128,64},{160,96},{192,0},{224,... | collective-permute-start | bytes 245768 | tf_op jit(solution)/shard_map/ppermute | solution.py:497
  480.5 10.7 %collective-permute-start.4 = (bf16[80,512]{1,0:T(8,128)(2,1)S(1)}, bf16[80,512]{1,0:T(8,128)(2,1)S(1)}, u32[]{:S(2)}, u32[]{:S(2)}) collective-permute-start(bf16[80,512]{1,0:T(8,128)(2,1)S(1)} %shard_map.114.refs_0_), channel_id=1, source_target_pairs={{0,128},{32,160},{64,192},{96,224},{128,0},{160,32},{192,64},{224,... | collective-permute-start | bytes 245768 | tf_op jit(solution)/shard_map/ppermute | solution.py:497
  481.2 11.9 %collective-permute-start.5 = (bf16[80,512]{1,0:T(8,128)(2,1)S(1)}, bf16[80,512]{1,0:T(8,128)(2,1)S(1)}, u32[]{:S(2)}, u32[]{:S(2)}) collective-permute-start(bf16[80,512]{1,0:T(8,128)(2,1)S(1)} %shard_map.114.refs_0_), channel_id=1, source_target_pairs={{0,64},{32,96},{64,0},{96,32},{128,192},{160,224},{192,128},{224,1... | collective-permute-start | bytes 245768 | tf_op jit(solution)/shard_map/ppermute | solution.py:497
  483.3 10.2 %collective-permute-start.6 = (bf16[80,512]{1,0:T(8,128)(2,1)S(1)}, bf16[80,512]{1,0:T(8,128)(2,1)S(1)}, u32[]{:S(2)}, u32[]{:S(2)}) collective-permute-start(bf16[80,512]{1,0:T(8,128)(2,1)S(1)} %shard_map.114.refs_0_), channel_id=1, source_target_pairs={{0,192},{32,224},{64,128},{96,160},{128,64},{160,96},{192,0},{224,... | collective-permute-start | bytes 245768 | tf_op jit(solution)/shard_map/ppermute | solution.py:497
  483.9 10.8 %collective-permute-start.7 = (bf16[80,512]{1,0:T(8,128)(2,1)S(1)}, bf16[80,512]{1,0:T(8,128)(2,1)S(1)}, u32[]{:S(2)}, u32[]{:S(2)}) collective-permute-start(bf16[80,512]{1,0:T(8,128)(2,1)S(1)} %shard_map.114.refs_0_), channel_id=1, source_target_pairs={{0,32},{32,0},{64,96},{96,64},{128,160},{160,128},{192,224},{224,1... | collective-permute-start | bytes 245768 | tf_op jit(solution)/shard_map/ppermute | solution.py:497
  491.2 3.4 collective-permute-start.8
  493.0 1.6 collective-permute-start.9
  493.4 2.1 collective-permute-start.10
